TPU v7x, 512 devices: a whole 4x8x8 slice. The times are simulated.
512 devices in a mesh: gx: 64 (over y, z), gy: 8 (over x, core).
Axes of the slice: x: 4, y: 8, z: 8, core: 2. Of those that a mesh axis runs over, the one named last changes fastest.
Arguments:
- velocity: float32 [2048, 256, 128], P('gx', 'gy'), may hold values from -6 to 6
Outputs:
- coefficients: float32 [2048, 256, 128], P('gx', 'gy')
All inputs are finite; a program needn't handle non-finite values.
Results may differ from a plain program's by a relative error of at most 0.00002.
Values sent between devices are 32-bit elements; how exact they have to be, the bound alone decides.
A program may use at most 128 MiB of HBM per device.

v0:
```python
import jax
import jax.numpy as jnp
from jax import lax
from jax.sharding import PartitionSpec as P

LEVELS = 4


lift_alpha = -1.586134342
lift_beta = -0.05298011854
lift_gamma = 0.8829110762
lift_delta = 0.4435068522
lift_scale = 1.149604398


def passed_along(value, axis, by):
    length = lax.axis_size(axis)
    return lax.ppermute(value, axis, [(i, (i + by) % length) for i in range(length)])


def lift_core(even, odd, forward, backward):
    odd = odd + lift_alpha * (even + forward(even))
    even = even + lift_beta * (backward(odd) + odd)
    odd = odd + lift_gamma * (even + forward(even))
    even = even + lift_delta * (backward(odd) + odd)
    return (even / lift_scale, odd * lift_scale)


def split_axis(array, axis, forward, backward):
    count = array.shape[axis]
    even = lax.slice_in_dim(array, 0, count, 2, axis)
    odd = lax.slice_in_dim(array, 1, count, 2, axis)
    return lift_core(even, odd, forward, backward)


def periodic_split(array, axis):

    def forward(values):
        return jnp.roll(values, -1, axis)

    def backward(values):
        return jnp.roll(values, 1, axis)

    return split_axis(array, axis, forward, backward)


def chained_x(array):

    def forward(values):
        count = values.shape[0]
        incoming = passed_along(lax.slice_in_dim(values, 0, 1, 1, 0), "gx", -1)
        return jnp.concatenate([lax.slice_in_dim(values, 1, count, 1, 0), incoming], 0)

    def backward(values):
        count = values.shape[0]
        incoming = passed_along(lax.slice_in_dim(values, count - 1, count, 1, 0), "gx", 1)
        return jnp.concatenate([incoming, lax.slice_in_dim(values, 0, count - 1, 1, 0)], 0)

    return split_axis(array, 0, forward, backward)


def chained_y(array):

    def forward(values):
        count = values.shape[2]
        incoming = passed_along(lax.slice_in_dim(values, 0, 1, 1, 2), "gy", -1)
        return jnp.concatenate([lax.slice_in_dim(values, 1, count, 1, 2), incoming], 2)

    def backward(values):
        count = values.shape[2]
        incoming = passed_along(lax.slice_in_dim(values, count - 1, count, 1, 2), "gy", 1)
        return jnp.concatenate([incoming, lax.slice_in_dim(values, 0, count - 1, 1, 2)], 2)

    return split_axis(array, 2, forward, backward)


def split_x(array):
    result = chained_x(array)
    return result


def split_y(bands):
    result = chained_y(bands)
    return result


def split_level(array):
    low, high = split_x(array)
    bands = jnp.stack([low, high])
    low, high = split_y(bands)
    bands = jnp.stack([low, high])
    low, high = periodic_split(bands, 4)
    return jnp.stack([low, high])


def alternate(bands):
    size_x, size_y, size_z = (bands.shape[3], bands.shape[4], bands.shape[5])
    return jnp.transpose(bands, (3, 2, 4, 1, 5, 0)).reshape(2 * size_x, 2 * size_y, 2 * size_z)


def decompose(array, level):
    bands = split_level(array)
    if level < LEVELS:
        result = decompose(bands[0, 0, 0], level + 1)
        bands = bands.at[0, 0, 0].set(result)
    return alternate(bands)


def local(velocity):
    return decompose(velocity, 1)


def solution(mesh):
    placed = (P("gx", "gy", None),)
    return jax.shard_map(
        local, mesh=mesh, in_specs=placed, out_specs=P("gx", "gy", None), check_vma=False
    )
```

profile of v0, /device:TPU:1, one launch (start us, length us, event | category | flops | bytes accessed | tf_op | source)
XLA Modules:
  0.0 251.3 jit_solution(9435905591057850165)
XLA Ops:
  1.0 14.4 %collective-permute-start = (f32[1,32,128]{2,1,0:T(8,128)S(1)}, f32[1,32,128]{2,1,0:T(8,128)S(1)}, u32[]{:S(2)}, u32[]{:S(2)}) collective-permute-start(f32[1,32,128]{2,1,0:T(8,128)S(1)} %slice.623), channel_id=1, source_target_pairs={{0,504},{8,0},{16,8},{24,16},{32,24},{40,32},{48,40},{56,48},{64,5... | collective-permute-start | bytes 49160 | tf_op jit(solution)/shard_map/ppermute | solution.py:18
  19.3 6.1 %collective-permute-done.1 = f32[1,32,128]{2,1,0:T(8,128)S(1)} collective-permute-done((f32[1,32,128]{2,1,0:T(8,128)S(1)}, f32[1,32,128]{2,1,0:T(8,128)S(1)}, u32[]{:S(2)}, u32[]{:S(2)}) %collective-permute-start.1) | collective-permute-done | bytes 16416 | tf_op jit(solution)/shard_map/ppermute | solution.py:18
  33.0 5.8 %collective-permute-done.3 = f32[1,32,128]{2,1,0:T(8,128)S(1)} collective-permute-done((f32[1,32,128]{2,1,0:T(8,128)S(1)}, f32[1,32,128]{2,1,0:T(8,128)S(1)}, u32[]{:S(2)}, u32[]{:S(2)}) %collective-permute-start.3) | collective-permute-done | bytes 16416 | tf_op jit(solution)/shard_map/ppermute | solution.py:18
  39.1 5.0 %collective-permute-start.4 = (f32[2,16,1,128]{3,2,1,0:T(1,128)S(1)}, f32[2,16,1,128]{3,2,1,0:T(1,128)S(1)}, u32[]{:S(2)}, u32[]{:S(2)}) collective-permute-start(f32[2,16,1,128]{3,2,1,0:T(1,128)S(1)} %slice.631), channel_id=1, source_target_pairs={{0,7},{1,0},{2,1},{3,2},{4,3},{5,4},{6,5},{7,6},{8,15},{9,8},{10,9... | collective-permute-start | bytes 49160 | tf_op jit(solution)/shard_map/ppermute | solution.py:18
  52.9 9.2 %slice.519 = f32[2,2,16,16,64]{4,3,2,1,0:T(8,128)S(1)} slice(f32[2,2,16,16,128]{4,3,2,1,0:T(8,128)S(1)} %pad_maximum_fusion.2), slice={[0:2:1], [0:2:1], [0:16:1], [0:16:1], [0:128:2]} | slice | bytes 524288 | tf_op jit(solution)/shard_map/slice | solution.py:31
  62.2 9.4 %slice.520 = f32[2,2,16,16,64]{4,3,2,1,0:T(8,128)S(1)} slice(f32[2,2,16,16,128]{4,3,2,1,0:T(8,128)S(1)} %pad_maximum_fusion.2), slice={[0:2:1], [0:2:1], [0:16:1], [0:16:1], [1:128:2]} | slice | bytes 524288 | tf_op jit(solution)/shard_map/slice | solution.py:32
  73.3 3.6 %collective-permute-start.8 = (f32[1,16,64]{2,1,0:T(8,128)S(1)}, f32[1,16,64]{2,1,0:T(8,128)S(1)}, u32[]{:S(2)}, u32[]{:S(2)}) collective-permute-start(f32[1,16,64]{2,1,0:T(8,128)S(1)} %slice.648), channel_id=1, source_target_pairs={{0,504},{8,0},{16,8},{24,16},{32,24},{40,32},{48,40},{56,48},{64,5... | collective-permute-start | bytes 12296 | tf_op jit(solution)/shard_map/ppermute | solution.py:18
  79.7 6.0 %collective-permute-done.9 = f32[1,16,64]{2,1,0:T(8,128)S(1)} collective-permute-done((f32[1,16,64]{2,1,0:T(8,128)S(1)}, f32[1,16,64]{2,1,0:T(8,128)S(1)}, u32[]{:S(2)}, u32[]{:S(2)}) %collective-permute-start.9) | collective-permute-done | bytes 4128 | tf_op jit(solution)/shard_map/ppermute | solution.py:18
  92.4 5.8 %collective-permute-done.11 = f32[1,16,64]{2,1,0:T(8,128)S(1)} collective-permute-done((f32[1,16,64]{2,1,0:T(8,128)S(1)}, f32[1,16,64]{2,1,0:T(8,128)S(1)}, u32[]{:S(2)}, u32[]{:S(2)}) %collective-permute-start.11) | collective-permute-done | bytes 4128 | tf_op jit(solution)/shard_map/ppermute | solution.py:18
  98.3 7.4 %collective-permute-start.12 = (f32[2,8,1,64]{3,2,1,0:T(1,128)S(1)}, f32[2,8,1,64]{3,2,1,0:T(1,128)S(1)}, u32[]{:S(2)}, u32[]{:S(2)}) collective-permute-start(f32[2,8,1,64]{3,2,1,0:T(1,128)S(1)} %slice.656), channel_id=1, source_target_pairs={{0,7},{1,0},{2,1},{3,2},{4,3},{5,4},{6,5},{7,6},{8,15},{9,8},{10,9... | collective-permute-start | bytes 12296 | tf_op jit(solution)/shard_map/ppermute | solution.py:18
  107.8 3.6 %collective-permute-start.14 = (f32[2,8,1,64]{3,2,1,0:T(1,128)S(1)}, f32[2,8,1,64]{3,2,1,0:T(1,128)S(1)}, u32[]{:S(2)}, u32[]{:S(2)}) collective-permute-start(f32[2,8,1,64]{3,2,1,0:T(1,128)S(1)} %slice.660), channel_id=1, source_target_pairs={{0,7},{1,0},{2,1},{3,2},{4,3},{5,4},{6,5},{7,6},{8,15},{9,8},{10,9... | collective-permute-start | bytes 12296 | tf_op jit(solution)/shard_map/ppermute | solution.py:18
  117.3 3.6 %collective-permute-start.16 = (f32[1,8,32]{2,1,0:T(8,128)S(1)}, f32[1,8,32]{2,1,0:T(8,128)S(1)}, u32[]{:S(2)}, u32[]{:S(2)}) collective-permute-start(f32[1,8,32]{2,1,0:T(8,128)S(1)} %slice.673), channel_id=1, source_target_pairs={{0,504},{8,0},{16,8},{24,16},{32,24},{40,32},{48,40},{56,48},{64,5... | collective-permute-start | bytes 3080 | tf_op jit(solution)/shard_map/ppermute | solution.py:18
  123.7 6.0 %collective-permute-done.17 = f32[1,8,32]{2,1,0:T(8,128)S(1)} collective-permute-done((f32[1,8,32]{2,1,0:T(8,128)S(1)}, f32[1,8,32]{2,1,0:T(8,128)S(1)}, u32[]{:S(2)}, u32[]{:S(2)}) %collective-permute-start.17) | collective-permute-done | bytes 1056 | tf_op jit(solution)/shard_map/ppermute | solution.py:18
  136.3 5.7 %collective-permute-done.19 = f32[1,8,32]{2,1,0:T(8,128)S(1)} collective-permute-done((f32[1,8,32]{2,1,0:T(8,128)S(1)}, f32[1,8,32]{2,1,0:T(8,128)S(1)}, u32[]{:S(2)}, u32[]{:S(2)}) %collective-permute-start.19) | collective-permute-done | bytes 1056 | tf_op jit(solution)/shard_map/ppermute | solution.py:18
  142.2 7.7 %collective-permute-start.20 = (f32[2,4,1,32]{3,2,1,0:T(1,128)S(1)}, f32[2,4,1,32]{3,2,1,0:T(1,128)S(1)}, u32[]{:S(2)}, u32[]{:S(2)}) collective-permute-start(f32[2,4,1,32]{3,2,1,0:T(1,128)S(1)} %slice.681), channel_id=1, source_target_pairs={{0,7},{1,0},{2,1},{3,2},{4,3},{5,4},{6,5},{7,6},{8,15},{9,8},{10,9... | collective-permute-start | bytes 3080 | tf_op jit(solution)/shard_map/ppermute | solution.py:18
  151.9 3.6 %collective-permute-start.22 = (f32[2,4,1,32]{3,2,1,0:T(1,128)S(1)}, f32[2,4,1,32]{3,2,1,0:T(1,128)S(1)}, u32[]{:S(2)}, u32[]{:S(2)}) collective-permute-start(f32[2,4,1,32]{3,2,1,0:T(1,128)S(1)} %slice.685), channel_id=1, source_target_pairs={{0,7},{1,0},{2,1},{3,2},{4,3},{5,4},{6,5},{7,6},{8,15},{9,8},{10,9... | collective-permute-start | bytes 3080 | tf_op jit(solution)/shard_map/ppermute | solution.py:18
  159.4 3.6 %collective-permute-start.24 = (f32[1,4,16]{2,1,0:T(4,128)S(1)}, f32[1,4,16]{2,1,0:T(4,128)S(1)}, u32[]{:S(2)}, u32[]{:S(2)}) collective-permute-start(f32[1,4,16]{2,1,0:T(4,128)S(1)} %get-tuple-element.80), channel_id=1, source_target_pairs={{0,504},{8,0},{16,8},{24,16},{32,24},{40,32},{48,40},{56,48},{64,5... | collective-permute-start | bytes 776 | tf_op jit(solution)/shard_map/ppermute | solution.py:18
  165.7 6.0 %collective-permute-done.25 = f32[1,4,16]{2,1,0:T(4,128)S(1)} collective-permute-done((f32[1,4,16]{2,1,0:T(4,128)S(1)}, f32[1,4,16]{2,1,0:T(4,128)S(1)}, u32[]{:S(2)}, u32[]{:S(2)}) %collective-permute-start.25) | collective-permute-done | bytes 288 | tf_op jit(solution)/shard_map/ppermute | solution.py:18
  178.4 5.5 %collective-permute-done.27 = f32[1,4,16]{2,1,0:T(4,128)S(1)} collective-permute-done((f32[1,4,16]{2,1,0:T(4,128)S(1)}, f32[1,4,16]{2,1,0:T(4,128)S(1)}, u32[]{:S(2)}, u32[]{:S(2)}) %collective-permute-start.27) | collective-permute-done | bytes 288 | tf_op jit(solution)/shard_map/ppermute | solution.py:18
  184.1 7.6 %collective-permute-start.28 = (f32[2,2,1,16]{3,2,1,0:T(1,128)S(1)}, f32[2,2,1,16]{3,2,1,0:T(1,128)S(1)}, u32[]{:S(2)}, u32[]{:S(2)}) collective-permute-start(f32[2,2,1,16]{3,2,1,0:T(1,128)S(1)} %get-tuple-element.72), channel_id=1, source_target_pairs={{0,7},{1,0},{2,1},{3,2},{4,3},{5,4},{6,5},{7,6},{8,15},{9,8},{10,9... | collective-permute-start | bytes 776 | tf_op jit(solution)/shard_map/ppermute | solution.py:18
  193.8 3.6 %collective-permute-start.30 = (f32[2,2,1,16]{3,2,1,0:T(1,128)S(1)}, f32[2,2,1,16]{3,2,1,0:T(1,128)S(1)}, u32[]{:S(2)}, u32[]{:S(2)}) collective-permute-start(f32[2,2,1,16]{3,2,1,0:T(1,128)S(1)} %get-tuple-element.68), channel_id=1, source_target_pairs={{0,7},{1,0},{2,1},{3,2},{4,3},{5,4},{6,5},{7,6},{8,15},{9,8},{10,9... | collective-permute-start | bytes 776 | tf_op jit(solution)/shard_map/ppermute | solution.py:18
  204.9 4.9 %reshape.143 = f32[1,1,1,16,16,64]{5,4,3,2,1,0:T(8,128)S(1)} reshape(f32[8,2,8,2,32,2]{5,4,3,2,1,0:T(8,128)} %copy.7) | data formatting | bytes 131072 | tf_op jit(solution)/shard_map/reshape.111
  209.7 17.1 %copy.8 = f32[16,2,16,2,64,2]{5,4,3,2,1,0:T(8,128)} copy(f32[16,2,16,2,64,2]{4,2,0,1,3,5:T(8,128)S(1)} %bitcast.94) | data formatting | bytes 1048576 | tf_op jit(solution)/shard_map/transpose | solution.py:98
  226.9 24.5 %reshape.144 = f32[32,32,128]{2,1,0:T(8,128)} reshape(f32[16,2,16,2,64,2]{5,4,3,2,1,0:T(8,128)} %copy.8) | data formatting | bytes 1048576 | tf_op jit(solution)/shard_map/reshape | solution.py:98
  (200 shorter events, 74.5 us)
Async XLA Ops:
  1.0 15.3 %collective-permute-start = (f32[1,32,128]{2,1,0:T(8,128)S(1)}, f32[1,32,128]{2,1,0:T(8,128)S(1)}, u32[]{:S(2)}, u32[]{:S(2)}) collective-permute-start(f32[1,32,128]{2,1,0:T(8,128)S(1)} %slice.623), channel_id=1, source_target_pairs={{0,504},{8,0},{16,8},{24,16},{32,24},{40,32},{48,40},{56,48},{64,5... | collective-permute-start | bytes 49160 | tf_op jit(solution)/shard_map/ppermute | solution.py:18
  17.4 8.1 %collective-permute-start.1 = (f32[1,32,128]{2,1,0:T(8,128)S(1)}, f32[1,32,128]{2,1,0:T(8,128)S(1)}, u32[]{:S(2)}, u32[]{:S(2)}) collective-permute-start(f32[1,32,128]{2,1,0:T(8,128)S(1)} %slice.624), channel_id=1, source_target_pairs={{0,8},{8,16},{16,24},{24,32},{32,40},{40,48},{48,56},{56,64},{64,7... | collective-permute-start | bytes 49160 | tf_op jit(solution)/shard_map/ppermute | solution.py:18
  26.5 4.5 %collective-permute-start.2 = (f32[1,32,128]{2,1,0:T(8,128)S(1)}, f32[1,32,128]{2,1,0:T(8,128)S(1)}, u32[]{:S(2)}, u32[]{:S(2)}) collective-permute-start(f32[1,32,128]{2,1,0:T(8,128)S(1)} %slice.627), channel_id=1, source_target_pairs={{0,504},{8,0},{16,8},{24,16},{32,24},{40,32},{48,40},{56,48},{64,5... | collective-permute-start | bytes 49160 | tf_op jit(solution)/shard_map/ppermute | solution.py:18
  31.0 7.8 %collective-permute-start.3 = (f32[1,32,128]{2,1,0:T(8,128)S(1)}, f32[1,32,128]{2,1,0:T(8,128)S(1)}, u32[]{:S(2)}, u32[]{:S(2)}) collective-permute-start(f32[1,32,128]{2,1,0:T(8,128)S(1)} %slice.628), channel_id=1, source_target_pairs={{0,8},{8,16},{16,24},{24,32},{32,40},{40,48},{48,56},{56,64},{64,7... | collective-permute-start | bytes 49160 | tf_op jit(solution)/shard_map/ppermute | solution.py:18
  39.1 7.5 %collective-permute-start.4 = (f32[2,16,1,128]{3,2,1,0:T(1,128)S(1)}, f32[2,16,1,128]{3,2,1,0:T(1,128)S(1)}, u32[]{:S(2)}, u32[]{:S(2)}) collective-permute-start(f32[2,16,1,128]{3,2,1,0:T(1,128)S(1)} %slice.631), channel_id=1, source_target_pairs={{0,7},{1,0},{2,1},{3,2},{4,3},{5,4},{6,5},{7,6},{8,15},{9,8},{10,9... | collective-permute-start | bytes 49160 | tf_op jit(solution)/shard_map/ppermute | solution.py:18
  48.1 3.4 %collective-permute-start.6 = (f32[2,16,1,128]{3,2,1,0:T(1,128)S(1)}, f32[2,16,1,128]{3,2,1,0:T(1,128)S(1)}, u32[]{:S(2)}, u32[]{:S(2)}) collective-permute-start(f32[2,16,1,128]{3,2,1,0:T(1,128)S(1)} %slice.635), channel_id=1, source_target_pairs={{0,7},{1,0},{2,1},{3,2},{4,3},{5,4},{6,5},{7,6},{8,15},{9,8},{10,9... | collective-permute-start | bytes 49160 | tf_op jit(solution)/shard_map/ppermute | solution.py:18
  73.3 4.4 %collective-permute-start.8 = (f32[1,16,64]{2,1,0:T(8,128)S(1)}, f32[1,16,64]{2,1,0:T(8,128)S(1)}, u32[]{:S(2)}, u32[]{:S(2)}) collective-permute-start(f32[1,16,64]{2,1,0:T(8,128)S(1)} %slice.648), channel_id=1, source_target_pairs={{0,504},{8,0},{16,8},{24,16},{32,24},{40,32},{48,40},{56,48},{64,5... | collective-permute-start | bytes 12296 | tf_op jit(solution)/shard_map/ppermute | solution.py:18
  77.7 8.0 %collective-permute-start.9 = (f32[1,16,64]{2,1,0:T(8,128)S(1)}, f32[1,16,64]{2,1,0:T(8,128)S(1)}, u32[]{:S(2)}, u32[]{:S(2)}) collective-permute-start(f32[1,16,64]{2,1,0:T(8,128)S(1)} %slice.649), channel_id=1, source_target_pairs={{0,8},{8,16},{16,24},{24,32},{32,40},{40,48},{48,56},{56,64},{64,7... | collective-permute-start | bytes 12296 | tf_op jit(solution)/shard_map/ppermute | solution.py:18
  85.7 4.7 %collective-permute-start.10 = (f32[1,16,64]{2,1,0:T(8,128)S(1)}, f32[1,16,64]{2,1,0:T(8,128)S(1)}, u32[]{:S(2)}, u32[]{:S(2)}) collective-permute-start(f32[1,16,64]{2,1,0:T(8,128)S(1)} %slice.652), channel_id=1, source_target_pairs={{0,504},{8,0},{16,8},{24,16},{32,24},{40,32},{48,40},{56,48},{64,5... | collective-permute-start | bytes 12296 | tf_op jit(solution)/shard_map/ppermute | solution.py:18
  90.4 7.7 %collective-permute-start.11 = (f32[1,16,64]{2,1,0:T(8,128)S(1)}, f32[1,16,64]{2,1,0:T(8,128)S(1)}, u32[]{:S(2)}, u32[]{:S(2)}) collective-permute-start(f32[1,16,64]{2,1,0:T(8,128)S(1)} %slice.653), channel_id=1, source_target_pairs={{0,8},{8,16},{16,24},{24,32},{32,40},{40,48},{48,56},{56,64},{64,7... | collective-permute-start | bytes 12296 | tf_op jit(solution)/shard_map/ppermute | solution.py:18
  98.3 8.2 %collective-permute-start.12 = (f32[2,8,1,64]{3,2,1,0:T(1,128)S(1)}, f32[2,8,1,64]{3,2,1,0:T(1,128)S(1)}, u32[]{:S(2)}, u32[]{:S(2)}) collective-permute-start(f32[2,8,1,64]{3,2,1,0:T(1,128)S(1)} %slice.656), channel_id=1, source_target_pairs={{0,7},{1,0},{2,1},{3,2},{4,3},{5,4},{6,5},{7,6},{8,15},{9,8},{10,9... | collective-permute-start | bytes 12296 | tf_op jit(solution)/shard_map/ppermute | solution.py:18
  107.8 4.5 %collective-permute-start.14 = (f32[2,8,1,64]{3,2,1,0:T(1,128)S(1)}, f32[2,8,1,64]{3,2,1,0:T(1,128)S(1)}, u32[]{:S(2)}, u32[]{:S(2)}) collective-permute-start(f32[2,8,1,64]{3,2,1,0:T(1,128)S(1)} %slice.660), channel_id=1, source_target_pairs={{0,7},{1,0},{2,1},{3,2},{4,3},{5,4},{6,5},{7,6},{8,15},{9,8},{10,9... | collective-permute-start | bytes 12296 | tf_op jit(solution)/shard_map/ppermute | solution.py:18
  117.3 4.4 %collective-permute-start.16 = (f32[1,8,32]{2,1,0:T(8,128)S(1)}, f32[1,8,32]{2,1,0:T(8,128)S(1)}, u32[]{:S(2)}, u32[]{:S(2)}) collective-permute-start(f32[1,8,32]{2,1,0:T(8,128)S(1)} %slice.673), channel_id=1, source_target_pairs={{0,504},{8,0},{16,8},{24,16},{32,24},{40,32},{48,40},{56,48},{64,5... | collective-permute-start | bytes 3080 | tf_op jit(solution)/shard_map/ppermute | solution.py:18
  121.7 7.9 %collective-permute-start.17 = (f32[1,8,32]{2,1,0:T(8,128)S(1)}, f32[1,8,32]{2,1,0:T(8,128)S(1)}, u32[]{:S(2)}, u32[]{:S(2)}) collective-permute-start(f32[1,8,32]{2,1,0:T(8,128)S(1)} %slice.674), channel_id=1, source_target_pairs={{0,8},{8,16},{16,24},{24,32},{32,40},{40,48},{48,56},{56,64},{64,7... | collective-permute-start | bytes 3080 | tf_op jit(solution)/shard_map/ppermute | solution.py:18
  129.7 4.6 %collective-permute-start.18 = (f32[1,8,32]{2,1,0:T(8,128)S(1)}, f32[1,8,32]{2,1,0:T(8,128)S(1)}, u32[]{:S(2)}, u32[]{:S(2)}) collective-permute-start(f32[1,8,32]{2,1,0:T(8,128)S(1)} %slice.677), channel_id=1, source_target_pairs={{0,504},{8,0},{16,8},{24,16},{32,24},{40,32},{48,40},{56,48},{64,5... | collective-permute-start | bytes 3080 | tf_op jit(solution)/shard_map/ppermute | solution.py:18
  134.4 7.7 %collective-permute-start.19 = (f32[1,8,32]{2,1,0:T(8,128)S(1)}, f32[1,8,32]{2,1,0:T(8,128)S(1)}, u32[]{:S(2)}, u32[]{:S(2)}) collective-permute-start(f32[1,8,32]{2,1,0:T(8,128)S(1)} %slice.678), channel_id=1, source_target_pairs={{0,8},{8,16},{16,24},{24,32},{32,40},{40,48},{48,56},{56,64},{64,7... | collective-permute-start | bytes 3080 | tf_op jit(solution)/shard_map/ppermute | solution.py:18
  142.2 8.5 %collective-permute-start.20 = (f32[2,4,1,32]{3,2,1,0:T(1,128)S(1)}, f32[2,4,1,32]{3,2,1,0:T(1,128)S(1)}, u32[]{:S(2)}, u32[]{:S(2)}) collective-permute-start(f32[2,4,1,32]{3,2,1,0:T(1,128)S(1)} %slice.681), channel_id=1, source_target_pairs={{0,7},{1,0},{2,1},{3,2},{4,3},{5,4},{6,5},{7,6},{8,15},{9,8},{10,9... | collective-permute-start | bytes 3080 | tf_op jit(solution)/shard_map/ppermute | solution.py:18
  151.9 4.4 %collective-permute-start.22 = (f32[2,4,1,32]{3,2,1,0:T(1,128)S(1)}, f32[2,4,1,32]{3,2,1,0:T(1,128)S(1)}, u32[]{:S(2)}, u32[]{:S(2)}) collective-permute-start(f32[2,4,1,32]{3,2,1,0:T(1,128)S(1)} %slice.685), channel_id=1, source_target_pairs={{0,7},{1,0},{2,1},{3,2},{4,3},{5,4},{6,5},{7,6},{8,15},{9,8},{10,9... | collective-permute-start | bytes 3080 | tf_op jit(solution)/shard_map/ppermute | solution.py:18
  159.4 4.4 %collective-permute-start.24 = (f32[1,4,16]{2,1,0:T(4,128)S(1)}, f32[1,4,16]{2,1,0:T(4,128)S(1)}, u32[]{:S(2)}, u32[]{:S(2)}) collective-permute-start(f32[1,4,16]{2,1,0:T(4,128)S(1)} %get-tuple-element.80), channel_id=1, source_target_pairs={{0,504},{8,0},{16,8},{24,16},{32,24},{40,32},{48,40},{56,48},{64,5... | collective-permute-start | bytes 776 | tf_op jit(solution)/shard_map/ppermute | solution.py:18
  163.8 7.9 %collective-permute-start.25 = (f32[1,4,16]{2,1,0:T(4,128)S(1)}, f32[1,4,16]{2,1,0:T(4,128)S(1)}, u32[]{:S(2)}, u32[]{:S(2)}) collective-permute-start(f32[1,4,16]{2,1,0:T(4,128)S(1)} %get-tuple-element.77), channel_id=1, source_target_pairs={{0,8},{8,16},{16,24},{24,32},{32,40},{40,48},{48,56},{56,64},{64,7... | collective-permute-start | bytes 776 | tf_op jit(solution)/shard_map/ppermute | solution.py:18
  171.7 4.6 %collective-permute-start.26 = (f32[1,4,16]{2,1,0:T(4,128)S(1)}, f32[1,4,16]{2,1,0:T(4,128)S(1)}, u32[]{:S(2)}, u32[]{:S(2)}) collective-permute-start(f32[1,4,16]{2,1,0:T(4,128)S(1)} %get-tuple-element.76), channel_id=1, source_target_pairs={{0,504},{8,0},{16,8},{24,16},{32,24},{40,32},{48,40},{56,48},{64,5... | collective-permute-start | bytes 776 | tf_op jit(solution)/shard_map/ppermute | solution.py:18
  176.3 7.6 %collective-permute-start.27 = (f32[1,4,16]{2,1,0:T(4,128)S(1)}, f32[1,4,16]{2,1,0:T(4,128)S(1)}, u32[]{:S(2)}, u32[]{:S(2)}) collective-permute-start(f32[1,4,16]{2,1,0:T(4,128)S(1)} %get-tuple-element.73), channel_id=1, source_target_pairs={{0,8},{8,16},{16,24},{24,32},{32,40},{40,48},{48,56},{56,64},{64,7... | collective-permute-start | bytes 776 | tf_op jit(solution)/shard_map/ppermute | solution.py:18
  184.1 8.4 %collective-permute-start.28 = (f32[2,2,1,16]{3,2,1,0:T(1,128)S(1)}, f32[2,2,1,16]{3,2,1,0:T(1,128)S(1)}, u32[]{:S(2)}, u32[]{:S(2)}) collective-permute-start(f32[2,2,1,16]{3,2,1,0:T(1,128)S(1)} %get-tuple-element.72), channel_id=1, source_target_pairs={{0,7},{1,0},{2,1},{3,2},{4,3},{5,4},{6,5},{7,6},{8,15},{9,8},{10,9... | collective-permute-start | bytes 776 | tf_op jit(solution)/shard_map/ppermute | solution.py:18
  193.8 4.4 %collective-permute-start.30 = (f32[2,2,1,16]{3,2,1,0:T(1,128)S(1)}, f32[2,2,1,16]{3,2,1,0:T(1,128)S(1)}, u32[]{:S(2)}, u32[]{:S(2)}) collective-permute-start(f32[2,2,1,16]{3,2,1,0:T(1,128)S(1)} %get-tuple-element.68), channel_id=1, source_target_pairs={{0,7},{1,0},{2,1},{3,2},{4,3},{5,4},{6,5},{7,6},{8,15},{9,8},{10,9... | collective-permute-start | bytes 776 | tf_op jit(solution)/shard_map/ppermute | solution.py:18
  (8 other events, 9.5 us)
where the time goes:
time: 252 us; the launch traced here: 251 us
  starting transfers between devices  95 us (38%)
  local copies, waits for them, and re-layouts  77.5 us (31%)
  waiting for transfers between devices  72.4 us (29%)
  other arithmetic  5.29 us (2%)
    ppermute x32, starting transfers between devices, passed_along(): lax.ppermute(value, axis, [(i, (i + by) % length) for i in range(length)])  95 us
    ppermute x32, waiting for transfers between devices, passed_along(): lax.ppermute(value, axis, [(i, (i + by) % length) for i in range(length)])  72.4 us
    reshape x1, local copies, waits for them, and re-layouts, alternate(): jnp.transpose(bands, (3, 2, 4, 1, 5, 0))  24.5 us
    transpose x4, local copies, waits for them, and re-layouts, alternate(): jnp.transpose(bands, (3, 2, 4, 1, 5, 0))  20.8 us
    slice x12, local copies, waits for them, and re-layouts, split_axis(): even = lax.slice_in_dim(array, 0, count, 2, axis)  12.9 us
    slice x8, local copies, waits for them, and re-layouts, split_axis(): odd = lax.slice_in_dim(array, 1, count, 2, axis)  12 us
    another operation x3, local copies, waits for them, and re-layouts  5.19 us
  transfers between devices with their start and end apart: 32, of which 32 were waited for; matrix products, arithmetic and copies ran while one was open for 0% of the time, Pallas kernels for 0%

commit v1 on v0

v1 whole, which is shorter than its diff:
```python
import jax
import jax.numpy as jnp
import numpy as np
from jax import lax
from jax.experimental import pallas as pl
from jax.experimental.pallas import tpu as pltpu
from jax.sharding import PartitionSpec as P

LIFT_A, LIFT_B, LIFT_C, LIFT_D = -1.586134342, -0.05298011854, 0.8829110762, 0.4435068522
LIFT_K = 1.149604398
MESH = pl.DeviceIdType.MESH
HIGHEST = lax.Precision.HIGHEST
F32 = jnp.float32

X_COUNT = {0: 20, -1: 8, 1: 8, -2: 2, 2: 2}
X_PAIR = {0: (0, 10), -1: (10, 4), 1: (14, 4), -2: (18, 1), 2: (19, 1)}
Y_ROWS = {0: (0, 24), -1: (24, 8), 1: (32, 8), -2: (40, 8), 2: (48, 8)}
PAIRS, ROWS = 20, 56
OTHERS = [(dx, dy) for dx in (-1, 1, 0, -2, 2) for dy in (0, -1, 1, -2, 2) if (dx, dy) != (0, 0)]


def lift_1d(v):
    even, odd = v[0::2], v[1::2]
    odd = odd + LIFT_A * (even + np.roll(even, -1, 0))
    even = even + LIFT_B * (np.roll(odd, 1, 0) + odd)
    odd = odd + LIFT_C * (even + np.roll(even, -1, 0))
    even = even + LIFT_D * (np.roll(odd, 1, 0) + odd)
    return even / LIFT_K, odd * LIFT_K


def interleave(low, high):
    out = np.empty((2 * low.shape[0], low.shape[1]))
    out[0::2], out[1::2] = low, high
    return out


def operators():
    n, blocks, mid = 32, 16, 8
    low, levels = np.eye(n * blocks), {}
    for level in range(1, 5):
        low, high = lift_1d(low)
        m = n >> level
        levels[level] = interleave(low[mid * m:(mid + 1) * m], high[mid * m:(mid + 1) * m])
    upper = np.concatenate([levels[2], levels[3], levels[4]])
    functional, combine = {}, {}
    for offset, count in X_COUNT.items():
        part = upper[:, (mid + offset) * n:(mid + offset + 1) * n]
        basis = np.linalg.svd(part)[2][:count]
        functional[offset], combine[offset] = basis, part @ basis.T
    fx = np.concatenate([functional[o][h * c // 2:(h + 1) * c // 2] for h in (0, 1) for o, c in X_COUNT.items()])
    cx = np.concatenate([combine[o][:, h * c // 2:(h + 1) * c // 2] for h in (0, 1) for o, c in X_COUNT.items()], 1)
    kx = np.kron(fx, np.eye(8))
    fy, cy = np.zeros((ROWS, 32)), np.zeros((28, ROWS))
    for offset, count in X_COUNT.items():
        at = Y_ROWS[offset][0]
        fy[at:at + count], cy[:, at:at + count] = functional[offset], combine[offset]
    ty = np.zeros((32, ROWS))
    ty[0:8], ty[8:16], ty[16:24], ty[24:32:2] = cy[0:16:2], cy[1:16:2], cy[16:24], cy[24:28]
    tx = [np.stack([np.kron(cx[rows, h * PAIRS:(h + 1) * PAIRS], np.eye(8)) for h in (0, 1)]) for rows in (slice(0, 16), slice(16, 24), slice(24, 28))]
    low, high = lift_1d(np.eye(128))
    z1, zl = interleave(low, high).T, low.T
    zp = np.zeros((2, 128, 128))
    zp[0, :, :64], zp[1, :, 64:] = zl, zl
    low, zu = np.eye(64), np.zeros((3, 2, 128, 128))
    for level in range(3):
        low, high = lift_1d(low)
        for h in (0, 1):
            zu[level, h, 64 * h:64 * (h + 1), ::2 << level] = interleave(low, high).T
    return [np.asarray(m, np.float32) for m in (kx, fy, z1, zp, ty, *tx, zu)]


def dot(a, b):
    return lax.dot_general(a, b, (((1,), (0,)), ((), ())), precision=HIGHEST, preferred_element_type=F32)


def states(s):
    a = s(31) + LIFT_A * s(30)
    b = s(30) + LIFT_B * (s(29) + LIFT_A * (s(28) + s(30)))
    c = s(0)
    d = s(0) + LIFT_B * (s(1) + LIFT_A * (s(0) + s(2)))
    return a, b, c, d


def prepare(v_ref, kx_ref, fy_ref, z1_ref, zp_ref, zt_ref, vo_ref, xh_ref, yh_ref, ch_ref, xf_ref):
    for t in range(4):
        block = v_ref[:, 8 * t:8 * t + 8, :].reshape(256, 128)
        xf_ref[:, 8 * t:8 * t + 8, :] = dot(kx_ref[...], block).reshape(2 * PAIRS, 8, 128)
        zt_ref[:, 8 * t:8 * t + 8, :] = dot(block, z1_ref[...]).reshape(32, 8, 128)
    packed = dot(xf_ref[:PAIRS].reshape(PAIRS * 32, 128), zp_ref[0]) + dot(xf_ref[PAIRS:].reshape(PAIRS * 32, 128), zp_ref[1])
    packed = packed.reshape(PAIRS, 32, 128)
    for p in range(PAIRS):
        vo_ref[p] = dot(fy_ref[...], packed[p])
    for q, plane in enumerate(states(lambda x: zt_ref[x])):
        xh_ref[q] = plane
    for q, rows in enumerate(states(lambda y: zt_ref[:, y, :])):
        yh_ref[q] = rows
    for q in range(4):
        for p, row in enumerate(states(lambda y: xh_ref[q, y:y + 1, :])):
            at = (q // 2) * 2 + p // 2
            ch_ref[at, (q % 2) * 2 + p % 2:(q % 2) * 2 + p % 2 + 1, :] = row
    ch_ref[:, 4:8, :] = jnp.zeros((4, 4, 128), F32)


def exchange(nx, ny, vo_ref, xh_ref, yh_ref, ch_ref, vi_ref, xi_ref, yi_ref, ci_ref, send, recv):
    x, y = lax.axis_index("gx"), lax.axis_index("gy")

    def device(dx, dy):
        return lax.rem(x + dx + nx, nx), lax.rem(y + dy + ny, ny)

    barrier = pltpu.get_barrier_semaphore()
    for dx, dy in OTHERS:
        pl.semaphore_signal(barrier, inc=1, device_id=device(dx, dy), device_id_type=MESH)
    pl.semaphore_wait(barrier, len(OTHERS))
    moves = []
    for dx, dy in OTHERS:
        pieces = []
        if abs(dx) + abs(dy) == 1:
            source, target = (xh_ref, xi_ref) if dx else (yh_ref, yi_ref)
            piece = pl.ds(0 if dx + dy < 0 else 2, 2)
            pieces.append((source.at[piece], target.at[piece]))
        elif abs(dx) == 1 and abs(dy) == 1:
            piece = (dx + 1) + (dy + 1) // 2
            pieces.append((ch_ref.at[piece], ci_ref.at[piece]))
        (p, np_), (r, nr) = X_PAIR[dx], Y_ROWS[dy]
        pieces.append((vo_ref.at[pl.ds(p, np_), pl.ds(r, nr)], vi_ref.at[pl.ds(p, np_), pl.ds(r, nr)]))
        moves += [(source, target, device(-dx, -dy)) for source, target in pieces]
    copies = []
    for i, (source, target, to) in enumerate(moves):
        copy = pltpu.make_async_remote_copy(
            src_ref=source, dst_ref=target, send_sem=send.at[i], recv_sem=recv.at[i], device_id=to, device_id_type=MESH)
        copy.start()
        copies.append(copy)
    for copy in copies:
        copy.wait_recv()
    for copy in copies:
        copy.wait_send()


N_COPIES = 24 + 8


def split_y(p, halo, first, last):
    a, b, c, d = halo
    p0, p1, p2, p3 = p

    def following(v, edge):
        return jnp.where(last, edge, pltpu.roll(v, 7, 0))

    def preceding(v, edge):
        return jnp.where(first, edge, pltpu.roll(v, 1, 0))

    o0 = p1 + LIFT_A * (p0 + p2)
    o1 = p3 + LIFT_A * (p2 + following(p0, c))
    before = a + LIFT_A * p0
    e0 = p0 + LIFT_B * (preceding(o1, before) + o0)
    e1 = p2 + LIFT_B * (o0 + o1)
    q0 = o0 + LIFT_C * (e0 + e1)
    q1 = o1 + LIFT_C * (e1 + following(e0, d + LIFT_B * o1))
    before = before + LIFT_C * (b + LIFT_B * before + e0)
    f0 = e0 + LIFT_D * (preceding(q1, before) + q0)
    f1 = e1 + LIFT_D * (q0 + q1)
    return f0 * (1 / LIFT_K), q0 * LIFT_K, f1 * (1 / LIFT_K), q1 * LIFT_K


def finish(zt_ref, vo_ref, vi_ref, xi_ref, yi_ref, ci_ref, ty_ref, t2_ref, t3_ref, t4_ref, zu_ref, out_ref, ys, tt, up, done, sems):
    sub = lax.broadcasted_iota(jnp.int32, (8, 128), 0)
    lane = lax.broadcasted_iota(jnp.int32, (8, 128), 1)
    first, last = sub == 0, sub == 7

    def row(ref, *at):
        return jnp.broadcast_to(ref[(*at[:-1], pl.ds(at[-1], 1), slice(None))], (8, 128))

    own_p, own_r = X_PAIR[0][1], Y_ROWS[0][1]
    for p in range(PAIRS):
        if p < own_p:
            v = jnp.concatenate([vo_ref[p, 0:own_r, :], vi_ref[p, own_r:ROWS, :]], 0)
        else:
            v = vi_ref[p]
        r = dot(ty_ref[...], v)
        for t in range(4):
            tt[t, p] = r[8 * t:8 * t + 8]

    def upper(t_ref, t, level):
        v = tt[t].reshape(PAIRS * 8, 128)
        return dot(dot(t_ref[0], v), zu_ref[level, 0]) + dot(dot(t_ref[1], v), zu_ref[level, 1])

    l2 = [upper(t2_ref, t, 0).reshape(16, 8, 128) for t in (0, 1)]
    l3 = upper(t3_ref, 2, 1).reshape(8, 8, 128)
    l4 = upper(t4_ref, 3, 2).reshape(4, 8, 128)
    for i in range(16):
        for t in (0, 1):
            v = l2[t][i]
            if i % 2 == 0 and t == 0:
                w = l3[i // 2]
                if i % 4 == 0:
                    w = jnp.where((lane % 8 == 0) & (sub % 2 == 0), l4[i // 4], w)
                v = jnp.where(lane % 4 == 0, w, v)
            up[i, t] = v

    for x in range(36):
        if 2 <= x < 34:
            p = [zt_ref[x - 2, pl.ds(r, 8, 4), :] for r in range(4)]
            halo = [row(yi_ref, q, x - 2) for q in range(4)]
        else:
            q = x if x < 2 else x - 32
            p = [xi_ref[q, pl.ds(r, 8, 4), :] for r in range(4)]
            at = 2 * (q // 2)
            halo = [row(ci_ref, at + k // 2, (q % 2) * 2 + k % 2) for k in range(4)]
        for r, v in enumerate(split_y(p, halo, first, last)):
            ys[x, r] = v

    odd_lane = lane % 2 == 1
    state = {}
    copies = []
    for r in range(4):
        before = ys[0, r] + LIFT_A * ys[2, r]
        state[r] = (before, ys[1, r] + LIFT_B * before, None)
    for i in range(17):
        for r in range(4):
            o, e, q = state[r]
            if i < 16:
                p = ys[2 + 2 * i, r]
                o_now = ys[3 + 2 * i, r] + LIFT_A * (p + ys[4 + 2 * i, r])
                e_now = p + LIFT_B * (o + o_now)
            else:
                o_now, e_now = None, ys[35, r] + LIFT_B * o
            q_now = o + LIFT_C * (e + e_now)
            if i > 0:
                low = (e + LIFT_D * (q + q_now)) * (1 / LIFT_K)
                if r % 2 == 0:
                    low = jnp.where(odd_lane, low, up[i - 1, r // 2])
                done[2 * i - 2, pl.ds(r, 8, 4), :] = low
                done[2 * i - 1, pl.ds(r, 8, 4), :] = q_now * LIFT_K
            state[r] = (o_now, e_now, q_now)
        if i in (4, 8, 12, 16):
            piece = pl.ds(2 * i - 8, 8)
            copy = pltpu.make_async_copy(done.at[piece], out_ref.at[piece], sems.at[i // 4 - 1])
            copy.start()
            copies.append(copy)
    for copy in copies:
        copy.wait()


def solution(mesh):
    nx, ny = mesh.shape["gx"], mesh.shape["gy"]
    kx, fy, z1, zp, ty, t2, t3, t4, zu = operators()
    vmem = pl.BlockSpec(memory_space=pltpu.VMEM)
    limit = 24 * 1024 * 1024
    halos = [(PAIRS, ROWS, 128), (4, 32, 128), (4, 32, 128), (4, 8, 128)]

    def local(v):
        zt, vo, xh, yh, ch = pl.pallas_call(
            prepare,
            out_shape=[KEEP(s, F32) for s in [(32, 32, 128), *halos]],
            in_specs=[vmem] * 5, out_specs=[vmem] * 5,
            scratch_shapes=[pltpu.VMEM((2 * PAIRS, 32, 128), F32)],
            compiler_params=pltpu.CompilerParams(vmem_limit_bytes=limit),
        )(v, kx, fy, z1, zp)
        vi, xi, yi, ci = pl.pallas_call(
            lambda *refs: exchange(nx, ny, *refs),
            out_shape=[KEEP(s, F32) for s in halos],
            in_specs=[vmem] * 4, out_specs=[vmem] * 4,
            scratch_shapes=[pltpu.SemaphoreType.DMA((N_COPIES,)), pltpu.SemaphoreType.DMA((N_COPIES,))],
            compiler_params=pltpu.CompilerParams(collective_id=0, has_side_effects=True, vmem_limit_bytes=limit),
        )(vo, xh, yh, ch)
        return pl.pallas_call(
            finish,
            out_shape=jax.ShapeDtypeStruct((32, 32, 128), F32),
            in_specs=[vmem] * 11, out_specs=pl.BlockSpec(memory_space=pl.ANY),
            scratch_shapes=[
                pltpu.VMEM((36, 4, 8, 128), F32), pltpu.VMEM((4, PAIRS, 8, 128), F32), pltpu.VMEM((16, 2, 8, 128), F32),
                pltpu.VMEM((32, 32, 128), F32), pltpu.SemaphoreType.DMA((4,))],
            compiler_params=pltpu.CompilerParams(vmem_limit_bytes=limit),
        )(zt, vo, vi, xi, yi, ci, ty, t2, t3, t4, zu)

    spec = P("gx", "gy", None)
    return jax.shard_map(local, mesh=mesh, in_specs=(spec,), out_specs=spec, check_vma=False)


def KEEP(shape, dtype):
    return pltpu.VMEM(shape, dtype)
```

time: 252 us -> 34.3 us (0.14)
  starting transfers between devices: 95 us -> 0 us
  local copies, waits for them, and re-layouts: 77.5 us -> 4.53 us
  waiting for transfers between devices: 72.4 us -> 0 us
  Pallas kernels: 0 us -> 29.4 us
  other arithmetic: 5.29 us -> 0 us
    ppermute x32 -> x0, starting transfers between devices: 95 us -> none  [passed_along(): lax.ppermute(value, axis, [(i, (i + by) % length) for i in range(length)])]
    ppermute x32 -> x0, waiting for transfers between devices: 72.4 us -> none  [passed_along(): lax.ppermute(value, axis, [(i, (i + by) % length) for i in range(length)])]
    pallas_call x0 -> x3, Pallas kernels: none -> 29.4 us  [the longest x1 22.1 us: local(): pl.pallas_call(lambda *refs: exchange(nx, ny, *refs), out_shape=[KEEP(s,...]
    slice x86 -> x0, local copies, waits for them, and re-layouts: 27 us -> none  [the longest x12 12.9 us: split_axis(): even = lax.slice_in_dim(array, 0, count, 2, axis)]
    reshape x1 -> x0, local copies, waits for them, and re-layouts: 24.5 us -> none  [alternate(): jnp.transpose(bands, (3, 2, 4, 1, 5, 0))]
    transpose x4 -> x0, local copies, waits for them, and re-layouts: 20.8 us -> none  [alternate(): jnp.transpose(bands, (3, 2, 4, 1, 5, 0))]
    another operation x3 -> x0, local copies, waits for them, and re-layouts: 5.19 us -> none
    unnamed x0 -> x20, local copies, waits for them, and re-layouts: none -> 4.53 us
  transfers between devices with their start and end apart: 32 -> 0, of which waited for: 32 -> 0; matrix products, arithmetic and copies ran while one was open for 0% -> 0% of each run, Pallas kernels for 0% -> 0%
where the time goes in v1:
time: 34.3 us; the launch traced here: 34 us
  Pallas kernels  29.4 us (86%)
  local copies, waits for them, and re-layouts  4.53 us (13%)
    pallas_call x1, Pallas kernels, local(): pl.pallas_call(lambda *refs: exchange(nx, ny, *refs), out_shape=[KEEP(s,...  22.1 us
    unnamed x20, local copies, waits for them, and re-layouts  4.53 us
    pallas_call x1, Pallas kernels, local(): pl.pallas_call(prepare, out_shape=[KEEP(s, F32) for s in [(32, 32, 128),...  4.12 us
    pallas_call x1, Pallas kernels, local(): pl.pallas_call(finish, out_shape=jax.ShapeDtypeStruct((32, 32, 128), F32)...  3.08 us

profile of v1, /device:TPU:1, one launch (start us, length us, event | category | flops | bytes accessed | tf_op | source)
XLA Modules:
  0.0 34.0 jit_solution(17977381093021494238)
XLA Ops:
  0.0 0.0 copy-start
  0.0 1.0 %copy-done = f32[32,32,128]{2,1,0:T(8,128)S(1)} copy-done((f32[32,32,128]{2,1,0:T(8,128)S(1)}, f32[32,32,128]{2,1,0:T(8,128)}, u32[]{:S(2)}) %copy-start) | copy-done | bytes 524312
  1.0 0.0 copy-start.2
  1.0 1.0 %copy-done.2 = f32[320,256]{1,0:T(8,128)S(1)} copy-done((f32[320,256]{1,0:T(8,128)S(1)}, f32[320,256]{1,0:T(8,128)}, u32[]{:S(2)}) %copy-start.2) | copy-done | bytes 327704
  2.0 0.0 copy-start.5
  2.0 0.9 %copy-done.5 = f32[2,128,128]{2,1,0:T(8,128)S(1)} copy-done((f32[2,128,128]{2,1,0:T(8,128)S(1)}, f32[2,128,128]{2,1,0:T(8,128)}, u32[]{:S(2)}) %copy-start.5) | copy-done | bytes 131096
  2.9 0.0 copy-start.7
  2.9 0.8 %copy-done.7 = f32[128,128]{1,0:T(8,128)S(1)} copy-done((f32[128,128]{1,0:T(8,128)S(1)}, f32[128,128]{1,0:T(8,128)}, u32[]{:S(2)}) %copy-start.7) | copy-done | bytes 65560
  3.8 0.0 copy-start.8
  3.8 0.7 %copy-done.8 = f32[56,32]{1,0:T(8,128)S(1)} copy-done((f32[56,32]{1,0:T(8,128)S(1)}, f32[56,32]{1,0:T(8,128)}, u32[]{:S(2)}) %copy-start.8) | copy-done | bytes 7192
  4.5 0.0 copy-start.4
  4.5 4.1 %shard_map.100 = (f32[32,32,128]{2,1,0:T(8,128)S(1)}, f32[20,56,128]{2,1,0:T(8,128)S(1)}, f32[4,32,128]{2,1,0:T(8,128)S(1)}, f32[4,32,128]{2,1,0:T(8,128)S(1)}, f32[4,8,128]{2,1,0:T(8,128)S(1)}) custom-call(f32[32,32,128]{2,1,0:T(8,128)S(1)} %copy-done, f32[320,256]{1,0:T(8,128)S(1)} %copy-done.2, f32[56,32]{1,0:T(8,128)S(1)} %copy-done.8, ...), custom_call_target="tpu_custom_call" | custom-call | tf_op jit(solution)/shard_map/pallas_call | solution.py:252
  8.6 0.0 copy-start.1
  8.6 0.0 copy-start.3
  8.7 0.0 copy-start.6
  8.7 0.0 copy-start.9
  8.7 22.1 %shard_map.101 = (f32[20,56,128]{2,1,0:T(8,128)S(1)}, f32[4,32,128]{2,1,0:T(8,128)S(1)}, f32[4,32,128]{2,1,0:T(8,128)S(1)}, f32[4,8,128]{2,1,0:T(8,128)S(1)}) custom-call(f32[20,56,128]{2,1,0:T(8,128)S(1)} %get-tuple-element.15.refs_0_.vo_ref, f32[4,32,128]{2,1,0:T(8,128)S(1)} %get-tuple-element.16.refs_1_, f32[4,32,128]{2,1,0:T(8,128)S(1)} %get-tuple-element.17.refs_2_, ...), custom_call_target="tpu_custom_call" | custom-call | tf_op jit(solution)/shard_map/pallas_call | solution.py:259
  30.8 0.0 copy-done.4
  30.9 0.0 copy-done.1
  30.9 0.0 copy-done.3
  30.9 0.0 copy-done.6
  30.9 0.0 copy-done.9
  30.9 3.1 %shard_map.102 = f32[32,32,128]{2,1,0:T(8,128)} custom-call(f32[32,32,128]{2,1,0:T(8,128)S(1)} %get-tuple-element.14.zt_ref, f32[20,56,128]{2,1,0:T(8,128)S(1)} %get-tuple-element.15.refs_0_.vo_ref, f32[20,56,128]{2,1,0:T(8,128)S(1)} %get-tuple-element.19.vi_ref, f32[4,32,128]{2,1,0:T(8,128)S(1)} %get-tuple-element.20.xi_ref, ...), custom_call_target="tpu_custom_call" | custom-call | tf_op jit(solution)/shard_map/pallas_call | solution.py:266
Async XLA Ops:
  0.0 1.0 %copy-start = (f32[32,32,128]{2,1,0:T(8,128)S(1)}, f32[32,32,128]{2,1,0:T(8,128)}, u32[]{:S(2)}) copy-start(f32[32,32,128]{2,1,0:T(8,128)} %v_ref.1) | copy-start | bytes 1572868
  1.0 1.0 %copy-start.2 = (f32[320,256]{1,0:T(8,128)S(1)}, f32[320,256]{1,0:T(8,128)}, u32[]{:S(2)}) copy-start(f32[320,256]{1,0:T(8,128)} %constant.18.clone.kx_ref) | copy-start | bytes 983044
  2.0 0.9 %copy-start.5 = (f32[2,128,128]{2,1,0:T(8,128)S(1)}, f32[2,128,128]{2,1,0:T(8,128)}, u32[]{:S(2)}) copy-start(f32[2,128,128]{2,1,0:T(8,128)} %constant.21.clone.zp_ref) | copy-start | bytes 393220
  2.9 0.8 %copy-start.7 = (f32[128,128]{1,0:T(8,128)S(1)}, f32[128,128]{1,0:T(8,128)}, u32[]{:S(2)}) copy-start(f32[128,128]{1,0:T(8,128)} %constant.20.clone.z1_ref) | copy-start | bytes 196612
  3.8 0.7 %copy-start.8 = (f32[56,32]{1,0:T(8,128)S(1)}, f32[56,32]{1,0:T(8,128)}, u32[]{:S(2)}) copy-start(f32[56,32]{1,0:T(8,128)} %constant.19.clone.fy_ref) | copy-start | bytes 21508
  4.5 26.3 %copy-start.4 = (f32[2,64,160]{2,1,0:T(8,128)S(1)}, f32[2,64,160]{2,1,0:T(8,128)}, u32[]{:S(2)}) copy-start(f32[2,64,160]{2,1,0:T(8,128)} %constant.24.clone.t3_ref) | copy-start | bytes 245764
  8.6 22.2 %copy-start.1 = (f32[3,2,128,128]{3,2,1,0:T(8,128)S(1)}, f32[3,2,128,128]{3,2,1,0:T(8,128)}, u32[]{:S(2)}) copy-start(f32[3,2,128,128]{3,2,1,0:T(8,128)} %constant.26.clone.zu_ref) | copy-start | bytes 1179652
  8.6 22.2 %copy-start.3 = (f32[2,128,160]{2,1,0:T(8,128)S(1)}, f32[2,128,160]{2,1,0:T(8,128)}, u32[]{:S(2)}) copy-start(f32[2,128,160]{2,1,0:T(8,128)} %constant.23.clone.t2_ref) | copy-start | bytes 491524
  8.7 22.2 %copy-start.6 = (f32[2,32,160]{2,1,0:T(8,128)S(1)}, f32[2,32,160]{2,1,0:T(8,128)}, u32[]{:S(2)}) copy-start(f32[2,32,160]{2,1,0:T(8,128)} %constant.25.clone.t4_ref) | copy-start | bytes 122884
  8.7 22.2 %copy-start.9 = (f32[32,56]{1,0:T(8,128)S(1)}, f32[32,56]{1,0:T(8,128)}, u32[]{:S(2)}) copy-start(f32[32,56]{1,0:T(8,128)} %constant.22.clone.ty_ref) | copy-start | bytes 21508

commit v2 on v1

v2 whole, which is shorter than its diff:
```python
import functools

import jax
import jax.numpy as jnp
import ml_dtypes
import numpy as np
from jax import lax
from jax.experimental import pallas as pl
from jax.experimental.pallas import tpu as pltpu
from jax.sharding import PartitionSpec as P

LIFT_A, LIFT_B, LIFT_C, LIFT_D = -1.586134342, -0.05298011854, 0.8829110762, 0.4435068522
LIFT_K = 1.149604398
MESH = pl.DeviceIdType.MESH
F32, BF16 = jnp.float32, jnp.bfloat16

COUNT = {0: 20, 1: 8, 2: 2, -1: 8, -2: 2}
X_AT = {0: 0, 1: 18, 2: 24, -1: 25, -2: 31}
Y_AT = {0: 0, -1: 32, 1: 40, -2: 48, 2: 56}
ENTRIES, ROWS = 32, 64
PAIRS = [X_AT[o] + p for o, c in COUNT.items() for p in range(c // 2)]
EARLY = 15
Y_STATES = 10
X_STATES = {1: 22, -1: 29}
OFFSETS = (0, -1, 1, -2, 2)
GROUP = {dx: [(dx, dy) for dy in OFFSETS if (dx, dy) != (0, 0)] for dx in OFFSETS}


def pieces(dx, dy):
    rows = (Y_AT[dy], 8)
    if dx == 0:
        return [((0, 18 if abs(dy) == 1 else 2), rows)]
    if abs(dx) == 2:
        return [((X_AT[dx], 1), rows)]
    if dy == 0:
        return [((X_STATES[dx], 2), (0, 32)), ((X_AT[dx], 4), (0, 24))]
    return [((X_AT[dx], 5 if abs(dy) == 1 else 2), rows)]


MOVES = [(o, piece) for dx in OFFSETS for o in GROUP[dx] for piece in pieces(*o)]


def lift_1d(v):
    even, odd = v[0::2], v[1::2]
    odd = odd + LIFT_A * (even + np.roll(even, -1, 0))
    even = even + LIFT_B * (np.roll(odd, 1, 0) + odd)
    odd = odd + LIFT_C * (even + np.roll(even, -1, 0))
    even = even + LIFT_D * (np.roll(odd, 1, 0) + odd)
    return even / LIFT_K, odd * LIFT_K


def interleave(low, high):
    out = np.empty((2 * low.shape[0], low.shape[1]))
    out[0::2], out[1::2] = low, high
    return out


def row_space(parts, count):
    basis = np.zeros((0, parts[0].shape[1]))
    for part in parts:
        rest = part - part @ basis.T @ basis
        size, rows = np.linalg.svd(rest)[1:]
        basis = np.concatenate([basis, rows[:int((size > 1e-9).sum())]])
    return np.concatenate([basis, np.zeros((count - len(basis), basis.shape[1]))])


def halves(matrix):
    high = np.asarray(matrix, np.float32).astype(ml_dtypes.bfloat16)
    return high, (np.asarray(matrix, np.float32) - high.astype(np.float32)).astype(ml_dtypes.bfloat16)


def operators():
    n, blocks, mid = 32, 16, 8
    low, levels = np.eye(n * blocks), {}
    for level in range(1, 5):
        low, high = lift_1d(low)
        m = n >> level
        levels[level] = interleave(low[mid * m:(mid + 1) * m], high[mid * m:(mid + 1) * m])
    functional, combine = {}, {}
    for offset, count in COUNT.items():
        parts = [levels[level][:, (mid + offset) * n:(mid + offset + 1) * n] for level in (4, 3, 2)]
        functional[offset] = row_space(parts, count)
        combine[offset] = np.concatenate(parts[::-1]) @ functional[offset].T
    fx = np.concatenate([functional[o][h::2] for h in (0, 1) for o in COUNT])
    kx = np.stack(halves(np.kron(fx, np.eye(8))))
    cx = [np.concatenate([combine[o][:, h::2] for o in COUNT], 1) for h in (0, 1)]
    early, late = [np.stack([np.kron(c[:, part], np.eye(8)) for c in cx]) for part in (slice(0, EARLY), slice(EARLY, None))]
    (high, low), (late_high, late_low) = halves(early), halves(late)
    early = np.stack([np.concatenate([high, high], 2), np.concatenate([low, np.zeros_like(low)], 2)])
    late = np.concatenate([late_high, late_high, late_low], 2)
    fy, cy = np.zeros((ROWS, 32)), np.zeros((28, ROWS))
    for offset, count in COUNT.items():
        at = Y_AT[offset]
        fy[at:at + count], cy[:, at:at + count] = functional[offset], combine[offset]
    ty = np.zeros((32, ROWS))
    ty[0:8], ty[8:16], ty[16:24], ty[24:32:2] = cy[0:16:2], cy[1:16:2], cy[16:24], cy[24:28]
    fy, ty = [np.concatenate([h, h, l], 1) for h, l in (halves(fy), halves(ty))]
    low, high = lift_1d(np.eye(128))
    z1 = wide(interleave(low, high).T)
    zp = np.concatenate(halves(np.kron(np.eye(2), low.T)), 1)
    low, zu = np.eye(64), np.zeros((3, 64, 128))
    for level in range(3):
        low, high = lift_1d(low)
        zu[level, :, ::2 << level] = interleave(low, high).T
    zu = np.stack([wide(np.concatenate([m, m])) for m in zu])
    return [tiles(m) for m in (kx, fy, z1, zp, ty, early, late, zu)]


def wide(matrix):
    high, low = halves(matrix)
    return np.concatenate([np.concatenate([high, high]), np.concatenate([low, np.zeros_like(low)])], 1)


def tiles(matrix):
    columns = -(-matrix.shape[-1] // 128) * 128
    padded = np.zeros((*matrix.shape[:-1], columns), matrix.dtype)
    padded[..., :matrix.shape[-1]] = matrix
    return np.moveaxis(padded.reshape(*matrix.shape[:-1], columns // 128, 128), -2, -3)


def whole(ref, *at, rows=slice(None), columns=None):
    count = ref.shape[len(at)]
    out = ref[(*at, 0, rows)] if count == 1 else jnp.concatenate([ref[(*at, i, rows)] for i in range(count)], 1)
    return out if columns is None else out[:, :columns]


def dot(a, b):
    return lax.dot_general(a, b, (((1,), (0,)), ((), ())), preferred_element_type=F32)


def split(v):
    high = v.astype(BF16)
    return high, (v - high.astype(F32)).astype(BF16)


def stacked(v):
    high, low = split(v)
    return jnp.concatenate([high, low, high], 0)


def wide_dot(v, ref, *at):
    v = dot(jnp.concatenate(split(v), 1), whole(ref, *at))
    return v[:, :128] + v[:, 128:]


def states(s):
    a = s(31) + LIFT_A * s(30)
    b = s(30) + LIFT_B * (s(29) + LIFT_A * (s(28) + s(30)))
    c = s(0)
    d = s(0) + LIFT_B * (s(1) + LIFT_A * (s(0) + s(2)))
    return a, b, c, d


def prepare(v_hbm, kx_hbm, fy_hbm, z1_hbm, zp_hbm, v_ref, vo_ref, kx_ref, fy_ref, z1_ref, zp_ref, xh, sems):
    loads = [pltpu.make_async_copy(v_hbm.at[:, pl.ds(8 * t, 8)], v_ref.at[:, pl.ds(8 * t, 8)], sems.at[t]) for t in range(4)]
    for i, (source, target) in enumerate(((kx_hbm, kx_ref), (zp_hbm, zp_ref), (fy_hbm, fy_ref), (z1_hbm, z1_ref))):
        loads.append(pltpu.make_async_copy(source, target, sems.at[4 + i]))
    for i in (4, 0, 1, 2, 3, 5, 6, 7):
        loads[i].start()
    loads[4].wait()
    parts = [[], []]
    for t in (0, 2):
        loads[t].wait()
        loads[t + 1].wait()
        high, low = split(jnp.concatenate([v_ref[:, 8 * u:8 * u + 8, :].reshape(256, 128) for u in (t, t + 1)], 1))
        x = dot(whole(kx_ref, 0), high) + dot(whole(kx_ref, 0), low) + dot(whole(kx_ref, 1), high)
        for u in (0, 1):
            for h in (0, 1):
                parts[h].append(x[160 * h:160 * h + 160, 128 * u:128 * u + 128])
    loads[5].wait()
    high, low = split(jnp.concatenate([jnp.concatenate(part, 0) for part in parts], 1))
    packed = dot(high, whole(zp_ref))
    packed = packed[:, :128] + packed[:, 128:] + dot(low, zp_ref[0])
    loads[6].wait()
    for i in range(0, len(PAIRS), 2):
        columns = [stacked(jnp.concatenate([packed[160 * t + 8 * j:160 * t + 8 * j + 8] for t in range(4)], 0)) for j in (i, i + 1)]
        rows = dot(whole(fy_ref, columns=96), jnp.concatenate(columns, 1))
        vo_ref[PAIRS[i]] = rows[:, :128]
        vo_ref[PAIRS[i + 1]] = rows[:, 128:]
    loads[7].wait()
    planes = [*states(lambda x: v_ref[x]), *states(lambda y: v_ref[:, y, :])]
    planes = wide_dot(jnp.concatenate(planes, 0), z1_ref)
    for q in range(4):
        plane, rows = planes[32 * q:32 * q + 32], planes[128 + 32 * q:160 + 32 * q]
        xh[q] = plane
        vo_ref[X_STATES[-1 if q < 2 else 1] + q % 2, 0:32, :] = plane
        at = Y_AT[-1 if q < 2 else 1]
        for t in range(4):
            vo_ref[Y_STATES + 4 * (q % 2) + t, at:at + 8, :] = rows[8 * t:8 * t + 8]
    for q in range(4):
        for p, row in enumerate(states(lambda y: xh[q, y:y + 1, :])):
            at = Y_AT[-1 if p < 2 else 1] + 2 * (q % 2) + p % 2
            vo_ref[X_STATES[-1 if q < 2 else 1], at:at + 1, :] = row
    for e in X_STATES.values():
        for dy in (-1, 1):
            vo_ref[e, Y_AT[dy] + 4:Y_AT[dy] + 8, :] = jnp.zeros((4, 128), F32)


def split_y(p, halo, first, last):
    a, b, c, d = halo
    p0, p1, p2, p3 = p

    def following(v, edge):
        return jnp.where(last, edge, pltpu.roll(v, 7, 0))

    def preceding(v, edge):
        return jnp.where(first, edge, pltpu.roll(v, 1, 0))

    o0 = p1 + LIFT_A * (p0 + p2)
    o1 = p3 + LIFT_A * (p2 + following(p0, c))
    before = a + LIFT_A * p0
    e0 = p0 + LIFT_B * (preceding(o1, before) + o0)
    e1 = p2 + LIFT_B * (o0 + o1)
    q0 = o0 + LIFT_C * (e0 + e1)
    q1 = o1 + LIFT_C * (e1 + following(e0, d + LIFT_B * o1))
    before = before + LIFT_C * (b + LIFT_B * before + e0)
    f0 = e0 + LIFT_D * (preceding(q1, before) + q0)
    f1 = e1 + LIFT_D * (q0 + q1)
    return f0 * (1 / LIFT_K), q0 * LIFT_K, f1 * (1 / LIFT_K), q1 * LIFT_K


def exchange(nx, ny, nz, v_ref, vo_ref, z1_hbm, ty_hbm, te_hbm, tl_hbm, zu_hbm, ys_ref, tl_out, e2_ref, e34_ref, tl_ref, zu_ref,
             vi_ref, z1_ref, ty_ref, te_ref, te_in, zt, send, recv, hello, sems):
    x, y = lax.axis_index("gx"), lax.axis_index("gy")
    z = lax.rem(x, nz)

    def device(dx, dy):
        return lax.rem(x + dx + nx, nx), lax.rem(y + dy + ny, ny)

    copies = {dx: [] for dx in OFFSETS}
    for i, ((dx, dy), ((e, ne), (r, nr))) in enumerate(MOVES):
        at = (pl.ds(e, ne), pl.ds(r, nr))
        copies[dx].append(pltpu.make_async_remote_copy(
            src_ref=vo_ref.at[at], dst_ref=vi_ref.at[at], send_sem=send.at[i], recv_sem=recv.at[i],
            device_id=device(-dx, -dy), device_id_type=MESH))

    def start(dx):
        for copy in copies[dx]:
            copy.start()

    def arrive(dx):
        for copy in copies[dx]:
            copy.wait_recv()

    barrier = pltpu.get_barrier_semaphore()

    def greet(dx):
        for o in GROUP[dx]:
            pl.semaphore_signal(barrier, inc=1, device_id=device(*o), device_id_type=MESH)

    greet(-2)
    pl.when(z != nz - 1)(lambda: greet(-1))
    pl.when(z < nz - 2)(lambda: greet(0))
    pl.when(z < nz - 3)(lambda: greet(1))
    pl.when(z < nz - 4)(lambda: greet(2))
    loads = [pltpu.make_async_copy(a, b, sems.at[i]) for i, (a, b) in enumerate(
        ((z1_hbm, z1_ref), (ty_hbm, ty_ref), (te_hbm, te_ref), (tl_hbm, tl_ref), (zu_hbm, zu_ref)))]
    for load in loads:
        load.start()
    for e in PAIRS:
        if e in (X_AT[2], X_AT[-2]):
            vi_ref[e, 8:24, :] = jnp.zeros((16, 128), F32)
        elif e not in (0, 1, X_AT[1], X_AT[1] + 1, X_AT[-1], X_AT[-1] + 1):
            vi_ref[e, 48:64, :] = jnp.zeros((16, 128), F32)
    greeted = jnp.where(z == 0, 14, jnp.where(z == 1, 19, jnp.where(z < nz - 2, 24, jnp.where(z == nz - 2, 5, 10))))
    pl.semaphore_wait(barrier, greeted)
    pl.when(z != nz - 2)(lambda: start(-1))
    start(-2)

    def say_hello(dx):
        for dy in range(-2, 3):
            pl.semaphore_signal(hello.at[dx - 1], inc=1, device_id=device(dx, dy), device_id_type=MESH)

    pl.when(z == nz - 1)(lambda: say_hello(1))
    pl.when(z >= nz - 2)(lambda: say_hello(2))

    @pl.when(z < nz - 2)
    def _():
        start(0)
        pl.when(z > 0)(lambda: start(1))
        pl.when(z > 1)(lambda: start(2))

    loads[0].wait()
    for t in range(4):
        zt[:, 8 * t:8 * t + 8, :] = wide_dot(v_ref[:, 8 * t:8 * t + 8, :].reshape(256, 128), z1_ref).reshape(32, 8, 128)

    @pl.when(z == nz - 2)
    def _():
        arrive(-1)
        start(-1)
        start(1)
        start(0)
        arrive(-2)
        start(2)

    @pl.when(z == nz - 1)
    def _():
        arrive(-2)
        start(0)
        start(2)
        arrive(-1)
        start(1)

    sub = lax.broadcasted_iota(jnp.int32, (8, 128), 0)
    first, last = sub == 0, sub == 7

    def plane(x):
        if 2 <= x < 34:
            x = x - 2
            p = [zt[x, pl.ds(r, 8, 4), :] for r in range(4)]
            at = [(Y_STATES + 4 * (k % 2) + x // 8, Y_AT[-1 if k < 2 else 1] + x % 8) for k in range(4)]
            x = x + 2
        else:
            dx, q = (-1, x) if x < 2 else (1, x - 34)
            p = [vi_ref[X_STATES[dx] + q, pl.ds(r, 8, 4), :] for r in range(4)]
            at = [(X_STATES[dx], Y_AT[-1 if k < 2 else 1] + 2 * q + k % 2) for k in range(4)]
        halo = [jnp.broadcast_to(vi_ref[e, pl.ds(r, 1), :], (8, 128)) for e, r in at]
        for r, v in enumerate(split_y(p, halo, first, last)):
            ys_ref[x, r] = v

    def upper(first_pair, count, out_ref):
        done = []
        for i in range(first_pair, first_pair + count):
            e = PAIRS[i]
            v = vi_ref[e]
            own = vo_ref[e, 0:32, :] if i < COUNT[0] // 2 else jnp.concatenate([v[0:24], jnp.zeros((8, 128), F32)], 0)
            done.append(stacked(jnp.concatenate([own, v[32:]], 0)))
        for i in range(0, count, 2):
            r = dot(whole(ty_ref, columns=192), jnp.concatenate(done[i:i + 2], 1))
            for j in range(min(2, count - i)):
                for t in range(4):
                    out_ref[t // 2, first_pair % EARLY + i + j, :, 128 * (t % 2):128 * (t % 2) + 128] = r[8 * t:8 * t + 8, 128 * j:128 * j + 128]

    loads[1].wait()
    arrive(0)
    for x in range(2, 34):
        plane(x)
    upper(0, 10, te_in)
    arrive(1)
    plane(34)
    plane(35)
    arrive(2)
    upper(10, 5, te_in)
    loads[2].wait()
    for u, (ref, at, rows) in enumerate(((e2_ref, 0, 128), (e34_ref, 128, 96))):
        high, low = split(te_in[u].reshape(8 * EARLY, 256))
        v = jnp.concatenate([high, low], 0)
        v = [dot(whole(te_ref, 0, h, rows=slice(at, at + rows), columns=240), v)
             + dot(whole(te_ref, 1, h, rows=slice(at, at + rows), columns=120), high) for h in (0, 1)]
        ref[...] = jnp.where(lax.broadcasted_iota(jnp.int32, (rows, 256), 1) % 128 < 64, v[0], v[1])

    @pl.when(z == 0)
    def _():
        pl.semaphore_wait(hello.at[0], 5)
        start(1)

    @pl.when(z < 2)
    def _():
        pl.semaphore_wait(hello.at[1], 5)
        start(2)

    @pl.when(z < nz - 2)
    def _():
        arrive(-1)
        arrive(-2)

    plane(0)
    plane(1)
    upper(15, 5, tl_out)
    loads[3].wait()
    loads[4].wait()
    for dx in OFFSETS:
        for copy in copies[dx]:
            copy.wait_send()


def finish(ys, tl, e2_ref, e34_ref, tl_ref, zu_ref, out_ref, up, done, sems):
    sub = lax.broadcasted_iota(jnp.int32, (8, 128), 0)
    lane = lax.broadcasted_iota(jnp.int32, (8, 128), 1)

    def upper(u, at, rows, early):
        v = stacked(tl[u].reshape(8 * (len(PAIRS) - EARLY), 256))
        v = [dot(whole(tl_ref, h, rows=slice(at, at + rows), columns=120), v) for h in (0, 1)]
        return early + jnp.where(lax.broadcasted_iota(jnp.int32, (rows, 256), 1) % 128 < 64, v[0], v[1])

    v = upper(0, 0, 128, e2_ref[...])
    l2 = wide_dot(jnp.concatenate([v[:, :128], v[:, 128:]], 0), zu_ref, 0).reshape(2, 16, 8, 128)
    v = upper(1, 128, 96, e34_ref[...])
    l3 = wide_dot(v[:64, :128], zu_ref, 1).reshape(8, 8, 128)
    l4 = wide_dot(v[64:, 128:], zu_ref, 2).reshape(4, 8, 128)
    for i in range(16):
        for t in (0, 1):
            v = l2[t][i]
            if i % 2 == 0 and t == 0:
                w = l3[i // 2]
                if i % 4 == 0:
                    w = jnp.where((lane % 8 == 0) & (sub % 2 == 0), l4[i // 4], w)
                v = jnp.where(lane % 4 == 0, w, v)
            up[i, t] = v

    odd_lane = lane % 2 == 1
    state = {}
    copies = []
    for r in range(4):
        before = ys[0, r] + LIFT_A * ys[2, r]
        state[r] = (before, ys[1, r] + LIFT_B * before, None)
    for i in range(17):
        for r in range(4):
            o, e, q = state[r]
            if i < 16:
                p = ys[2 + 2 * i, r]
                o_now = ys[3 + 2 * i, r] + LIFT_A * (p + ys[4 + 2 * i, r])
                e_now = p + LIFT_B * (o + o_now)
            else:
                o_now, e_now = None, ys[35, r] + LIFT_B * o
            q_now = o + LIFT_C * (e + e_now)
            if i > 0:
                low = (e + LIFT_D * (q + q_now)) * (1 / LIFT_K)
                if r % 2 == 0:
                    low = jnp.where(odd_lane, low, up[i - 1, r // 2])
                done[2 * i - 2, pl.ds(r, 8, 4), :] = low
                done[2 * i - 1, pl.ds(r, 8, 4), :] = q_now * LIFT_K
            state[r] = (o_now, e_now, q_now)
        if i in (4, 8, 12, 16):
            piece = pl.ds(2 * i - 8, 8)
            copy = pltpu.make_async_copy(done.at[piece], out_ref.at[piece], sems.at[i // 4 - 1])
            copy.start()
            copies.append(copy)
    for copy in copies:
        copy.wait()


def solution(mesh):
    nx, ny = mesh.shape["gx"], mesh.shape["gy"]
    kx, fy, z1, zp, ty, te, tl, zu = operators()
    vmem, hbm = pl.BlockSpec(memory_space=pltpu.VMEM), pl.BlockSpec(memory_space=pltpu.HBM)
    limit = 24 * 1024 * 1024
    block = (32, 32, 128)
    moves = pltpu.SemaphoreType.DMA((len(MOVES),))

    def kept(*ms):
        return [pltpu.with_memory_space_constraint(jnp.asarray(m), pltpu.HBM) for m in ms]

    def local(v):
        v, vo = pl.pallas_call(
            prepare,
            out_shape=[pltpu.VMEM(block, F32), pltpu.VMEM((ENTRIES, ROWS, 128), F32)],
            in_specs=[hbm] * 5, out_specs=[vmem] * 2,
            scratch_shapes=[*(pltpu.VMEM(m.shape, BF16) for m in (kx, fy, z1, zp)), pltpu.VMEM((4, 32, 128), F32), pltpu.SemaphoreType.DMA((8,))],
            compiler_params=pltpu.CompilerParams(vmem_limit_bytes=limit),
        )(*kept(v, kx, fy, z1, zp))
        parts = pl.pallas_call(
            functools.partial(exchange, nx, ny, 8),
            out_shape=[*(pltpu.VMEM(s, F32) for s in ((36, 4, 8, 128), (2, len(PAIRS) - EARLY, 8, 256), (128, 256), (96, 256))),
                       *(pltpu.VMEM(m.shape, BF16) for m in (tl, zu))],
            in_specs=[vmem] * 2 + [hbm] * 5, out_specs=[vmem] * 6,
            scratch_shapes=[pltpu.VMEM((ENTRIES, ROWS, 128), F32), *(pltpu.VMEM(m.shape, BF16) for m in (z1, ty, te)),
                            pltpu.VMEM((2, EARLY, 8, 256), F32), pltpu.VMEM(block, F32),
                            moves, moves, pltpu.SemaphoreType.REGULAR((2,)), pltpu.SemaphoreType.DMA((5,))],
            compiler_params=pltpu.CompilerParams(collective_id=0, has_side_effects=True, vmem_limit_bytes=limit),
        )(v, vo, *kept(z1, ty, te, tl, zu))
        return pl.pallas_call(
            finish,
            out_shape=jax.ShapeDtypeStruct(block, F32),
            in_specs=[vmem] * 6, out_specs=pl.BlockSpec(memory_space=pl.ANY),
            scratch_shapes=[pltpu.VMEM((16, 2, 8, 128), F32), pltpu.VMEM(block, F32), pltpu.SemaphoreType.DMA((4,))],
            compiler_params=pltpu.CompilerParams(vmem_limit_bytes=limit),
        )(*parts)

    spec = P("gx", "gy", None)
    return jax.shard_map(local, mesh=mesh, in_specs=(spec,), out_specs=spec, check_vma=False)
```

time: 34.3 us -> 27.3 us (0.80)
  the two profiles are of different devices: /device:TPU:1 before, /device:TPU:408 now
where the time goes in v2:
time: 27.3 us; the launch traced here: 27.2 us
  Pallas kernels  27.1 us (99%)
    pallas_call x1, Pallas kernels, local(): pl.pallas_call(functools.partial(exchange, nx, ny, 8), out_shape=[*(pltpu...  23.2 us
    pallas_call x1, Pallas kernels, local(): pl.pallas_call(prepare, out_shape=[pltpu.VMEM(block, F32), pltpu.VMEM((EN...  2.75 us
    pallas_call x1, Pallas kernels, local(): pl.pallas_call(finish, out_shape=jax.ShapeDtypeStruct(block, F32), in_spe...  1.17 us

profile of v2, /device:TPU:408, one launch (start us, length us, event | category | flops | bytes accessed | tf_op | source)
XLA Modules:
  0.0 27.2 jit_solution(10269393797863805441)
XLA Ops:
  0.0 2.8 %shard_map.91 = (f32[32,32,128]{2,1,0:T(8,128)S(1)}, f32[32,64,128]{2,1,0:T(8,128)S(1)}) custom-call(f32[32,32,128]{2,1,0:T(8,128)} %v_hbm.1, bf16[2,2,320,128]{3,2,1,0:T(8,128)(2,1)} %constant.16.clone.kx_hbm, bf16[1,64,128]{2,1,0:T(8,128)(2,1)} %constant.17.clone.fy_hbm, bf16[2,256,128]{2,1,0:T(8,128)(2,1)} %constant.18.clone.z1_hbm, ...), custom_call_target="tpu_custom_call" | custom-call | tf_op jit(solution)/shard_map/pallas_call | solution.py:445
  2.8 23.2 %shard_map.92 = (f32[36,4,8,128]{3,2,1,0:T(8,128)S(1)}, f32[2,5,8,256]{3,2,1,0:T(8,128)S(1)}, f32[128,256]{1,0:T(8,128)S(1)}, f32[96,256]{1,0:T(8,128)S(1)}, bf1...) custom-call(f32[32,32,128]{2,1,0:T(8,128)S(1)} %get-tuple-element.13.v_ref, ...), custom_call_target="tpu_custom_call" | custom-call | tf_op jit(solution)/shard_map/pallas_call | solution.py:452
  26.0 1.2 %shard_map.93 = f32[32,32,128]{2,1,0:T(8,128)} custom-call(f32[36,4,8,128]{3,2,1,0:T(8,128)S(1)} %get-tuple-element.15.ys, f32[2,5,8,256]{3,2,1,0:T(8,128)S(1)} %get-tuple-element.16.tl, f32[128,256]{1,0:T(8,128)S(1)} %get-tuple-element.17.e2_ref, f32[96,256]{1,0:T(8,128)S(1)} %get-tuple-element.18.e34_ref, ...), custom_call_target="tpu_custom_call" | custom-call | tf_op jit(solution)/shard_map/pallas_call | solution.py:462

commit v3 on v2

--- a/solution.py
+++ b/solution.py
@@ -29,7 +29,7 @@
 def pieces(dx, dy):
     rows = (Y_AT[dy], 8)
     if dx == 0:
-        return [((0, 18 if abs(dy) == 1 else 2), rows)]
+        return [((0, 18 if abs(dy) == 1 else 10), rows)]
     if abs(dx) == 2:
         return [((X_AT[dx], 1), rows)]
     if dy == 0:
@@ -64,9 +64,12 @@
     return np.concatenate([basis, np.zeros((count - len(basis), basis.shape[1]))])
 
 
-def halves(matrix):
-    high = np.asarray(matrix, np.float32).astype(ml_dtypes.bfloat16)
-    return high, (np.asarray(matrix, np.float32) - high.astype(np.float32)).astype(ml_dtypes.bfloat16)
+def thirds(matrix):
+    out, rest = [], np.asarray(matrix, np.float64)
+    for _ in range(3):
+        out.append(rest.astype(ml_dtypes.bfloat16))
+        rest = rest - out[-1].astype(np.float64)
+    return out
 
 
 def operators():
@@ -80,35 +83,39 @@
     for offset, count in COUNT.items():
         parts = [levels[level][:, (mid + offset) * n:(mid + offset + 1) * n] for level in (4, 3, 2)]
         functional[offset] = row_space(parts, count)
-        combine[offset] = np.concatenate(parts[::-1]) @ functional[offset].T
-    fx = np.concatenate([functional[o][h::2] for h in (0, 1) for o in COUNT])
-    kx = np.stack(halves(np.kron(fx, np.eye(8))))
-    cx = [np.concatenate([combine[o][:, h::2] for o in COUNT], 1) for h in (0, 1)]
+        combine[offset] = np.concatenate(parts[::-1])
+    basis = np.stack(own_basis(np.eye(n)))
+    inverse = np.linalg.pinv(basis)
+    weights = np.concatenate([functional[o] @ inverse for o in COUNT if o])
+    cx = [np.concatenate([(combine[o] @ (functional[o].T if o else inverse))[:, h::2] for o in COUNT], 1) for h in (0, 1)]
     early, late = [np.stack([np.kron(c[:, part], np.eye(8)) for c in cx]) for part in (slice(0, EARLY), slice(EARLY, None))]
-    (high, low), (late_high, late_low) = halves(early), halves(late)
-    early = np.stack([np.concatenate([high, high], 2), np.concatenate([low, np.zeros_like(low)], 2)])
-    late = np.concatenate([late_high, late_high, late_low], 2)
+    high, mid_, low = thirds(early)
+    early = np.stack([np.concatenate(m, 2) for m in ((high, high), (mid_, mid_), (low, high))])
+    high, mid_, low = thirds(late)
+    late = np.concatenate([high, high, high, mid_, mid_, low], 2)
     fy, cy = np.zeros((ROWS, 32)), np.zeros((28, ROWS))
     for offset, count in COUNT.items():
         at = Y_AT[offset]
-        fy[at:at + count], cy[:, at:at + count] = functional[offset], combine[offset]
+        fy[at:at + count], cy[:, at:at + count] = functional[offset], combine[offset] @ functional[offset].T
     ty = np.zeros((32, ROWS))
     ty[0:8], ty[8:16], ty[16:24], ty[24:32:2] = cy[0:16:2], cy[1:16:2], cy[16:24], cy[24:28]
-    fy, ty = [np.concatenate([h, h, l], 1) for h, l in (halves(fy), halves(ty))]
+    high, mid_, low = thirds(fy)
+    fy = np.concatenate([high, high, high, mid_, mid_, low], 1)
+    high, mid_, low = thirds(ty)
+    ty = np.stack([np.concatenate(m, 1) for m in ((high, high, high), (mid_, mid_, low))])
     low, high = lift_1d(np.eye(128))
-    z1 = wide(interleave(low, high).T)
-    zp = np.concatenate(halves(np.kron(np.eye(2), low.T)), 1)
+    z1 = wide(np.concatenate([interleave(low, high).T, low.T, low.T], 1))
     low, zu = np.eye(64), np.zeros((3, 64, 128))
     for level in range(3):
         low, high = lift_1d(low)
         zu[level, :, ::2 << level] = interleave(low, high).T
     zu = np.stack([wide(np.concatenate([m, m])) for m in zu])
-    return [tiles(m) for m in (kx, fy, z1, zp, ty, early, late, zu)]
+    return weights, [tiles(m) for m in (fy, z1, ty, early, late, zu)]
 
 
 def wide(matrix):
-    high, low = halves(matrix)
-    return np.concatenate([np.concatenate([high, high]), np.concatenate([low, np.zeros_like(low)])], 1)
+    high, mid, low = thirds(matrix)
+    return np.concatenate([np.concatenate(m) for m in ((high, high), (mid, mid), (low, high))], 1)
 
 
 def tiles(matrix):
@@ -130,17 +137,22 @@
 
 def split(v):
     high = v.astype(BF16)
-    return high, (v - high.astype(F32)).astype(BF16)
+    rest = v - high.astype(F32)
+    mid = rest.astype(BF16)
+    return high, mid, (rest - mid.astype(F32)).astype(BF16)
 
 
 def stacked(v):
-    high, low = split(v)
-    return jnp.concatenate([high, low, high], 0)
+    high, mid, low = split(v)
+    return jnp.concatenate([high, mid, low, high, mid, high], 0)
 
 
 def wide_dot(v, ref, *at):
-    v = dot(jnp.concatenate(split(v), 1), whole(ref, *at))
-    return v[:, :128] + v[:, 128:]
+    high, mid, low = split(v)
+    m = whole(ref, *at)
+    n = m.shape[1] // 3
+    v = dot(jnp.concatenate([high, mid], 1), m[:, :2 * n])
+    return dot(jnp.concatenate([high, low], 1), m[:, 2 * n:]) + v[:, n:] + v[:, :n]
 
 
 def states(s):
@@ -151,39 +163,49 @@
     return a, b, c, d
 
 
-def prepare(v_hbm, kx_hbm, fy_hbm, z1_hbm, zp_hbm, v_ref, vo_ref, kx_ref, fy_ref, z1_ref, zp_ref, xh, sems):
-    loads = [pltpu.make_async_copy(v_hbm.at[:, pl.ds(8 * t, 8)], v_ref.at[:, pl.ds(8 * t, 8)], sems.at[t]) for t in range(4)]
-    for i, (source, target) in enumerate(((kx_hbm, kx_ref), (zp_hbm, zp_ref), (fy_hbm, fy_ref), (z1_hbm, z1_ref))):
-        loads.append(pltpu.make_async_copy(source, target, sems.at[4 + i]))
-    for i in (4, 0, 1, 2, 3, 5, 6, 7):
-        loads[i].start()
-    loads[4].wait()
-    parts = [[], []]
-    for t in (0, 2):
+def own_basis(v):
+    out, odd, even, odd3 = [], 0.0, 0.0, 0.0
+    for i in range(17):
+        if i < 16:
+            after = v[2 * i + 2] if i < 15 else 0.0
+            odd_now = v[2 * i + 1] + LIFT_A * (v[2 * i] + after)
+            even_now = v[2 * i] + LIFT_B * (odd + odd_now)
+        else:
+            odd_now, even_now = None, LIFT_B * odd
+        if i > 0:
+            odd3_now = odd + LIFT_C * (even + even_now)
+            out.append(even + LIFT_D * (odd3 + odd3_now))
+            odd3 = odd3_now
+        odd, even = odd_now, even_now
+    return [*out, *states(lambda i: v[i])]
+
+
+def prepare(weights, z1_ref, fy_ref, v_ref, vo_ref, zt, xh, loads):
+    half = lax.broadcasted_iota(jnp.int32, (8, 128), 1) < 64
+    columns = [[] for _ in PAIRS]
+    loads["z1"].wait()
+    for t in range(4):
         loads[t].wait()
-        loads[t + 1].wait()
-        high, low = split(jnp.concatenate([v_ref[:, 8 * u:8 * u + 8, :].reshape(256, 128) for u in (t, t + 1)], 1))
-        x = dot(whole(kx_ref, 0), high) + dot(whole(kx_ref, 0), low) + dot(whole(kx_ref, 1), high)
-        for u in (0, 1):
-            for h in (0, 1):
-                parts[h].append(x[160 * h:160 * h + 160, 128 * u:128 * u + 128])
-    loads[5].wait()
-    high, low = split(jnp.concatenate([jnp.concatenate(part, 0) for part in parts], 1))
-    packed = dot(high, whole(zp_ref))
-    packed = packed[:, :128] + packed[:, 128:] + dot(low, zp_ref[0])
-    loads[6].wait()
+        v = wide_dot(v_ref[:, 8 * t:8 * t + 8, :].reshape(256, 128), z1_ref)
+        zt[:, 8 * t:8 * t + 8, :] = v[:, :128].reshape(32, 8, 128)
+        values = own_basis([v[8 * x:8 * x + 8, 128:] for x in range(32)])
+        for row in weights:
+            terms = [w * value for w, value in zip(row, values[:20]) if abs(w) > 1e-14]
+            while len(terms) > 1:
+                terms = [sum(terms[k:k + 2][1:], terms[k]) for k in range(0, len(terms), 2)]
+            values.append(terms[0] if terms else jnp.zeros((8, 128), F32))
+        for i, column in enumerate(columns):
+            column.append(jnp.where(half, values[2 * i], values[2 * i + 1]))
+    loads["fy"].wait()
     for i in range(0, len(PAIRS), 2):
-        columns = [stacked(jnp.concatenate([packed[160 * t + 8 * j:160 * t + 8 * j + 8] for t in range(4)], 0)) for j in (i, i + 1)]
-        rows = dot(whole(fy_ref, columns=96), jnp.concatenate(columns, 1))
+        two = [stacked(jnp.concatenate(columns[j], 0)) for j in (i, i + 1)]
+        rows = dot(whole(fy_ref, columns=192), jnp.concatenate(two, 1))
         vo_ref[PAIRS[i]] = rows[:, :128]
         vo_ref[PAIRS[i + 1]] = rows[:, 128:]
-    loads[7].wait()
-    planes = [*states(lambda x: v_ref[x]), *states(lambda y: v_ref[:, y, :])]
-    planes = wide_dot(jnp.concatenate(planes, 0), z1_ref)
-    for q in range(4):
-        plane, rows = planes[32 * q:32 * q + 32], planes[128 + 32 * q:160 + 32 * q]
+    for q, plane in enumerate(states(lambda x: zt[x])):
         xh[q] = plane
         vo_ref[X_STATES[-1 if q < 2 else 1] + q % 2, 0:32, :] = plane
+    for q, rows in enumerate(states(lambda y: zt[:, y, :])):
         at = Y_AT[-1 if q < 2 else 1]
         for t in range(4):
             vo_ref[Y_STATES + 4 * (q % 2) + t, at:at + 8, :] = rows[8 * t:8 * t + 8]
@@ -219,8 +241,8 @@
     return f0 * (1 / LIFT_K), q0 * LIFT_K, f1 * (1 / LIFT_K), q1 * LIFT_K
 
 
-def exchange(nx, ny, nz, v_ref, vo_ref, z1_hbm, ty_hbm, te_hbm, tl_hbm, zu_hbm, ys_ref, tl_out, e2_ref, e34_ref, tl_ref, zu_ref,
-             vi_ref, z1_ref, ty_ref, te_ref, te_in, zt, send, recv, hello, sems):
+def exchange(nx, ny, nz, weights, v_hbm, fy_hbm, z1_hbm, ty_hbm, te_hbm, tl_hbm, zu_hbm, ys_ref, tl_out, e2_ref, e34_ref, tl_ref, zu_ref,
+             v_ref, vo_ref, vi_ref, fy_ref, z1_ref, ty_ref, te_ref, te_in, zt, xh, send, recv, hello, sems):
     x, y = lax.axis_index("gx"), lax.axis_index("gy")
     z = lax.rem(x, nz)
 
@@ -250,29 +272,36 @@
 
     greet(-2)
     pl.when(z != nz - 1)(lambda: greet(-1))
+    loads = [pltpu.make_async_copy(v_hbm.at[:, pl.ds(8 * t, 8)], v_ref.at[:, pl.ds(8 * t, 8)], sems.at[t]) for t in range(4)]
+    loads += [pltpu.make_async_copy(a, b, sems.at[4 + i]) for i, (a, b) in enumerate(
+        ((z1_hbm, z1_ref), (fy_hbm, fy_ref), (ty_hbm, ty_ref), (te_hbm, te_ref), (tl_hbm, tl_ref), (zu_hbm, zu_ref)))]
+    for i in (0, 4, 1, 2, 3, 5, 6, 7, 8, 9):
+        loads[i].start()
     pl.when(z < nz - 2)(lambda: greet(0))
     pl.when(z < nz - 3)(lambda: greet(1))
     pl.when(z < nz - 4)(lambda: greet(2))
-    loads = [pltpu.make_async_copy(a, b, sems.at[i]) for i, (a, b) in enumerate(
-        ((z1_hbm, z1_ref), (ty_hbm, ty_ref), (te_hbm, te_ref), (tl_hbm, tl_ref), (zu_hbm, zu_ref)))]
-    for load in loads:
-        load.start()
     for e in PAIRS:
         if e in (X_AT[2], X_AT[-2]):
             vi_ref[e, 8:24, :] = jnp.zeros((16, 128), F32)
-        elif e not in (0, 1, X_AT[1], X_AT[1] + 1, X_AT[-1], X_AT[-1] + 1):
+        elif e >= X_AT[1] and e not in (X_AT[1], X_AT[1] + 1, X_AT[-1], X_AT[-1] + 1):
             vi_ref[e, 48:64, :] = jnp.zeros((16, 128), F32)
+    prepare(weights, z1_ref, fy_ref, v_ref, vo_ref, zt, xh, {**dict(enumerate(loads[:4])), "z1": loads[4], "fy": loads[5]})
     greeted = jnp.where(z == 0, 14, jnp.where(z == 1, 19, jnp.where(z < nz - 2, 24, jnp.where(z == nz - 2, 5, 10))))
     pl.semaphore_wait(barrier, greeted)
+
+    def say_hello(dx, dys):
+        for dy in dys:
+            pl.semaphore_signal(hello.at[dx - 1], inc=1, device_id=device(dx, dy), device_id_type=MESH)
+
+    @pl.when(z == nz - 3)
+    def _():
+        say_hello(1, (0,))
+        say_hello(2, (0,))
+
     pl.when(z != nz - 2)(lambda: start(-1))
     start(-2)
-
-    def say_hello(dx):
-        for dy in range(-2, 3):
-            pl.semaphore_signal(hello.at[dx - 1], inc=1, device_id=device(dx, dy), device_id_type=MESH)
-
-    pl.when(z == nz - 1)(lambda: say_hello(1))
-    pl.when(z >= nz - 2)(lambda: say_hello(2))
+    pl.when(z == nz - 1)(lambda: say_hello(1, range(-2, 3)))
+    pl.when(z >= nz - 2)(lambda: say_hello(2, range(-2, 3)))
 
     @pl.when(z < nz - 2)
     def _():
@@ -280,26 +309,20 @@
         pl.when(z > 0)(lambda: start(1))
         pl.when(z > 1)(lambda: start(2))
 
-    loads[0].wait()
-    for t in range(4):
-        zt[:, 8 * t:8 * t + 8, :] = wide_dot(v_ref[:, 8 * t:8 * t + 8, :].reshape(256, 128), z1_ref).reshape(32, 8, 128)
-
     @pl.when(z == nz - 2)
     def _():
-        arrive(-1)
+        pl.semaphore_wait(hello.at[0], 1)
         start(-1)
+
+    @pl.when(z == nz - 1)
+    def _():
+        pl.semaphore_wait(hello.at[1], 1)
+
+    @pl.when(z >= nz - 2)
+    def _():
         start(1)
         start(0)
-        arrive(-2)
         start(2)
-
-    @pl.when(z == nz - 1)
-    def _():
-        arrive(-2)
-        start(0)
-        start(2)
-        arrive(-1)
-        start(1)
 
     sub = lax.broadcasted_iota(jnp.int32, (8, 128), 0)
     first, last = sub == 0, sub == 7
@@ -324,14 +347,16 @@
             e = PAIRS[i]
             v = vi_ref[e]
             own = vo_ref[e, 0:32, :] if i < COUNT[0] // 2 else jnp.concatenate([v[0:24], jnp.zeros((8, 128), F32)], 0)
-            done.append(stacked(jnp.concatenate([own, v[32:]], 0)))
+            done.append(jnp.concatenate([own, v[32:]], 0))
         for i in range(0, count, 2):
-            r = dot(whole(ty_ref, columns=192), jnp.concatenate(done[i:i + 2], 1))
+            high, mid, low = split(jnp.concatenate(done[i:i + 2], 1))
+            r = (dot(whole(ty_ref, 1, columns=192), jnp.concatenate([high, mid, high], 0))
+                 + dot(whole(ty_ref, 0, columns=192), jnp.concatenate([high, mid, low], 0)))
             for j in range(min(2, count - i)):
                 for t in range(4):
                     out_ref[t // 2, first_pair % EARLY + i + j, :, 128 * (t % 2):128 * (t % 2) + 128] = r[8 * t:8 * t + 8, 128 * j:128 * j + 128]
 
-    loads[1].wait()
+    loads[6].wait()
     arrive(0)
     for x in range(2, 34):
         plane(x)
@@ -341,12 +366,12 @@
     plane(35)
     arrive(2)
     upper(10, 5, te_in)
-    loads[2].wait()
+    loads[7].wait()
     for u, (ref, at, rows) in enumerate(((e2_ref, 0, 128), (e34_ref, 128, 96))):
-        high, low = split(te_in[u].reshape(8 * EARLY, 256))
-        v = jnp.concatenate([high, low], 0)
-        v = [dot(whole(te_ref, 0, h, rows=slice(at, at + rows), columns=240), v)
-             + dot(whole(te_ref, 1, h, rows=slice(at, at + rows), columns=120), high) for h in (0, 1)]
+        high, mid, low = split(te_in[u].reshape(8 * EARLY, 256))
+        high_mid, high_low = [jnp.concatenate([high, w], 0) for w in (mid, low)]
+        m = [[whole(te_ref, k, h, rows=slice(at, at + rows), columns=240) for k in range(3)] for h in (0, 1)]
+        v = [dot(m[h][2], high_low) + dot(m[h][1], high_mid) + dot(m[h][0], high_mid) for h in (0, 1)]
         ref[...] = jnp.where(lax.broadcasted_iota(jnp.int32, (rows, 256), 1) % 128 < 64, v[0], v[1])
 
     @pl.when(z == 0)
@@ -359,16 +384,13 @@
         pl.semaphore_wait(hello.at[1], 5)
         start(2)
 
-    @pl.when(z < nz - 2)
-    def _():
-        arrive(-1)
-        arrive(-2)
-
+    arrive(-1)
+    arrive(-2)
     plane(0)
     plane(1)
     upper(15, 5, tl_out)
-    loads[3].wait()
-    loads[4].wait()
+    loads[8].wait()
+    loads[9].wait()
     for dx in OFFSETS:
         for copy in copies[dx]:
             copy.wait_send()
@@ -380,7 +402,7 @@
 
     def upper(u, at, rows, early):
         v = stacked(tl[u].reshape(8 * (len(PAIRS) - EARLY), 256))
-        v = [dot(whole(tl_ref, h, rows=slice(at, at + rows), columns=120), v) for h in (0, 1)]
+        v = [dot(whole(tl_ref, h, rows=slice(at, at + rows), columns=240), v) for h in (0, 1)]
         return early + jnp.where(lax.broadcasted_iota(jnp.int32, (rows, 256), 1) % 128 < 64, v[0], v[1])
 
     v = upper(0, 0, 128, e2_ref[...])
@@ -432,7 +454,7 @@
 
 def solution(mesh):
     nx, ny = mesh.shape["gx"], mesh.shape["gy"]
-    kx, fy, z1, zp, ty, te, tl, zu = operators()
+    weights, (fy, z1, ty, te, tl, zu) = operators()
     vmem, hbm = pl.BlockSpec(memory_space=pltpu.VMEM), pl.BlockSpec(memory_space=pltpu.HBM)
     limit = 24 * 1024 * 1024
     block = (32, 32, 128)
@@ -442,23 +464,16 @@
         return [pltpu.with_memory_space_constraint(jnp.asarray(m), pltpu.HBM) for m in ms]
 
     def local(v):
-        v, vo = pl.pallas_call(
-            prepare,
-            out_shape=[pltpu.VMEM(block, F32), pltpu.VMEM((ENTRIES, ROWS, 128), F32)],
-            in_specs=[hbm] * 5, out_specs=[vmem] * 2,
-            scratch_shapes=[*(pltpu.VMEM(m.shape, BF16) for m in (kx, fy, z1, zp)), pltpu.VMEM((4, 32, 128), F32), pltpu.SemaphoreType.DMA((8,))],
-            compiler_params=pltpu.CompilerParams(vmem_limit_bytes=limit),
-        )(*kept(v, kx, fy, z1, zp))
         parts = pl.pallas_call(
-            functools.partial(exchange, nx, ny, 8),
+            functools.partial(exchange, nx, ny, 8, weights.tolist()),
             out_shape=[*(pltpu.VMEM(s, F32) for s in ((36, 4, 8, 128), (2, len(PAIRS) - EARLY, 8, 256), (128, 256), (96, 256))),
                        *(pltpu.VMEM(m.shape, BF16) for m in (tl, zu))],
-            in_specs=[vmem] * 2 + [hbm] * 5, out_specs=[vmem] * 6,
-            scratch_shapes=[pltpu.VMEM((ENTRIES, ROWS, 128), F32), *(pltpu.VMEM(m.shape, BF16) for m in (z1, ty, te)),
-                            pltpu.VMEM((2, EARLY, 8, 256), F32), pltpu.VMEM(block, F32),
-                            moves, moves, pltpu.SemaphoreType.REGULAR((2,)), pltpu.SemaphoreType.DMA((5,))],
+            in_specs=[hbm] * 7, out_specs=[vmem] * 6,
+            scratch_shapes=[pltpu.VMEM(block, F32), *([pltpu.VMEM((ENTRIES, ROWS, 128), F32)] * 2), *(pltpu.VMEM(m.shape, BF16) for m in (fy, z1, ty, te)),
+                            pltpu.VMEM((2, EARLY, 8, 256), F32), pltpu.VMEM(block, F32), pltpu.VMEM((4, 32, 128), F32),
+                            moves, moves, pltpu.SemaphoreType.REGULAR((2,)), pltpu.SemaphoreType.DMA((10,))],
             compiler_params=pltpu.CompilerParams(collective_id=0, has_side_effects=True, vmem_limit_bytes=limit),
-        )(v, vo, *kept(z1, ty, te, tl, zu))
+        )(*kept(v, fy, z1, ty, te, tl, zu))
         return pl.pallas_call(
             finish,
             out_shape=jax.ShapeDtypeStruct(block, F32),

time: 27.3 us -> 24.4 us (0.89)
  the two profiles are of different devices: /device:TPU:408 before, /device:TPU:1 now
where the time goes in v3:
time: 24.4 us; the launch traced here: 24.2 us
  Pallas kernels  24.2 us (99%)
    pallas_call x1, Pallas kernels, local(): pl.pallas_call(functools.partial(exchange, nx, ny, 8, weights.tolist()),...  22.9 us
    pallas_call x1, Pallas kernels, local(): pl.pallas_call(finish, out_shape=jax.ShapeDtypeStruct(block, F32), in_spe...  1.36 us

profile of v3, /device:TPU:1, one launch (start us, length us, event | category | flops | bytes accessed | tf_op | source)
XLA Modules:
  0.0 24.2 jit_solution(17509973771819978403)
XLA Ops:
  0.0 22.9 %shard_map.73 = (f32[36,4,8,128]{3,2,1,0:T(8,128)S(1)}, f32[2,5,8,256]{3,2,1,0:T(8,128)S(1)}, f32[128,256]{1,0:T(8,128)S(1)}, f32[96,256]{1,0:T(8,128)S(1)}, bf1...) custom-call(f32[32,32,128]{2,1,0:T(8,128)} %v_hbm.1, bf16[2,64,128]{2,1,0:T(8,128)(2,1)} %constant.12.clone.fy_hbm, ...), custom_call_target="tpu_custom_call" | custom-call | tf_op jit(solution)/shard_map/pallas_call | solution.py:467
  22.9 1.4 %shard_map.74 = f32[32,32,128]{2,1,0:T(8,128)} custom-call(f32[36,4,8,128]{3,2,1,0:T(8,128)S(1)} %get-tuple-element.11.ys, f32[2,5,8,256]{3,2,1,0:T(8,128)S(1)} %get-tuple-element.12.tl, f32[128,256]{1,0:T(8,128)S(1)} %get-tuple-element.13.e2_ref, f32[96,256]{1,0:T(8,128)S(1)} %get-tuple-element.14.e34_ref, ...), custom_call_target="tpu_custom_call" | custom-call | tf_op jit(solution)/shard_map/pallas_call | solution.py:477

commit v4 on v3

--- a/solution.py
+++ b/solution.py
@@ -104,13 +104,14 @@
     high, mid_, low = thirds(ty)
     ty = np.stack([np.concatenate(m, 1) for m in ((high, high, high), (mid_, mid_, low))])
     low, high = lift_1d(np.eye(128))
-    z1 = wide(np.concatenate([interleave(low, high).T, low.T, low.T], 1))
+    z1 = wide(interleave(low, high).T)
+    zp = np.concatenate(thirds(np.kron(np.eye(2), low.T)), 1)
     low, zu = np.eye(64), np.zeros((3, 64, 128))
     for level in range(3):
         low, high = lift_1d(low)
         zu[level, :, ::2 << level] = interleave(low, high).T
     zu = np.stack([wide(np.concatenate([m, m])) for m in zu])
-    return weights, [tiles(m) for m in (fy, z1, ty, early, late, zu)]
+    return weights, [tiles(m) for m in (zp, fy, z1, ty, early, late, zu)]
 
 
 def wide(matrix):
@@ -180,42 +181,50 @@
     return [*out, *states(lambda i: v[i])]
 
 
-def prepare(weights, z1_ref, fy_ref, v_ref, vo_ref, zt, xh, loads):
-    half = lax.broadcasted_iota(jnp.int32, (8, 128), 1) < 64
-    columns = [[] for _ in PAIRS]
-    loads["z1"].wait()
-    for t in range(4):
-        loads[t].wait()
-        v = wide_dot(v_ref[:, 8 * t:8 * t + 8, :].reshape(256, 128), z1_ref)
-        zt[:, 8 * t:8 * t + 8, :] = v[:, :128].reshape(32, 8, 128)
-        values = own_basis([v[8 * x:8 * x + 8, 128:] for x in range(32)])
-        for row in weights:
-            terms = [w * value for w, value in zip(row, values[:20]) if abs(w) > 1e-14]
-            while len(terms) > 1:
-                terms = [sum(terms[k:k + 2][1:], terms[k]) for k in range(0, len(terms), 2)]
-            values.append(terms[0] if terms else jnp.zeros((8, 128), F32))
-        for i, column in enumerate(columns):
-            column.append(jnp.where(half, values[2 * i], values[2 * i + 1]))
-    loads["fy"].wait()
-    for i in range(0, len(PAIRS), 2):
-        two = [stacked(jnp.concatenate(columns[j], 0)) for j in (i, i + 1)]
-        rows = dot(whole(fy_ref, columns=192), jnp.concatenate(two, 1))
-        vo_ref[PAIRS[i]] = rows[:, :128]
-        vo_ref[PAIRS[i + 1]] = rows[:, 128:]
-    for q, plane in enumerate(states(lambda x: zt[x])):
+def prepare_states(v_ref, vo_ref, xh):
+    for q, plane in enumerate(states(lambda x: v_ref[x])):
         xh[q] = plane
         vo_ref[X_STATES[-1 if q < 2 else 1] + q % 2, 0:32, :] = plane
+    for p, rows in enumerate(states(lambda y: xh[:, y, :])):
+        at = Y_AT[-1 if p < 2 else 1] + 2 * (p % 2)
+        vo_ref[X_STATES[-1], at:at + 2, :] = rows[0:2]
+        vo_ref[X_STATES[1], at:at + 2, :] = rows[2:4]
+    for e in X_STATES.values():
+        for dy in (-1, 1):
+            vo_ref[e, Y_AT[dy] + 4:Y_AT[dy] + 8, :] = jnp.zeros((4, 128), F32)
+
+
+def prepare_pairs(first, count, weights, zp_ref, fy_ref, vo_ref, basis):
+    sides = []
+    for h in (0, 1):
+        rows = []
+        for i in range(first, first + count):
+            f = 2 * i + h
+            for t in range(4):
+                if f < 20:
+                    rows.append(basis[f, t])
+                    continue
+                terms = [w * basis[k, t] for k, w in enumerate(weights[f - 20]) if abs(w) > 1e-14]
+                while len(terms) > 1:
+                    terms = [sum(terms[k:k + 2][1:], terms[k]) for k in range(0, len(terms), 2)]
+                rows.append(terms[0] if terms else jnp.zeros((8, 128), F32))
+        sides.append(jnp.concatenate(rows, 0))
+    high, mid, low = split(jnp.concatenate(sides, 1))
+    m = whole(zp_ref)
+    packed = dot(high, m[:, :256]) + dot(mid, m[:, :256])
+    packed = dot(low, m[:, :128]) + dot(high, m[:, 256:]) + packed[:, 128:] + packed[:, :128]
+    columns = [stacked(packed[32 * i:32 * i + 32]) for i in range(count)]
+    for i in range(0, count, 2):
+        rows = dot(whole(fy_ref, columns=192), jnp.concatenate(columns[i:i + 2], 1))
+        for j in range(min(2, count - i)):
+            vo_ref[PAIRS[first + i + j]] = rows[:, 128 * j:128 * j + 128]
+
+
+def prepare_rows(vo_ref, zt):
     for q, rows in enumerate(states(lambda y: zt[:, y, :])):
         at = Y_AT[-1 if q < 2 else 1]
         for t in range(4):
             vo_ref[Y_STATES + 4 * (q % 2) + t, at:at + 8, :] = rows[8 * t:8 * t + 8]
-    for q in range(4):
-        for p, row in enumerate(states(lambda y: xh[q, y:y + 1, :])):
-            at = Y_AT[-1 if p < 2 else 1] + 2 * (q % 2) + p % 2
-            vo_ref[X_STATES[-1 if q < 2 else 1], at:at + 1, :] = row
-    for e in X_STATES.values():
-        for dy in (-1, 1):
-            vo_ref[e, Y_AT[dy] + 4:Y_AT[dy] + 8, :] = jnp.zeros((4, 128), F32)
 
 
 def split_y(p, halo, first, last):
@@ -241,8 +250,9 @@
     return f0 * (1 / LIFT_K), q0 * LIFT_K, f1 * (1 / LIFT_K), q1 * LIFT_K
 
 
-def exchange(nx, ny, nz, weights, v_hbm, fy_hbm, z1_hbm, ty_hbm, te_hbm, tl_hbm, zu_hbm, ys_ref, tl_out, e2_ref, e34_ref, tl_ref, zu_ref,
-             v_ref, vo_ref, vi_ref, fy_ref, z1_ref, ty_ref, te_ref, te_in, zt, xh, send, recv, hello, sems):
+def exchange(nx, ny, nz, weights, v_hbm, zp_hbm, fy_hbm, z1_hbm, ty_hbm, te_hbm, tl_hbm, zu_hbm,
+             ys_ref, done, tl_out, e2_ref, e34_ref, tl_ref, zu_ref,
+             v_ref, vo_ref, vi_ref, zp_ref, fy_ref, z1_ref, ty_ref, te_ref, te_in, zt, basis, xh, xz, send, recv, hello, sems):
     x, y = lax.axis_index("gx"), lax.axis_index("gy")
     z = lax.rem(x, nz)
 
@@ -256,8 +266,8 @@
             src_ref=vo_ref.at[at], dst_ref=vi_ref.at[at], send_sem=send.at[i], recv_sem=recv.at[i],
             device_id=device(-dx, -dy), device_id_type=MESH))
 
-    def start(dx):
-        for copy in copies[dx]:
+    def start(dx, part=slice(None)):
+        for copy in copies[dx][part]:
             copy.start()
 
     def arrive(dx):
@@ -270,12 +280,16 @@
         for o in GROUP[dx]:
             pl.semaphore_signal(barrier, inc=1, device_id=device(*o), device_id_type=MESH)
 
+    def say_hello(dx, dys):
+        for dy in dys:
+            pl.semaphore_signal(hello.at[dx - 1], inc=1, device_id=device(dx, dy), device_id_type=MESH)
+
     greet(-2)
     pl.when(z != nz - 1)(lambda: greet(-1))
-    loads = [pltpu.make_async_copy(v_hbm.at[:, pl.ds(8 * t, 8)], v_ref.at[:, pl.ds(8 * t, 8)], sems.at[t]) for t in range(4)]
+    loads = [pltpu.make_async_copy(v_hbm.at[pl.ds(8 * t, 8)], v_ref.at[pl.ds(8 * t, 8)], sems.at[t]) for t in range(4)]
     loads += [pltpu.make_async_copy(a, b, sems.at[4 + i]) for i, (a, b) in enumerate(
-        ((z1_hbm, z1_ref), (fy_hbm, fy_ref), (ty_hbm, ty_ref), (te_hbm, te_ref), (tl_hbm, tl_ref), (zu_hbm, zu_ref)))]
-    for i in (0, 4, 1, 2, 3, 5, 6, 7, 8, 9):
+        ((zp_hbm, zp_ref), (fy_hbm, fy_ref), (z1_hbm, z1_ref), (ty_hbm, ty_ref), (te_hbm, te_ref), (tl_hbm, tl_ref), (zu_hbm, zu_ref)))]
+    for i in (3, 0, 1, 2, 4, 5):
         loads[i].start()
     pl.when(z < nz - 2)(lambda: greet(0))
     pl.when(z < nz - 3)(lambda: greet(1))
@@ -285,29 +299,51 @@
             vi_ref[e, 8:24, :] = jnp.zeros((16, 128), F32)
         elif e >= X_AT[1] and e not in (X_AT[1], X_AT[1] + 1, X_AT[-1], X_AT[-1] + 1):
             vi_ref[e, 48:64, :] = jnp.zeros((16, 128), F32)
-    prepare(weights, z1_ref, fy_ref, v_ref, vo_ref, zt, xh, {**dict(enumerate(loads[:4])), "z1": loads[4], "fy": loads[5]})
-    greeted = jnp.where(z == 0, 14, jnp.where(z == 1, 19, jnp.where(z < nz - 2, 24, jnp.where(z == nz - 2, 5, 10))))
-    pl.semaphore_wait(barrier, greeted)
-
-    def say_hello(dx, dys):
-        for dy in dys:
-            pl.semaphore_signal(hello.at[dx - 1], inc=1, device_id=device(dx, dy), device_id_type=MESH)
-
-    @pl.when(z == nz - 3)
-    def _():
-        say_hello(1, (0,))
-        say_hello(2, (0,))
-
-    pl.when(z != nz - 2)(lambda: start(-1))
-    start(-2)
-    pl.when(z == nz - 1)(lambda: say_hello(1, range(-2, 3)))
-    pl.when(z >= nz - 2)(lambda: say_hello(2, range(-2, 3)))
+
+    @pl.when(z >= nz - 2)
+    def _():
+        pl.semaphore_wait(barrier, jnp.where(z == nz - 2, 5, 10))
+        say_hello(2, range(-2, 3))
+        pl.when(z == nz - 1)(lambda: say_hello(1, range(-2, 3)))
+
+    for load in loads[:4]:
+        load.wait()
+    prepare_states(v_ref, vo_ref, xh)
+    pl.when(z == nz - 1)(lambda: start(-1, slice(0, 1)))
+    for t in range(4):
+        for i, value in enumerate(own_basis([v_ref[x, 8 * t:8 * t + 8, :] for x in range(32)])):
+            basis[i, t] = value
+    loads[4].wait()
+    loads[5].wait()
+    prepare_pairs(EARLY, len(PAIRS) - EARLY, weights, zp_ref, fy_ref, vo_ref, basis)
+
+    @pl.when(z >= nz - 2)
+    def _():
+        start(-2)
+        pl.when(z == nz - 1)(lambda: start(-1, slice(1, None)))
+
+    for load in loads[6:]:
+        load.start()
+    prepare_pairs(0, EARLY, weights, zp_ref, fy_ref, vo_ref, basis)
+    loads[6].wait()
+    for t in range(4):
+        zt[:, 8 * t:8 * t + 8, :] = wide_dot(v_ref[:, 8 * t:8 * t + 8, :].reshape(256, 128), z1_ref).reshape(32, 8, 128)
+    prepare_rows(vo_ref, zt)
 
     @pl.when(z < nz - 2)
     def _():
+        pl.semaphore_wait(barrier, jnp.where(z == 0, 14, jnp.where(z == 1, 19, 24)))
+
+        @pl.when(z == nz - 3)
+        def _():
+            say_hello(1, (0,))
+            say_hello(2, (0,))
+
+        start(-2)
+        pl.when(z > 1)(lambda: start(2))
+        start(-1)
+        pl.when(z > 0)(lambda: start(1))
         start(0)
-        pl.when(z > 0)(lambda: start(1))
-        pl.when(z > 1)(lambda: start(2))
 
     @pl.when(z == nz - 2)
     def _():
@@ -320,26 +356,30 @@
 
     @pl.when(z >= nz - 2)
     def _():
+        start(2)
         start(1)
         start(0)
-        start(2)
 
     sub = lax.broadcasted_iota(jnp.int32, (8, 128), 0)
     first, last = sub == 0, sub == 7
 
+    def row(ref, e, r):
+        return jnp.broadcast_to(ref[e, pl.ds(r, 1), :], (8, 128))
+
     def plane(x):
-        if 2 <= x < 34:
-            x = x - 2
-            p = [zt[x, pl.ds(r, 8, 4), :] for r in range(4)]
-            at = [(Y_STATES + 4 * (k % 2) + x // 8, Y_AT[-1 if k < 2 else 1] + x % 8) for k in range(4)]
-            x = x + 2
-        else:
-            dx, q = (-1, x) if x < 2 else (1, x - 34)
-            p = [vi_ref[X_STATES[dx] + q, pl.ds(r, 8, 4), :] for r in range(4)]
-            at = [(X_STATES[dx], Y_AT[-1 if k < 2 else 1] + 2 * q + k % 2) for k in range(4)]
-        halo = [jnp.broadcast_to(vi_ref[e, pl.ds(r, 1), :], (8, 128)) for e, r in at]
+        p = [zt[x, pl.ds(r, 8, 4), :] for r in range(4)]
+        halo = [row(vi_ref, Y_STATES + 4 * (k % 2) + x // 8, Y_AT[-1 if k < 2 else 1] + x % 8) for k in range(4)]
         for r, v in enumerate(split_y(p, halo, first, last)):
-            ys_ref[x, r] = v
+            ys_ref[x + 2, r] = v
+
+    def state_planes(dx):
+        e, side = X_STATES[dx], (dx + 1) // 2
+        xz[side] = wide_dot(jnp.concatenate([vi_ref[e, 0:32, :], vi_ref[e + 1, 0:32, :], vi_ref[e, 32:48, :]], 0), z1_ref)
+        for q in (0, 1):
+            p = [xz[side, pl.ds(32 * q + r, 8, 4), :] for r in range(4)]
+            halo = [row(xz, side, 64 + 8 * (k // 2) + 2 * (k % 2) + q) for k in range(4)]
+            for r, v in enumerate(split_y(p, halo, first, last)):
+                ys_ref[34 * side + q, r] = v
 
     def upper(first_pair, count, out_ref):
         done = []
@@ -356,17 +396,27 @@
                 for t in range(4):
                     out_ref[t // 2, first_pair % EARLY + i + j, :, 128 * (t % 2):128 * (t % 2) + 128] = r[8 * t:8 * t + 8, 128 * j:128 * j + 128]
 
-    loads[6].wait()
+    loads[7].wait()
     arrive(0)
-    for x in range(2, 34):
+    for x in range(32):
         plane(x)
     upper(0, 10, te_in)
+
+    @pl.when(z < 2)
+    def _():
+        pl.semaphore_wait(hello.at[1], 5)
+        start(2)
+
+    @pl.when(z == 0)
+    def _():
+        pl.semaphore_wait(hello.at[0], 5)
+        start(1)
+
     arrive(1)
-    plane(34)
-    plane(35)
+    state_planes(1)
     arrive(2)
     upper(10, 5, te_in)
-    loads[7].wait()
+    loads[8].wait()
     for u, (ref, at, rows) in enumerate(((e2_ref, 0, 128), (e34_ref, 128, 96))):
         high, mid, low = split(te_in[u].reshape(8 * EARLY, 256))
         high_mid, high_low = [jnp.concatenate([high, w], 0) for w in (mid, low)]
@@ -374,59 +424,23 @@
         v = [dot(m[h][2], high_low) + dot(m[h][1], high_mid) + dot(m[h][0], high_mid) for h in (0, 1)]
         ref[...] = jnp.where(lax.broadcasted_iota(jnp.int32, (rows, 256), 1) % 128 < 64, v[0], v[1])
 
-    @pl.when(z == 0)
-    def _():
-        pl.semaphore_wait(hello.at[0], 5)
-        start(1)
-
-    @pl.when(z < 2)
-    def _():
-        pl.semaphore_wait(hello.at[1], 5)
-        start(2)
-
+    lift_x(ys_ref, done)
+    loads[9].wait()
+    loads[10].wait()
     arrive(-1)
     arrive(-2)
-    plane(0)
-    plane(1)
+    state_planes(-1)
     upper(15, 5, tl_out)
-    loads[8].wait()
-    loads[9].wait()
     for dx in OFFSETS:
         for copy in copies[dx]:
             copy.wait_send()
 
 
-def finish(ys, tl, e2_ref, e34_ref, tl_ref, zu_ref, out_ref, up, done, sems):
-    sub = lax.broadcasted_iota(jnp.int32, (8, 128), 0)
-    lane = lax.broadcasted_iota(jnp.int32, (8, 128), 1)
-
-    def upper(u, at, rows, early):
-        v = stacked(tl[u].reshape(8 * (len(PAIRS) - EARLY), 256))
-        v = [dot(whole(tl_ref, h, rows=slice(at, at + rows), columns=240), v) for h in (0, 1)]
-        return early + jnp.where(lax.broadcasted_iota(jnp.int32, (rows, 256), 1) % 128 < 64, v[0], v[1])
-
-    v = upper(0, 0, 128, e2_ref[...])
-    l2 = wide_dot(jnp.concatenate([v[:, :128], v[:, 128:]], 0), zu_ref, 0).reshape(2, 16, 8, 128)
-    v = upper(1, 128, 96, e34_ref[...])
-    l3 = wide_dot(v[:64, :128], zu_ref, 1).reshape(8, 8, 128)
-    l4 = wide_dot(v[64:, 128:], zu_ref, 2).reshape(4, 8, 128)
-    for i in range(16):
-        for t in (0, 1):
-            v = l2[t][i]
-            if i % 2 == 0 and t == 0:
-                w = l3[i // 2]
-                if i % 4 == 0:
-                    w = jnp.where((lane % 8 == 0) & (sub % 2 == 0), l4[i // 4], w)
-                v = jnp.where(lane % 4 == 0, w, v)
-            up[i, t] = v
-
-    odd_lane = lane % 2 == 1
+def lift_x(ys, done):
     state = {}
-    copies = []
     for r in range(4):
-        before = ys[0, r] + LIFT_A * ys[2, r]
-        state[r] = (before, ys[1, r] + LIFT_B * before, None)
-    for i in range(17):
+        state[r] = (ys[3, r] + LIFT_A * (ys[2, r] + ys[4, r]), None, None)
+    for i in range(1, 17):
         for r in range(4):
             o, e, q = state[r]
             if i < 16:
@@ -435,29 +449,72 @@
                 e_now = p + LIFT_B * (o + o_now)
             else:
                 o_now, e_now = None, ys[35, r] + LIFT_B * o
-            q_now = o + LIFT_C * (e + e_now)
-            if i > 0:
-                low = (e + LIFT_D * (q + q_now)) * (1 / LIFT_K)
-                if r % 2 == 0:
-                    low = jnp.where(odd_lane, low, up[i - 1, r // 2])
-                done[2 * i - 2, pl.ds(r, 8, 4), :] = low
-                done[2 * i - 1, pl.ds(r, 8, 4), :] = q_now * LIFT_K
+            q_now = None
+            if i > 1:
+                q_now = o + LIFT_C * (e + e_now)
+                done[i - 1, 1, pl.ds(r, 8, 4), :] = q_now * LIFT_K
+            if i > 2:
+                done[i - 1, 0, pl.ds(r, 8, 4), :] = (e + LIFT_D * (q + q_now)) * (1 / LIFT_K)
             state[r] = (o_now, e_now, q_now)
-        if i in (4, 8, 12, 16):
-            piece = pl.ds(2 * i - 8, 8)
-            copy = pltpu.make_async_copy(done.at[piece], out_ref.at[piece], sems.at[i // 4 - 1])
-            copy.start()
-            copies.append(copy)
+
+
+def first_x(ys, r):
+    o = [ys[0, r] + LIFT_A * ys[2, r], *(ys[3 + 2 * i, r] + LIFT_A * (ys[2 + 2 * i, r] + ys[4 + 2 * i, r]) for i in range(3))]
+    e = [ys[1, r] + LIFT_B * o[0], *(ys[2 + 2 * i, r] + LIFT_B * (o[i] + o[i + 1]) for i in range(3))]
+    q = [o[i] + LIFT_C * (e[i] + e[i + 1]) for i in range(3)]
+    low = [(e[i + 1] + LIFT_D * (q[i] + q[i + 1])) * (1 / LIFT_K) for i in range(2)]
+    return low[0], q[1] * LIFT_K, low[1]
+
+
+def finish(ys, done, tl, e2_ref, e34_ref, tl_ref, zu_ref, out_ref, even, odd, sems):
+    sub = lax.broadcasted_iota(jnp.int32, (8, 128), 0)
+    lane = lax.broadcasted_iota(jnp.int32, (8, 128), 1)
+    copies = [pltpu.make_async_copy(done.at[pl.ds(1, 15), 1], out_ref.at[pl.ds(1, 15), 1], sems.at[0])]
+    copies[0].start()
+
+    def upper(u, at, rows, early):
+        v = stacked(tl[u].reshape(8 * (len(PAIRS) - EARLY), 256))
+        v = [dot(whole(tl_ref, h, rows=slice(at, at + rows), columns=240), v) for h in (0, 1)]
+        return early + jnp.where(lax.broadcasted_iota(jnp.int32, (rows, 256), 1) % 128 < 64, v[0], v[1])
+
+    v = upper(0, 0, 128, e2_ref[...])
+    l2 = wide_dot(jnp.concatenate([v[:, :128], v[:, 128:]], 0), zu_ref, 0).reshape(2, 16, 8, 128)
+    v = upper(1, 128, 96, e34_ref[...])
+    l3 = wide_dot(v[:64, :128], zu_ref, 1).reshape(8, 8, 128)
+    l4 = wide_dot(v[64:, 128:], zu_ref, 2).reshape(4, 8, 128)
+    low = {}
+    for r in range(4):
+        low[0, r], v, low[1, r] = first_x(ys, r)
+        odd[pl.ds(r, 8, 4), :] = v
+    copies.append(pltpu.make_async_copy(odd, out_ref.at[0, 1], sems.at[1]))
+    copies[-1].start()
+    odd_lane = lane % 2 == 1
+    for i in range(16):
+        for r in range(4):
+            v = low[i, r] if i < 2 else done[i, 0, pl.ds(r, 8, 4), :]
+            if r % 2 == 0:
+                w = l2[r // 2, i]
+                if i % 2 == 0 and r == 0:
+                    u = l3[i // 2]
+                    if i % 4 == 0:
+                        u = jnp.where((lane % 8 == 0) & (sub % 2 == 0), l4[i // 4], u)
+                    w = jnp.where(lane % 4 == 0, u, w)
+                v = jnp.where(odd_lane, v, w)
+            even[i, pl.ds(r, 8, 4), :] = v
+        if i % 4 == 3:
+            piece = pl.ds(i - 3, 4)
+            copies.append(pltpu.make_async_copy(even.at[piece], out_ref.at[piece, 0], sems.at[2 + i // 4]))
+            copies[-1].start()
     for copy in copies:
         copy.wait()
 
 
 def solution(mesh):
     nx, ny = mesh.shape["gx"], mesh.shape["gy"]
-    weights, (fy, z1, ty, te, tl, zu) = operators()
+    weights, (zp, fy, z1, ty, te, tl, zu) = operators()
     vmem, hbm = pl.BlockSpec(memory_space=pltpu.VMEM), pl.BlockSpec(memory_space=pltpu.HBM)
     limit = 24 * 1024 * 1024
-    block = (32, 32, 128)
+    block, pairs = (32, 32, 128), (16, 2, 32, 128)
     moves = pltpu.SemaphoreType.DMA((len(MOVES),))
 
     def kept(*ms):
@@ -466,21 +523,21 @@
     def local(v):
         parts = pl.pallas_call(
             functools.partial(exchange, nx, ny, 8, weights.tolist()),
-            out_shape=[*(pltpu.VMEM(s, F32) for s in ((36, 4, 8, 128), (2, len(PAIRS) - EARLY, 8, 256), (128, 256), (96, 256))),
+            out_shape=[*(pltpu.VMEM(s, F32) for s in ((36, 4, 8, 128), pairs, (2, len(PAIRS) - EARLY, 8, 256), (128, 256), (96, 256))),
                        *(pltpu.VMEM(m.shape, BF16) for m in (tl, zu))],
-            in_specs=[hbm] * 7, out_specs=[vmem] * 6,
-            scratch_shapes=[pltpu.VMEM(block, F32), *([pltpu.VMEM((ENTRIES, ROWS, 128), F32)] * 2), *(pltpu.VMEM(m.shape, BF16) for m in (fy, z1, ty, te)),
-                            pltpu.VMEM((2, EARLY, 8, 256), F32), pltpu.VMEM(block, F32), pltpu.VMEM((4, 32, 128), F32),
-                            moves, moves, pltpu.SemaphoreType.REGULAR((2,)), pltpu.SemaphoreType.DMA((10,))],
+            in_specs=[hbm] * 8, out_specs=[vmem] * 7,
+            scratch_shapes=[pltpu.VMEM(block, F32), *([pltpu.VMEM((ENTRIES, ROWS, 128), F32)] * 2), *(pltpu.VMEM(m.shape, BF16) for m in (zp, fy, z1, ty, te)),
+                            pltpu.VMEM((2, EARLY, 8, 256), F32), pltpu.VMEM(block, F32), pltpu.VMEM((20, 4, 8, 128), F32), pltpu.VMEM((4, 32, 128), F32),
+                            pltpu.VMEM((2, 80, 128), F32), moves, moves, pltpu.SemaphoreType.REGULAR((2,)), pltpu.SemaphoreType.DMA((11,))],
             compiler_params=pltpu.CompilerParams(collective_id=0, has_side_effects=True, vmem_limit_bytes=limit),
-        )(*kept(v, fy, z1, ty, te, tl, zu))
+        )(*kept(v, zp, fy, z1, ty, te, tl, zu))
         return pl.pallas_call(
             finish,
-            out_shape=jax.ShapeDtypeStruct(block, F32),
-            in_specs=[vmem] * 6, out_specs=pl.BlockSpec(memory_space=pl.ANY),
-            scratch_shapes=[pltpu.VMEM((16, 2, 8, 128), F32), pltpu.VMEM(block, F32), pltpu.SemaphoreType.DMA((4,))],
+            out_shape=jax.ShapeDtypeStruct(pairs, F32),
+            in_specs=[vmem] * 7, out_specs=pl.BlockSpec(memory_space=pl.ANY),
+            scratch_shapes=[pltpu.VMEM((16, 32, 128), F32), pltpu.VMEM((32, 128), F32), pltpu.SemaphoreType.DMA((6,))],
             compiler_params=pltpu.CompilerParams(vmem_limit_bytes=limit),
-        )(*parts)
+        )(*parts).reshape(block)
 
     spec = P("gx", "gy", None)
     return jax.shard_map(local, mesh=mesh, in_specs=(spec,), out_specs=spec, check_vma=False)

time: 24.4 us -> 23.3 us (0.955)
  Pallas kernels: 24.2 us -> 23.2 us
    pallas_call x1, Pallas kernels: 22.9 us -> 21.9 us  [local(): pl.pallas_call(functools.partial(exchange, nx, ny, 8, weights.tolist()),...]
where the time goes in v4:
time: 23.3 us; the launch traced here: 23.2 us
  Pallas kernels  23.2 us (100%)
    pallas_call x1, Pallas kernels, local(): pl.pallas_call(functools.partial(exchange, nx, ny, 8, weights.tolist()),...  21.9 us
    pallas_call x1, Pallas kernels, local(): pl.pallas_call(finish, out_shape=jax.ShapeDtypeStruct(pairs, F32), in_spe...  1.29 us

profile of v4, /device:TPU:1, one launch (start us, length us, event | category | flops | bytes accessed | tf_op | source)
XLA Modules:
  0.0 23.2 jit_solution(3254142965716819201)
XLA Ops:
  0.0 21.9 %shard_map.82 = (f32[36,4,8,128]{3,2,1,0:T(8,128)S(1)}, f32[16,2,32,128]{3,2,1,0:T(8,128)S(1)}, f32[2,5,8,256]{3,2,1,0:T(8,128)S(1)}, f32[128,256]{1,0:T(8,128)S...) custom-call(f32[32,32,128]{2,1,0:T(8,128)} %v_hbm.1, ...), custom_call_target="tpu_custom_call" | custom-call | tf_op jit(solution)/shard_map/pallas_call | solution.py:524
  21.9 1.3 %shard_map.83 = f32[16,2,32,128]{3,2,1,0:T(8,128)} custom-call(f32[36,4,8,128]{3,2,1,0:T(8,128)S(1)} %get-tuple-element.12.ys, f32[16,2,32,128]{3,2,1,0:T(8,128)S(1)} %get-tuple-element.13.done, f32[2,5,8,256]{3,2,1,0:T(8,128)S(1)} %get-tuple-element.14.tl, f32[128,256]{1,0:T(8,128)S(1)} %get-tuple-element.15.e2_ref, ...), custom_call_target="tpu_custom_call" | custom-call | tf_op jit(solution)/shard_map/pallas_call | solution.py:534

commit v5 on v4

--- a/solution.py
+++ b/solution.py
@@ -19,25 +19,38 @@
 Y_AT = {0: 0, -1: 32, 1: 40, -2: 48, 2: 56}
 ENTRIES, ROWS = 32, 64
 PAIRS = [X_AT[o] + p for o, c in COUNT.items() for p in range(c // 2)]
+LATE = (6, 8, 4)
 EARLY = 15
 Y_STATES = 10
 X_STATES = {1: 22, -1: 29}
 OFFSETS = (0, -1, 1, -2, 2)
-GROUP = {dx: [(dx, dy) for dy in OFFSETS if (dx, dy) != (0, 0)] for dx in OFFSETS}
+GROUP = {dx: [(dx, dy) for dy in (-2, 2, -1, 1, 0) if (dx, dy) != (0, 0)] for dx in OFFSETS}
 
 
 def pieces(dx, dy):
-    rows = (Y_AT[dy], 8)
     if dx == 0:
-        return [((0, 18 if abs(dy) == 1 else 10), rows)]
+        return [(False, (0, 18), (Y_AT[dy], 8))] if abs(dy) == 1 else [(False, (0, 10), (Y_AT[dy], 2))]
     if abs(dx) == 2:
-        return [((X_AT[dx], 1), rows)]
+        return [(False, (X_AT[dx], 1), (Y_AT[dy], 2 if abs(dy) == 2 else 4))]
     if dy == 0:
-        return [((X_STATES[dx], 2), (0, 32)), ((X_AT[dx], 4), (0, 24))]
-    return [((X_AT[dx], 5 if abs(dy) == 1 else 2), rows)]
-
-
-MOVES = [(o, piece) for dx in OFFSETS for o in GROUP[dx] for piece in pieces(*o)]
+        return [(True, (X_STATES[dx], 2), (0, 32)), (False, (X_AT[dx], 4), (0, 20))]
+    if abs(dy) == 1:
+        return [(True, (X_STATES[dx], 1), (Y_AT[dy], 4)), (False, (X_AT[dx], 4), (Y_AT[dy], 8))]
+    return [(False, (X_AT[dx], 2), (Y_AT[dy], 2))]
+
+
+MOVES = [(dx, dy, *piece) for dx in OFFSETS for dx, dy in GROUP[dx] for piece in pieces(dx, dy)]
+
+
+def unsent():
+    sent = {(e, r) for _, _, _, (e0, ne), (r0, nr) in MOVES for e in range(e0, e0 + ne) for r in range(r0, r0 + nr)}
+    out = [(e, Y_AT[dy] + 4, 4) for e in X_STATES.values() for dy in (-1, 1)]
+    for e in PAIRS:
+        for tile in range(32 if e < X_AT[1] else 0, ROWS, 8):
+            count = sum((e, r) in sent for r in range(tile, tile + 8))
+            if count < 8 and tile != 24:
+                out.append((e, tile + count, 8 - count))
+    return out
 
 
 def lift_1d(v):
@@ -88,7 +101,10 @@
     inverse = np.linalg.pinv(basis)
     weights = np.concatenate([functional[o] @ inverse for o in COUNT if o])
     cx = [np.concatenate([(combine[o] @ (functional[o].T if o else inverse))[:, h::2] for o in COUNT], 1) for h in (0, 1)]
-    early, late = [np.stack([np.kron(c[:, part], np.eye(8)) for c in cx]) for part in (slice(0, EARLY), slice(EARLY, None))]
+    first = [at + i for at, count in zip((0, 16, 24), LATE) for i in range(count)]
+    assert all(np.abs(np.delete(c[:, EARLY:], first, 0)).max() < 1e-12 for c in cx)
+    early = np.stack([np.kron(c[:, :EARLY], np.eye(8)) for c in cx])
+    late = np.stack([np.kron(c[first, EARLY:], np.eye(8)) for c in cx])
     high, mid_, low = thirds(early)
     early = np.stack([np.concatenate(m, 2) for m in ((high, high), (mid_, mid_), (low, high))])
     high, mid_, low = thirds(late)
@@ -156,12 +172,10 @@
     return dot(jnp.concatenate([high, low], 1), m[:, 2 * n:]) + v[:, n:] + v[:, :n]
 
 
-def states(s):
-    a = s(31) + LIFT_A * s(30)
-    b = s(30) + LIFT_B * (s(29) + LIFT_A * (s(28) + s(30)))
-    c = s(0)
-    d = s(0) + LIFT_B * (s(1) + LIFT_A * (s(0) + s(2)))
-    return a, b, c, d
+def states(s, side):
+    if side < 0:
+        return s(31) + LIFT_A * s(30), s(30) + LIFT_B * (s(29) + LIFT_A * (s(28) + s(30)))
+    return s(0), s(0) + LIFT_B * (s(1) + LIFT_A * (s(0) + s(2)))
 
 
 def own_basis(v):
@@ -178,20 +192,19 @@
             out.append(even + LIFT_D * (odd3 + odd3_now))
             odd3 = odd3_now
         odd, even = odd_now, even_now
-    return [*out, *states(lambda i: v[i])]
-
-
-def prepare_states(v_ref, vo_ref, xh):
-    for q, plane in enumerate(states(lambda x: v_ref[x])):
+    return [*out, *states(lambda i: v[i], -1), *states(lambda i: v[i], 1)]
+
+
+def prepare_states(dx, v_ref, vo_ref, xh):
+    e = X_STATES[dx]
+    for q, plane in enumerate(states(lambda x: v_ref[x], dx)):
         xh[q] = plane
-        vo_ref[X_STATES[-1 if q < 2 else 1] + q % 2, 0:32, :] = plane
-    for p, rows in enumerate(states(lambda y: xh[:, y, :])):
-        at = Y_AT[-1 if p < 2 else 1] + 2 * (p % 2)
-        vo_ref[X_STATES[-1], at:at + 2, :] = rows[0:2]
-        vo_ref[X_STATES[1], at:at + 2, :] = rows[2:4]
-    for e in X_STATES.values():
-        for dy in (-1, 1):
-            vo_ref[e, Y_AT[dy] + 4:Y_AT[dy] + 8, :] = jnp.zeros((4, 128), F32)
+        vo_ref[e + q, 0:32, :] = plane
+    for dy in (-1, 1):
+        at = Y_AT[dy]
+        for p, rows in enumerate(states(lambda y: xh[:, y, :], dy)):
+            vo_ref[e, at + 2 * p:at + 2 * p + 2, :] = rows
+        vo_ref[e, at + 4:at + 8, :] = jnp.zeros((4, 128), F32)
 
 
 def prepare_pairs(first, count, weights, zp_ref, fy_ref, vo_ref, basis):
@@ -221,10 +234,10 @@
 
 
 def prepare_rows(vo_ref, zt):
-    for q, rows in enumerate(states(lambda y: zt[:, y, :])):
-        at = Y_AT[-1 if q < 2 else 1]
-        for t in range(4):
-            vo_ref[Y_STATES + 4 * (q % 2) + t, at:at + 8, :] = rows[8 * t:8 * t + 8]
+    for dy in (-1, 1):
+        for q, rows in enumerate(states(lambda y: zt[:, y, :], dy)):
+            for t in range(4):
+                vo_ref[Y_STATES + 4 * q + t, Y_AT[dy]:Y_AT[dy] + 8, :] = rows[8 * t:8 * t + 8]
 
 
 def split_y(p, halo, first, last):
@@ -251,28 +264,38 @@
 
 
 def exchange(nx, ny, nz, weights, v_hbm, zp_hbm, fy_hbm, z1_hbm, ty_hbm, te_hbm, tl_hbm, zu_hbm,
-             ys_ref, done, tl_out, e2_ref, e34_ref, tl_ref, zu_ref,
-             v_ref, vo_ref, vi_ref, zp_ref, fy_ref, z1_ref, ty_ref, te_ref, te_in, zt, basis, xh, xz, send, recv, hello, sems):
+             done, tl_out, e2_ref, e34_ref, tl_ref, zu_ref,
+             v_ref, vo_ref, vi_ref, ys_ref, zp_ref, fy_ref, z1_ref, ty_ref, te_ref, te_in, zt, basis, xh, up, xz, send, recv, hello, sems):
     x, y = lax.axis_index("gx"), lax.axis_index("gy")
     z = lax.rem(x, nz)
 
     def device(dx, dy):
         return lax.rem(x + dx + nx, nx), lax.rem(y + dy + ny, ny)
 
-    copies = {dx: [] for dx in OFFSETS}
-    for i, ((dx, dy), ((e, ne), (r, nr))) in enumerate(MOVES):
+    copies = []
+    for i, (dx, dy, is_states, (e, ne), (r, nr)) in enumerate(MOVES):
         at = (pl.ds(e, ne), pl.ds(r, nr))
-        copies[dx].append(pltpu.make_async_remote_copy(
+        copies.append((dx, dy, is_states, pltpu.make_async_remote_copy(
             src_ref=vo_ref.at[at], dst_ref=vi_ref.at[at], send_sem=send.at[i], recv_sem=recv.at[i],
-            device_id=device(-dx, -dy), device_id_type=MESH))
-
-    def start(dx, part=slice(None)):
-        for copy in copies[dx][part]:
-            copy.start()
-
-    def arrive(dx):
-        for copy in copies[dx]:
-            copy.wait_recv()
+            device_id=device(-dx, -dy), device_id_type=MESH)))
+
+    def start(which, kinds=(True, False)):
+        for dx, _, is_states, copy in copies:
+            if dx == which and is_states in kinds:
+                copy.start()
+
+    def start_ahead(kinds, waits):
+        for dx, dy, is_states, copy in copies:
+            if dx == -1 and is_states in kinds:
+                if dy in (0, 1):
+                    pl.when(((x == nx - 1) & (y == dy)) == waits)(copy.start)
+                elif not waits:
+                    copy.start()
+
+    def arrive(which, kinds=(True, False)):
+        for dx, _, is_states, copy in copies:
+            if dx == which and is_states in kinds:
+                copy.wait_recv()
 
     barrier = pltpu.get_barrier_semaphore()
 
@@ -294,11 +317,8 @@
     pl.when(z < nz - 2)(lambda: greet(0))
     pl.when(z < nz - 3)(lambda: greet(1))
     pl.when(z < nz - 4)(lambda: greet(2))
-    for e in PAIRS:
-        if e in (X_AT[2], X_AT[-2]):
-            vi_ref[e, 8:24, :] = jnp.zeros((16, 128), F32)
-        elif e >= X_AT[1] and e not in (X_AT[1], X_AT[1] + 1, X_AT[-1], X_AT[-1] + 1):
-            vi_ref[e, 48:64, :] = jnp.zeros((16, 128), F32)
+    for e, r, count in unsent():
+        vi_ref[e, r:r + count, :] = jnp.zeros((count, 128), F32)
 
     @pl.when(z >= nz - 2)
     def _():
@@ -306,10 +326,11 @@
         say_hello(2, range(-2, 3))
         pl.when(z == nz - 1)(lambda: say_hello(1, range(-2, 3)))
 
-    for load in loads[:4]:
+    loads[3].wait()
+    prepare_states(-1, v_ref, vo_ref, xh)
+    pl.when(z == nz - 1)(lambda: start_ahead((True,), False))
+    for load in loads[:3]:
         load.wait()
-    prepare_states(v_ref, vo_ref, xh)
-    pl.when(z == nz - 1)(lambda: start(-1, slice(0, 1)))
     for t in range(4):
         for i, value in enumerate(own_basis([v_ref[x, 8 * t:8 * t + 8, :] for x in range(32)])):
             basis[i, t] = value
@@ -320,10 +341,11 @@
     @pl.when(z >= nz - 2)
     def _():
         start(-2)
-        pl.when(z == nz - 1)(lambda: start(-1, slice(1, None)))
+        pl.when(z == nz - 1)(lambda: start_ahead((False,), False))
 
     for load in loads[6:]:
         load.start()
+    prepare_states(1, v_ref, vo_ref, xh)
     prepare_pairs(0, EARLY, weights, zp_ref, fy_ref, vo_ref, basis)
     loads[6].wait()
     for t in range(4):
@@ -353,6 +375,7 @@
     @pl.when(z == nz - 1)
     def _():
         pl.semaphore_wait(hello.at[1], 1)
+        start_ahead((True, False), True)
 
     @pl.when(z >= nz - 2)
     def _():
@@ -402,16 +425,6 @@
         plane(x)
     upper(0, 10, te_in)
 
-    @pl.when(z < 2)
-    def _():
-        pl.semaphore_wait(hello.at[1], 5)
-        start(2)
-
-    @pl.when(z == 0)
-    def _():
-        pl.semaphore_wait(hello.at[0], 5)
-        start(1)
-
     arrive(1)
     state_planes(1)
     arrive(2)
@@ -424,19 +437,49 @@
         v = [dot(m[h][2], high_low) + dot(m[h][1], high_mid) + dot(m[h][0], high_mid) for h in (0, 1)]
         ref[...] = jnp.where(lax.broadcasted_iota(jnp.int32, (rows, 256), 1) % 128 < 64, v[0], v[1])
 
-    lift_x(ys_ref, done)
+    loads[10].wait()
+    l2 = wide_dot(jnp.concatenate([e2_ref[:, :128], e2_ref[:, 128:]], 0), zu_ref, 0).reshape(2, 16, 8, 128)
+    l3 = wide_dot(e34_ref[:64, :128], zu_ref, 1).reshape(8, 8, 128)
+    l4 = wide_dot(e34_ref[64:, 128:], zu_ref, 2).reshape(4, 8, 128)
+    for i in range(2, 16):
+        for t in (0, 1):
+            up[i, t] = merge(i, t, l2[t, i], l3, l4)
+    lift_x(ys_ref, up, done)
     loads[9].wait()
-    loads[10].wait()
-    arrive(-1)
+
+    @pl.when(z < 2)
+    def _():
+        pl.semaphore_wait(hello.at[1], 5)
+        start(2)
+
+    @pl.when(z == 0)
+    def _():
+        pl.semaphore_wait(hello.at[0], 5)
+        start(1)
+
+    arrive(-1, (True,))
+    state_planes(-1)
+    first_x(ys_ref, done)
     arrive(-2)
-    state_planes(-1)
+    arrive(-1, (False,))
     upper(15, 5, tl_out)
-    for dx in OFFSETS:
-        for copy in copies[dx]:
-            copy.wait_send()
-
-
-def lift_x(ys, done):
+    for *_, copy in copies:
+        copy.wait_send()
+
+
+def merge(i, t, v, l3, l4):
+    sub = lax.broadcasted_iota(jnp.int32, (8, 128), 0)
+    lane = lax.broadcasted_iota(jnp.int32, (8, 128), 1)
+    if i % 2 or t:
+        return v
+    w = l3[i // 2]
+    if i % 4 == 0:
+        w = jnp.where((lane % 8 == 0) & (sub % 2 == 0), l4[i // 4], w)
+    return jnp.where(lane % 4 == 0, w, v)
+
+
+def lift_x(ys, up, done):
+    odd_lane = lax.broadcasted_iota(jnp.int32, (8, 128), 1) % 2 == 1
     state = {}
     for r in range(4):
         state[r] = (ys[3, r] + LIFT_A * (ys[2, r] + ys[4, r]), None, None)
@@ -454,57 +497,55 @@
                 q_now = o + LIFT_C * (e + e_now)
                 done[i - 1, 1, pl.ds(r, 8, 4), :] = q_now * LIFT_K
             if i > 2:
-                done[i - 1, 0, pl.ds(r, 8, 4), :] = (e + LIFT_D * (q + q_now)) * (1 / LIFT_K)
+                low = (e + LIFT_D * (q + q_now)) * (1 / LIFT_K)
+                done[i - 1, 0, pl.ds(r, 8, 4), :] = low if r % 2 else jnp.where(odd_lane, low, up[i - 1, r // 2])
             state[r] = (o_now, e_now, q_now)
 
 
-def first_x(ys, r):
-    o = [ys[0, r] + LIFT_A * ys[2, r], *(ys[3 + 2 * i, r] + LIFT_A * (ys[2 + 2 * i, r] + ys[4 + 2 * i, r]) for i in range(3))]
-    e = [ys[1, r] + LIFT_B * o[0], *(ys[2 + 2 * i, r] + LIFT_B * (o[i] + o[i + 1]) for i in range(3))]
-    q = [o[i] + LIFT_C * (e[i] + e[i + 1]) for i in range(3)]
-    low = [(e[i + 1] + LIFT_D * (q[i] + q[i + 1])) * (1 / LIFT_K) for i in range(2)]
-    return low[0], q[1] * LIFT_K, low[1]
-
-
-def finish(ys, done, tl, e2_ref, e34_ref, tl_ref, zu_ref, out_ref, even, odd, sems):
-    sub = lax.broadcasted_iota(jnp.int32, (8, 128), 0)
+def first_x(ys, done):
+    for r in range(4):
+        o = [ys[0, r] + LIFT_A * ys[2, r], *(ys[3 + 2 * i, r] + LIFT_A * (ys[2 + 2 * i, r] + ys[4 + 2 * i, r]) for i in range(3))]
+        e = [ys[1, r] + LIFT_B * o[0], *(ys[2 + 2 * i, r] + LIFT_B * (o[i] + o[i + 1]) for i in range(3))]
+        q = [o[i] + LIFT_C * (e[i] + e[i + 1]) for i in range(3)]
+        for i in range(2):
+            done[i, 0, pl.ds(r, 8, 4), :] = (e[i + 1] + LIFT_D * (q[i] + q[i + 1])) * (1 / LIFT_K)
+        done[0, 1, pl.ds(r, 8, 4), :] = q[1] * LIFT_K
+
+
+def finish(done, tl, e2_ref, e34_ref, tl_ref, zu_ref, out_ref, even, sems):
     lane = lax.broadcasted_iota(jnp.int32, (8, 128), 1)
-    copies = [pltpu.make_async_copy(done.at[pl.ds(1, 15), 1], out_ref.at[pl.ds(1, 15), 1], sems.at[0])]
-    copies[0].start()
-
-    def upper(u, at, rows, early):
+    copies = []
+
+    def store(source, at, side):
+        copies.append(pltpu.make_async_copy(source, out_ref.at[at, side], sems.at[len(copies)]))
+        copies[-1].start()
+
+    for at in ((0, 16, 1), (5, 6, 0), (7, 8, 0), (9, 10, 0), (11, 12, 0), (13, 16, 0)):
+        piece = pl.ds(at[0], at[1] - at[0])
+        store(done.at[piece, at[2]], piece, at[2])
+
+    def late(u, at, rows):
         v = stacked(tl[u].reshape(8 * (len(PAIRS) - EARLY), 256))
         v = [dot(whole(tl_ref, h, rows=slice(at, at + rows), columns=240), v) for h in (0, 1)]
-        return early + jnp.where(lax.broadcasted_iota(jnp.int32, (rows, 256), 1) % 128 < 64, v[0], v[1])
-
-    v = upper(0, 0, 128, e2_ref[...])
-    l2 = wide_dot(jnp.concatenate([v[:, :128], v[:, 128:]], 0), zu_ref, 0).reshape(2, 16, 8, 128)
-    v = upper(1, 128, 96, e34_ref[...])
+        return jnp.where(lax.broadcasted_iota(jnp.int32, (rows, 256), 1) % 128 < 64, v[0], v[1])
+
+    v = e2_ref[0:48, :] + late(0, 0, 48)
+    l2 = wide_dot(jnp.concatenate([v[:, :128], v[:, 128:]], 0), zu_ref, 0).reshape(2, 6, 8, 128)
+    v = e34_ref[...] + late(1, 48, 96)
     l3 = wide_dot(v[:64, :128], zu_ref, 1).reshape(8, 8, 128)
     l4 = wide_dot(v[64:, 128:], zu_ref, 2).reshape(4, 8, 128)
-    low = {}
-    for r in range(4):
-        low[0, r], v, low[1, r] = first_x(ys, r)
-        odd[pl.ds(r, 8, 4), :] = v
-    copies.append(pltpu.make_async_copy(odd, out_ref.at[0, 1], sems.at[1]))
-    copies[-1].start()
-    odd_lane = lane % 2 == 1
-    for i in range(16):
+    for k, i in enumerate((0, 1, 2, 3, 4, 6, 8, 10, 12)):
         for r in range(4):
-            v = low[i, r] if i < 2 else done[i, 0, pl.ds(r, 8, 4), :]
-            if r % 2 == 0:
-                w = l2[r // 2, i]
-                if i % 2 == 0 and r == 0:
-                    u = l3[i // 2]
-                    if i % 4 == 0:
-                        u = jnp.where((lane % 8 == 0) & (sub % 2 == 0), l4[i // 4], u)
-                    w = jnp.where(lane % 4 == 0, u, w)
-                v = jnp.where(odd_lane, v, w)
-            even[i, pl.ds(r, 8, 4), :] = v
-        if i % 4 == 3:
-            piece = pl.ds(i - 3, 4)
-            copies.append(pltpu.make_async_copy(even.at[piece], out_ref.at[piece, 0], sems.at[2 + i // 4]))
-            copies[-1].start()
+            v = done[i, 0, pl.ds(r, 8, 4), :]
+            if i < 5 and r % 2 == 0:
+                v = jnp.where(lane % 2 == 1, v, merge(i, r // 2, l2[r // 2, i], l3, l4))
+            elif r == 0:
+                v = merge(i, 0, v, l3, l4)
+            even[k, pl.ds(r, 8, 4), :] = v
+        if i == 4:
+            store(even.at[pl.ds(0, 5)], pl.ds(0, 5), 0)
+        elif i > 4:
+            store(even.at[k], i, 0)
     for copy in copies:
         copy.wait()
 
@@ -523,19 +564,19 @@
     def local(v):
         parts = pl.pallas_call(
             functools.partial(exchange, nx, ny, 8, weights.tolist()),
-            out_shape=[*(pltpu.VMEM(s, F32) for s in ((36, 4, 8, 128), pairs, (2, len(PAIRS) - EARLY, 8, 256), (128, 256), (96, 256))),
+            out_shape=[*(pltpu.VMEM(s, F32) for s in (pairs, (2, len(PAIRS) - EARLY, 8, 256), (128, 256), (96, 256))),
                        *(pltpu.VMEM(m.shape, BF16) for m in (tl, zu))],
-            in_specs=[hbm] * 8, out_specs=[vmem] * 7,
-            scratch_shapes=[pltpu.VMEM(block, F32), *([pltpu.VMEM((ENTRIES, ROWS, 128), F32)] * 2), *(pltpu.VMEM(m.shape, BF16) for m in (zp, fy, z1, ty, te)),
-                            pltpu.VMEM((2, EARLY, 8, 256), F32), pltpu.VMEM(block, F32), pltpu.VMEM((20, 4, 8, 128), F32), pltpu.VMEM((4, 32, 128), F32),
+            in_specs=[hbm] * 8, out_specs=[vmem] * 6,
+            scratch_shapes=[pltpu.VMEM(block, F32), *([pltpu.VMEM((ENTRIES, ROWS, 128), F32)] * 2), pltpu.VMEM((36, 4, 8, 128), F32), *(pltpu.VMEM(m.shape, BF16) for m in (zp, fy, z1, ty, te)),
+                            pltpu.VMEM((2, EARLY, 8, 256), F32), pltpu.VMEM(block, F32), pltpu.VMEM((20, 4, 8, 128), F32), pltpu.VMEM((2, 32, 128), F32), pltpu.VMEM((16, 2, 8, 128), F32),
                             pltpu.VMEM((2, 80, 128), F32), moves, moves, pltpu.SemaphoreType.REGULAR((2,)), pltpu.SemaphoreType.DMA((11,))],
             compiler_params=pltpu.CompilerParams(collective_id=0, has_side_effects=True, vmem_limit_bytes=limit),
         )(*kept(v, zp, fy, z1, ty, te, tl, zu))
         return pl.pallas_call(
             finish,
             out_shape=jax.ShapeDtypeStruct(pairs, F32),
-            in_specs=[vmem] * 7, out_specs=pl.BlockSpec(memory_space=pl.ANY),
-            scratch_shapes=[pltpu.VMEM((16, 32, 128), F32), pltpu.VMEM((32, 128), F32), pltpu.SemaphoreType.DMA((6,))],
+            in_specs=[vmem] * 6, out_specs=pl.BlockSpec(memory_space=pl.ANY),
+            scratch_shapes=[pltpu.VMEM((9, 32, 128), F32), pltpu.SemaphoreType.DMA((11,))],
             compiler_params=pltpu.CompilerParams(vmem_limit_bytes=limit),
         )(*parts).reshape(block)
 

time: 23.3 us -> 21.3 us (0.914)
  Pallas kernels: 23.2 us -> 21.2 us
    pallas_call x1, Pallas kernels: 21.9 us -> 19.9 us  [local(): pl.pallas_call(functools.partial(exchange, nx, ny, 8, weights.tolist()),...]
where the time goes in v5:
time: 21.3 us; the launch traced here: 21.2 us
  Pallas kernels  21.2 us (100%)
    pallas_call x1, Pallas kernels, local(): pl.pallas_call(functools.partial(exchange, nx, ny, 8, weights.tolist()),...  19.9 us
    pallas_call x1, Pallas kernels, local(): pl.pallas_call(finish, out_shape=jax.ShapeDtypeStruct(pairs, F32), in_spe...  1.24 us

profile of v5, /device:TPU:1, one launch (start us, length us, event | category | flops | bytes accessed | tf_op | source)
XLA Modules:
  0.0 21.2 jit_solution(14310576035615135580)
XLA Ops:
  0.0 19.9 %shard_map.82 = (f32[16,2,32,128]{3,2,1,0:T(8,128)S(1)}, f32[2,5,8,256]{3,2,1,0:T(8,128)S(1)}, f32[128,256]{1,0:T(8,128)S(1)}, f32[96,256]{1,0:T(8,128)S(1)}, bf...) custom-call(f32[32,32,128]{2,1,0:T(8,128)} %v_hbm.1, ...), custom_call_target="tpu_custom_call" | custom-call | tf_op jit(solution)/shard_map/pallas_call | solution.py:565
  19.9 1.2 %shard_map.83 = f32[16,2,32,128]{3,2,1,0:T(8,128)} custom-call(f32[16,2,32,128]{3,2,1,0:T(8,128)S(1)} %get-tuple-element.11.done, f32[2,5,8,256]{3,2,1,0:T(8,128)S(1)} %get-tuple-element.12.tl, f32[128,256]{1,0:T(8,128)S(1)} %get-tuple-element.13.e2_ref, f32[96,256]{1,0:T(8,128)S(1)} %get-tuple-element.14.e34_ref, ...), custom_call_target="tpu_custom_call" | custom-call | tf_op jit(solution)/shard_map/pallas_call | solution.py:575

commit v6 on v5

--- a/solution.py
+++ b/solution.py
@@ -35,11 +35,22 @@
     if dy == 0:
         return [(True, (X_STATES[dx], 2), (0, 32)), (False, (X_AT[dx], 4), (0, 20))]
     if abs(dy) == 1:
-        return [(True, (X_STATES[dx], 1), (Y_AT[dy], 4)), (False, (X_AT[dx], 4), (Y_AT[dy], 8))]
+        return [(True, (X_STATES[dx], 1), (Y_AT[dy], 4)), (False, (X_AT[dx], 4), (Y_AT[dy], 7))]
     return [(False, (X_AT[dx], 2), (Y_AT[dy], 2))]
 
 
 MOVES = [(dx, dy, *piece) for dx in OFFSETS for dx, dy in GROUP[dx] for piece in pieces(dx, dy)]
+
+
+def counter(dx, dy, is_states):
+    return ["0 1", "0 2", "-1 s", "-1 p", "1 s", "1 p", "-2 p", "2 p"].index(f"0 {abs(dy)}" if dx == 0 else f"{dx} {'s' if is_states else 'p'}")
+
+
+COUNTERS = 8
+
+
+def area(rows):
+    return next((rows // r, r) for r in range(ROWS, 0, -1) if rows % r == 0 and rows // r <= ENTRIES)
 
 
 def unsent():
@@ -272,12 +283,18 @@
     def device(dx, dy):
         return lax.rem(x + dx + nx, nx), lax.rem(y + dy + ny, ny)
 
-    copies = []
-    for i, (dx, dy, is_states, (e, ne), (r, nr)) in enumerate(MOVES):
-        at = (pl.ds(e, ne), pl.ds(r, nr))
+    copies, arriving = [], [0] * COUNTERS
+    for dx, dy, is_states, (e, ne), (r, nr) in MOVES:
+        at, k = (pl.ds(e, ne), pl.ds(r, nr)), counter(dx, dy, is_states)
+        arriving[k] += ne * nr
         copies.append((dx, dy, is_states, pltpu.make_async_remote_copy(
-            src_ref=vo_ref.at[at], dst_ref=vi_ref.at[at], send_sem=send.at[i], recv_sem=recv.at[i],
+            src_ref=vo_ref.at[at], dst_ref=vi_ref.at[at], send_sem=send, recv_sem=recv.at[k],
             device_id=device(-dx, -dy), device_id_type=MESH)))
+
+    def wait_rows(sem, rows):
+        n, r = area(rows)
+        some = vi_ref.at[pl.ds(0, n), pl.ds(0, r)]
+        pltpu.make_async_copy(some, some, sem).wait()
 
     def start(which, kinds=(True, False)):
         for dx, _, is_states, copy in copies:
@@ -293,9 +310,8 @@
                     copy.start()
 
     def arrive(which, kinds=(True, False)):
-        for dx, _, is_states, copy in copies:
-            if dx == which and is_states in kinds:
-                copy.wait_recv()
+        for k in sorted({counter(dx, dy, is_states) for dx, dy, is_states, _ in copies if dx == which and is_states in kinds}):
+            wait_rows(recv.at[k], arriving[k])
 
     barrier = pltpu.get_barrier_semaphore()
 
@@ -307,35 +323,36 @@
         for dy in dys:
             pl.semaphore_signal(hello.at[dx - 1], inc=1, device_id=device(dx, dy), device_id_type=MESH)
 
+    loads = [pltpu.make_async_copy(a, b, sems.at[i]) for i, (a, b) in enumerate(
+        ((v_hbm, v_ref), (zp_hbm, zp_ref), (fy_hbm, fy_ref), (z1_hbm, z1_ref), (ty_hbm, ty_ref), (te_hbm, te_ref), (tl_hbm, tl_ref), (zu_hbm, zu_ref)))]
+    loads[0].start()
+    pl.when(z != nz - 1)(lambda: greet(-1))
     greet(-2)
-    pl.when(z != nz - 1)(lambda: greet(-1))
-    loads = [pltpu.make_async_copy(v_hbm.at[pl.ds(8 * t, 8)], v_ref.at[pl.ds(8 * t, 8)], sems.at[t]) for t in range(4)]
-    loads += [pltpu.make_async_copy(a, b, sems.at[4 + i]) for i, (a, b) in enumerate(
-        ((zp_hbm, zp_ref), (fy_hbm, fy_ref), (z1_hbm, z1_ref), (ty_hbm, ty_ref), (te_hbm, te_ref), (tl_hbm, tl_ref), (zu_hbm, zu_ref)))]
-    for i in (3, 0, 1, 2, 4, 5):
-        loads[i].start()
-    pl.when(z < nz - 2)(lambda: greet(0))
-    pl.when(z < nz - 3)(lambda: greet(1))
-    pl.when(z < nz - 4)(lambda: greet(2))
+    loads[1].start()
+    loads[2].start()
+
+    @pl.when(z >= nz - 2)
+    def _():
+        pl.semaphore_wait(barrier, jnp.where(z == nz - 2, 5, 10))
+        pl.when(z == nz - 1)(lambda: say_hello(1, range(-2, 3)))
+        say_hello(2, range(-2, 3))
+
+    @pl.when(z < nz - 2)
+    def _():
+        greet(0)
+        pl.when(z < nz - 3)(lambda: greet(1))
+        pl.when(z < nz - 4)(lambda: greet(2))
+
     for e, r, count in unsent():
         vi_ref[e, r:r + count, :] = jnp.zeros((count, 128), F32)
-
-    @pl.when(z >= nz - 2)
-    def _():
-        pl.semaphore_wait(barrier, jnp.where(z == nz - 2, 5, 10))
-        say_hello(2, range(-2, 3))
-        pl.when(z == nz - 1)(lambda: say_hello(1, range(-2, 3)))
-
-    loads[3].wait()
+    loads[0].wait()
     prepare_states(-1, v_ref, vo_ref, xh)
     pl.when(z == nz - 1)(lambda: start_ahead((True,), False))
-    for load in loads[:3]:
-        load.wait()
     for t in range(4):
         for i, value in enumerate(own_basis([v_ref[x, 8 * t:8 * t + 8, :] for x in range(32)])):
             basis[i, t] = value
-    loads[4].wait()
-    loads[5].wait()
+    loads[1].wait()
+    loads[2].wait()
     prepare_pairs(EARLY, len(PAIRS) - EARLY, weights, zp_ref, fy_ref, vo_ref, basis)
 
     @pl.when(z >= nz - 2)
@@ -343,11 +360,11 @@
         start(-2)
         pl.when(z == nz - 1)(lambda: start_ahead((False,), False))
 
-    for load in loads[6:]:
+    for load in loads[3:]:
         load.start()
     prepare_states(1, v_ref, vo_ref, xh)
     prepare_pairs(0, EARLY, weights, zp_ref, fy_ref, vo_ref, basis)
-    loads[6].wait()
+    loads[3].wait()
     for t in range(4):
         zt[:, 8 * t:8 * t + 8, :] = wide_dot(v_ref[:, 8 * t:8 * t + 8, :].reshape(256, 128), z1_ref).reshape(32, 8, 128)
     prepare_rows(vo_ref, zt)
@@ -419,7 +436,7 @@
                 for t in range(4):
                     out_ref[t // 2, first_pair % EARLY + i + j, :, 128 * (t % 2):128 * (t % 2) + 128] = r[8 * t:8 * t + 8, 128 * j:128 * j + 128]
 
-    loads[7].wait()
+    loads[4].wait()
     arrive(0)
     for x in range(32):
         plane(x)
@@ -429,7 +446,7 @@
     state_planes(1)
     arrive(2)
     upper(10, 5, te_in)
-    loads[8].wait()
+    loads[5].wait()
     for u, (ref, at, rows) in enumerate(((e2_ref, 0, 128), (e34_ref, 128, 96))):
         high, mid, low = split(te_in[u].reshape(8 * EARLY, 256))
         high_mid, high_low = [jnp.concatenate([high, w], 0) for w in (mid, low)]
@@ -437,7 +454,7 @@
         v = [dot(m[h][2], high_low) + dot(m[h][1], high_mid) + dot(m[h][0], high_mid) for h in (0, 1)]
         ref[...] = jnp.where(lax.broadcasted_iota(jnp.int32, (rows, 256), 1) % 128 < 64, v[0], v[1])
 
-    loads[10].wait()
+    loads[7].wait()
     l2 = wide_dot(jnp.concatenate([e2_ref[:, :128], e2_ref[:, 128:]], 0), zu_ref, 0).reshape(2, 16, 8, 128)
     l3 = wide_dot(e34_ref[:64, :128], zu_ref, 1).reshape(8, 8, 128)
     l4 = wide_dot(e34_ref[64:, 128:], zu_ref, 2).reshape(4, 8, 128)
@@ -445,7 +462,7 @@
         for t in (0, 1):
             up[i, t] = merge(i, t, l2[t, i], l3, l4)
     lift_x(ys_ref, up, done)
-    loads[9].wait()
+    loads[6].wait()
 
     @pl.when(z < 2)
     def _():
@@ -463,8 +480,7 @@
     arrive(-2)
     arrive(-1, (False,))
     upper(15, 5, tl_out)
-    for *_, copy in copies:
-        copy.wait_send()
+    wait_rows(send, sum(arriving))
 
 
 def merge(i, t, v, l3, l4):
@@ -512,13 +528,11 @@
         done[0, 1, pl.ds(r, 8, 4), :] = q[1] * LIFT_K
 
 
-def finish(done, tl, e2_ref, e34_ref, tl_ref, zu_ref, out_ref, even, sems):
+def finish(done, tl, e2_ref, e34_ref, tl_ref, zu_ref, out_ref, even, sem):
     lane = lax.broadcasted_iota(jnp.int32, (8, 128), 1)
-    copies = []
 
     def store(source, at, side):
-        copies.append(pltpu.make_async_copy(source, out_ref.at[at, side], sems.at[len(copies)]))
-        copies[-1].start()
+        pltpu.make_async_copy(source, out_ref.at[at, side], sem).start()
 
     for at in ((0, 16, 1), (5, 6, 0), (7, 8, 0), (9, 10, 0), (11, 12, 0), (13, 16, 0)):
         piece = pl.ds(at[0], at[1] - at[0])
@@ -546,8 +560,7 @@
             store(even.at[pl.ds(0, 5)], pl.ds(0, 5), 0)
         elif i > 4:
             store(even.at[k], i, 0)
-    for copy in copies:
-        copy.wait()
+    pltpu.make_async_copy(done, out_ref, sem).wait()
 
 
 def solution(mesh):
@@ -556,7 +569,6 @@
     vmem, hbm = pl.BlockSpec(memory_space=pltpu.VMEM), pl.BlockSpec(memory_space=pltpu.HBM)
     limit = 24 * 1024 * 1024
     block, pairs = (32, 32, 128), (16, 2, 32, 128)
-    moves = pltpu.SemaphoreType.DMA((len(MOVES),))
 
     def kept(*ms):
         return [pltpu.with_memory_space_constraint(jnp.asarray(m), pltpu.HBM) for m in ms]
@@ -569,14 +581,14 @@
             in_specs=[hbm] * 8, out_specs=[vmem] * 6,
             scratch_shapes=[pltpu.VMEM(block, F32), *([pltpu.VMEM((ENTRIES, ROWS, 128), F32)] * 2), pltpu.VMEM((36, 4, 8, 128), F32), *(pltpu.VMEM(m.shape, BF16) for m in (zp, fy, z1, ty, te)),
                             pltpu.VMEM((2, EARLY, 8, 256), F32), pltpu.VMEM(block, F32), pltpu.VMEM((20, 4, 8, 128), F32), pltpu.VMEM((2, 32, 128), F32), pltpu.VMEM((16, 2, 8, 128), F32),
-                            pltpu.VMEM((2, 80, 128), F32), moves, moves, pltpu.SemaphoreType.REGULAR((2,)), pltpu.SemaphoreType.DMA((11,))],
+                            pltpu.VMEM((2, 80, 128), F32), pltpu.SemaphoreType.DMA, pltpu.SemaphoreType.DMA((COUNTERS,)), pltpu.SemaphoreType.REGULAR((2,)), pltpu.SemaphoreType.DMA((8,))],
             compiler_params=pltpu.CompilerParams(collective_id=0, has_side_effects=True, vmem_limit_bytes=limit),
         )(*kept(v, zp, fy, z1, ty, te, tl, zu))
         return pl.pallas_call(
             finish,
             out_shape=jax.ShapeDtypeStruct(pairs, F32),
             in_specs=[vmem] * 6, out_specs=pl.BlockSpec(memory_space=pl.ANY),
-            scratch_shapes=[pltpu.VMEM((9, 32, 128), F32), pltpu.SemaphoreType.DMA((11,))],
+            scratch_shapes=[pltpu.VMEM((9, 32, 128), F32), pltpu.SemaphoreType.DMA],
             compiler_params=pltpu.CompilerParams(vmem_limit_bytes=limit),
         )(*parts).reshape(block)
 

time: 21.3 us -> 20.5 us (0.962)
  Pallas kernels: 21.2 us -> 20.4 us
    pallas_call x1, Pallas kernels: 19.9 us -> 19.2 us  [local(): pl.pallas_call(functools.partial(exchange, nx, ny, 8, weights.tolist()),...]
where the time goes in v6:
time: 20.5 us; the launch traced here: 20.4 us
  Pallas kernels  20.4 us (100%)
    pallas_call x1, Pallas kernels, local(): pl.pallas_call(functools.partial(exchange, nx, ny, 8, weights.tolist()),...  19.2 us
    pallas_call x1, Pallas kernels, local(): pl.pallas_call(finish, out_shape=jax.ShapeDtypeStruct(pairs, F32), in_spe...  1.15 us

profile of v6, /device:TPU:1, one launch (start us, length us, event | category | flops | bytes accessed | tf_op | source)
XLA Modules:
  0.0 20.4 jit_solution(10906238190679309791)
XLA Ops:
  0.0 19.2 %shard_map.82 = (f32[16,2,32,128]{3,2,1,0:T(8,128)S(1)}, f32[2,5,8,256]{3,2,1,0:T(8,128)S(1)}, f32[128,256]{1,0:T(8,128)S(1)}, f32[96,256]{1,0:T(8,128)S(1)}, bf...) custom-call(f32[32,32,128]{2,1,0:T(8,128)} %v_hbm.1, ...), custom_call_target="tpu_custom_call" | custom-call | tf_op jit(solution)/shard_map/pallas_call | solution.py:577
  19.2 1.1 %shard_map.83 = f32[16,2,32,128]{3,2,1,0:T(8,128)} custom-call(f32[16,2,32,128]{3,2,1,0:T(8,128)S(1)} %get-tuple-element.11.done, f32[2,5,8,256]{3,2,1,0:T(8,128)S(1)} %get-tuple-element.12.tl, f32[128,256]{1,0:T(8,128)S(1)} %get-tuple-element.13.e2_ref, f32[96,256]{1,0:T(8,128)S(1)} %get-tuple-element.14.e34_ref, ...), custom_call_target="tpu_custom_call" | custom-call | tf_op jit(solution)/shard_map/pallas_call | solution.py:587

commit v7 on v6

--- a/solution.py
+++ b/solution.py
@@ -19,7 +19,7 @@
 Y_AT = {0: 0, -1: 32, 1: 40, -2: 48, 2: 56}
 ENTRIES, ROWS = 32, 64
 PAIRS = [X_AT[o] + p for o, c in COUNT.items() for p in range(c // 2)]
-LATE = (6, 8, 4)
+LATE = (5, 7, 4)
 EARLY = 15
 Y_STATES = 10
 X_STATES = {1: 22, -1: 29}
@@ -42,11 +42,11 @@
 MOVES = [(dx, dy, *piece) for dx in OFFSETS for dx, dy in GROUP[dx] for piece in pieces(dx, dy)]
 
 
-def counter(dx, dy, is_states):
-    return ["0 1", "0 2", "-1 s", "-1 p", "1 s", "1 p", "-2 p", "2 p"].index(f"0 {abs(dy)}" if dx == 0 else f"{dx} {'s' if is_states else 'p'}")
-
-
-COUNTERS = 8
+def counter(dx, is_states):
+    return 0 if dx == 0 else 1 if dx > 0 else 2 if is_states else 3
+
+
+COUNTERS = 4
 
 
 def area(rows):
@@ -112,14 +112,11 @@
     inverse = np.linalg.pinv(basis)
     weights = np.concatenate([functional[o] @ inverse for o in COUNT if o])
     cx = [np.concatenate([(combine[o] @ (functional[o].T if o else inverse))[:, h::2] for o in COUNT], 1) for h in (0, 1)]
-    first = [at + i for at, count in zip((0, 16, 24), LATE) for i in range(count)]
-    assert all(np.abs(np.delete(c[:, EARLY:], first, 0)).max() < 1e-12 for c in cx)
+    late = [[[tuple(c[at + i, p] for c in cx) for p in range(EARLY, len(PAIRS))] for i in range(count)] for at, count in zip((0, 16, 24), LATE)]
+    assert all(np.abs(c[at + count:end, EARLY:]).max(initial=0) < 1e-12 for c in cx for at, count, end in zip((0, 16, 24), LATE, (16, 24, 28)))
     early = np.stack([np.kron(c[:, :EARLY], np.eye(8)) for c in cx])
-    late = np.stack([np.kron(c[first, EARLY:], np.eye(8)) for c in cx])
     high, mid_, low = thirds(early)
     early = np.stack([np.concatenate(m, 2) for m in ((high, high), (mid_, mid_), (low, high))])
-    high, mid_, low = thirds(late)
-    late = np.concatenate([high, high, high, mid_, mid_, low], 2)
     fy, cy = np.zeros((ROWS, 32)), np.zeros((28, ROWS))
     for offset, count in COUNT.items():
         at = Y_AT[offset]
@@ -138,7 +135,7 @@
         low, high = lift_1d(low)
         zu[level, :, ::2 << level] = interleave(low, high).T
     zu = np.stack([wide(np.concatenate([m, m])) for m in zu])
-    return weights, [tiles(m) for m in (zp, fy, z1, ty, early, late, zu)]
+    return weights, late, [tiles(m) for m in (zp, fy, z1, ty, early, zu)]
 
 
 def wide(matrix):
@@ -218,25 +215,21 @@
         vo_ref[e, at + 4:at + 8, :] = jnp.zeros((4, 128), F32)
 
 
-def prepare_pairs(first, count, weights, zp_ref, fy_ref, vo_ref, basis):
-    sides = []
-    for h in (0, 1):
-        rows = []
-        for i in range(first, first + count):
-            f = 2 * i + h
-            for t in range(4):
-                if f < 20:
-                    rows.append(basis[f, t])
-                    continue
-                terms = [w * basis[k, t] for k, w in enumerate(weights[f - 20]) if abs(w) > 1e-14]
-                while len(terms) > 1:
-                    terms = [sum(terms[k:k + 2][1:], terms[k]) for k in range(0, len(terms), 2)]
-                rows.append(terms[0] if terms else jnp.zeros((8, 128), F32))
-        sides.append(jnp.concatenate(rows, 0))
+def functional(f, values, weights):
+    if f < 20:
+        return values[f]
+    terms = [w * value for w, value in zip(weights[f - 20], values) if abs(w) > 1e-14]
+    while len(terms) > 1:
+        terms = [sum(terms[k:k + 2][1:], terms[k]) for k in range(0, len(terms), 2)]
+    return terms[0] if terms else jnp.zeros((8, 128), F32)
+
+
+def prepare_pairs(first, sides, zp_ref, fy_ref, vo_ref):
     high, mid, low = split(jnp.concatenate(sides, 1))
     m = whole(zp_ref)
     packed = dot(high, m[:, :256]) + dot(mid, m[:, :256])
     packed = dot(low, m[:, :128]) + dot(high, m[:, 256:]) + packed[:, 128:] + packed[:, :128]
+    count = packed.shape[0] // 32
     columns = [stacked(packed[32 * i:32 * i + 32]) for i in range(count)]
     for i in range(0, count, 2):
         rows = dot(whole(fy_ref, columns=192), jnp.concatenate(columns[i:i + 2], 1))
@@ -274,9 +267,9 @@
     return f0 * (1 / LIFT_K), q0 * LIFT_K, f1 * (1 / LIFT_K), q1 * LIFT_K
 
 
-def exchange(nx, ny, nz, weights, v_hbm, zp_hbm, fy_hbm, z1_hbm, ty_hbm, te_hbm, tl_hbm, zu_hbm,
-             done, tl_out, e2_ref, e34_ref, tl_ref, zu_ref,
-             v_ref, vo_ref, vi_ref, ys_ref, zp_ref, fy_ref, z1_ref, ty_ref, te_ref, te_in, zt, basis, xh, up, xz, send, recv, hello, sems):
+def exchange(nx, ny, nz, weights, late, v_hbm, zp_hbm, fy_hbm, z1_hbm, ty_hbm, te_hbm, zu_hbm, done,
+             v_ref, vo_ref, vi_ref, ys_ref, zp_ref, fy_ref, z1_ref, ty_ref, te_ref, zu_ref, te_in, tl_in, e2_ref, e34_ref,
+             zt, basis, sides, xh, up, xz, send, recv, hello, sems):
     x, y = lax.axis_index("gx"), lax.axis_index("gy")
     z = lax.rem(x, nz)
 
@@ -285,7 +278,7 @@
 
     copies, arriving = [], [0] * COUNTERS
     for dx, dy, is_states, (e, ne), (r, nr) in MOVES:
-        at, k = (pl.ds(e, ne), pl.ds(r, nr)), counter(dx, dy, is_states)
+        at, k = (pl.ds(e, ne), pl.ds(r, nr)), counter(dx, is_states)
         arriving[k] += ne * nr
         copies.append((dx, dy, is_states, pltpu.make_async_remote_copy(
             src_ref=vo_ref.at[at], dst_ref=vi_ref.at[at], send_sem=send, recv_sem=recv.at[k],
@@ -309,9 +302,8 @@
                 elif not waits:
                     copy.start()
 
-    def arrive(which, kinds=(True, False)):
-        for k in sorted({counter(dx, dy, is_states) for dx, dy, is_states, _ in copies if dx == which and is_states in kinds}):
-            wait_rows(recv.at[k], arriving[k])
+    def arrive(k):
+        wait_rows(recv.at[k], arriving[k])
 
     barrier = pltpu.get_barrier_semaphore()
 
@@ -324,12 +316,14 @@
             pl.semaphore_signal(hello.at[dx - 1], inc=1, device_id=device(dx, dy), device_id_type=MESH)
 
     loads = [pltpu.make_async_copy(a, b, sems.at[i]) for i, (a, b) in enumerate(
-        ((v_hbm, v_ref), (zp_hbm, zp_ref), (fy_hbm, fy_ref), (z1_hbm, z1_ref), (ty_hbm, ty_ref), (te_hbm, te_ref), (tl_hbm, tl_ref), (zu_hbm, zu_ref)))]
-    loads[0].start()
+        (*((v_hbm.at[:, pl.ds(8 * t, 8)], v_ref.at[:, pl.ds(8 * t, 8)]) for t in range(4)),
+         (zp_hbm, zp_ref), (fy_hbm, fy_ref), (z1_hbm, z1_ref), (ty_hbm, ty_ref), (te_hbm, te_ref), (zu_hbm, zu_ref)))]
+    for load in loads[:4]:
+        load.start()
     pl.when(z != nz - 1)(lambda: greet(-1))
     greet(-2)
-    loads[1].start()
-    loads[2].start()
+    loads[4].start()
+    loads[5].start()
 
     @pl.when(z >= nz - 2)
     def _():
@@ -345,26 +339,31 @@
 
     for e, r, count in unsent():
         vi_ref[e, r:r + count, :] = jnp.zeros((count, 128), F32)
-    loads[0].wait()
+    for t in range(4):
+        loads[t].wait()
+        values = own_basis([v_ref[x, 8 * t:8 * t + 8, :] for x in range(32)])
+        for i, value in enumerate(values):
+            basis[i, t] = value
+        for i in range(EARLY, len(PAIRS)):
+            for h in (0, 1):
+                sides[h, 4 * (i - EARLY) + t] = functional(2 * i + h, values, weights)
     prepare_states(-1, v_ref, vo_ref, xh)
     pl.when(z == nz - 1)(lambda: start_ahead((True,), False))
-    for t in range(4):
-        for i, value in enumerate(own_basis([v_ref[x, 8 * t:8 * t + 8, :] for x in range(32)])):
-            basis[i, t] = value
-    loads[1].wait()
-    loads[2].wait()
-    prepare_pairs(EARLY, len(PAIRS) - EARLY, weights, zp_ref, fy_ref, vo_ref, basis)
+    loads[4].wait()
+    loads[5].wait()
+    prepare_pairs(EARLY, [sides[h].reshape(32 * (len(PAIRS) - EARLY), 128) for h in (0, 1)], zp_ref, fy_ref, vo_ref)
 
     @pl.when(z >= nz - 2)
     def _():
         start(-2)
         pl.when(z == nz - 1)(lambda: start_ahead((False,), False))
 
-    for load in loads[3:]:
+    for load in loads[6:]:
         load.start()
     prepare_states(1, v_ref, vo_ref, xh)
-    prepare_pairs(0, EARLY, weights, zp_ref, fy_ref, vo_ref, basis)
-    loads[3].wait()
+    early = [[functional(2 * i + h, [basis[k, t] for k in range(20)], weights) for i in range(EARLY) for t in range(4)] for h in (0, 1)]
+    prepare_pairs(0, [jnp.concatenate(side, 0) for side in early], zp_ref, fy_ref, vo_ref)
+    loads[6].wait()
     for t in range(4):
         zt[:, 8 * t:8 * t + 8, :] = wide_dot(v_ref[:, 8 * t:8 * t + 8, :].reshape(256, 128), z1_ref).reshape(32, 8, 128)
     prepare_rows(vo_ref, zt)
@@ -436,7 +435,7 @@
                 for t in range(4):
                     out_ref[t // 2, first_pair % EARLY + i + j, :, 128 * (t % 2):128 * (t % 2) + 128] = r[8 * t:8 * t + 8, 128 * j:128 * j + 128]
 
-    loads[4].wait()
+    loads[7].wait()
     arrive(0)
     for x in range(32):
         plane(x)
@@ -444,9 +443,8 @@
 
     arrive(1)
     state_planes(1)
-    arrive(2)
     upper(10, 5, te_in)
-    loads[5].wait()
+    loads[8].wait()
     for u, (ref, at, rows) in enumerate(((e2_ref, 0, 128), (e34_ref, 128, 96))):
         high, mid, low = split(te_in[u].reshape(8 * EARLY, 256))
         high_mid, high_low = [jnp.concatenate([high, w], 0) for w in (mid, low)]
@@ -454,7 +452,7 @@
         v = [dot(m[h][2], high_low) + dot(m[h][1], high_mid) + dot(m[h][0], high_mid) for h in (0, 1)]
         ref[...] = jnp.where(lax.broadcasted_iota(jnp.int32, (rows, 256), 1) % 128 < 64, v[0], v[1])
 
-    loads[7].wait()
+    loads[9].wait()
     l2 = wide_dot(jnp.concatenate([e2_ref[:, :128], e2_ref[:, 128:]], 0), zu_ref, 0).reshape(2, 16, 8, 128)
     l3 = wide_dot(e34_ref[:64, :128], zu_ref, 1).reshape(8, 8, 128)
     l4 = wide_dot(e34_ref[64:, 128:], zu_ref, 2).reshape(4, 8, 128)
@@ -462,7 +460,6 @@
         for t in (0, 1):
             up[i, t] = merge(i, t, l2[t, i], l3, l4)
     lift_x(ys_ref, up, done)
-    loads[6].wait()
 
     @pl.when(z < 2)
     def _():
@@ -474,12 +471,35 @@
         pl.semaphore_wait(hello.at[0], 5)
         start(1)
 
-    arrive(-1, (True,))
+    arrive(2)
     state_planes(-1)
     first_x(ys_ref, done)
-    arrive(-2)
-    arrive(-1, (False,))
-    upper(15, 5, tl_out)
+    arrive(3)
+    upper(15, 5, tl_in)
+
+    half = lax.broadcasted_iota(jnp.int32, (8, 128), 1) < 64
+
+    def changed(level, u, lanes, early):
+        rows = []
+        for i, pairs in enumerate(late[level]):
+            terms = [jnp.where(half, *pair) * tl_in[u, p, :, lanes:lanes + 128] for p, pair in enumerate(pairs) if max(map(abs, pair)) > 1e-14]
+            while len(terms) > 1:
+                terms = [sum(terms[k:k + 2][1:], terms[k]) for k in range(0, len(terms), 2)]
+            rows.append(early(8 * i) + terms[0])
+        return rows
+
+    l2 = [changed(0, 0, 128 * t, lambda r: e2_ref[r:r + 8, 128 * t:128 * t + 128]) for t in (0, 1)]
+    l2 = wide_dot(jnp.concatenate(l2[0] + l2[1], 0), zu_ref, 0).reshape(2, LATE[0], 8, 128)
+    l3 = wide_dot(jnp.concatenate(changed(1, 1, 0, lambda r: e34_ref[r:r + 8, :128]), 0), zu_ref, 1).reshape(LATE[1], 8, 128)
+    l4 = wide_dot(jnp.concatenate(changed(2, 1, 128, lambda r: e34_ref[64 + r:72 + r, 128:]), 0), zu_ref, 2).reshape(LATE[2], 8, 128)
+    odd_lane = lax.broadcasted_iota(jnp.int32, (8, 128), 1) % 2 == 1
+    for i in range(2 * LATE[1]):
+        for t in (0, 1):
+            at = (i, 0, pl.ds(2 * t, 8, 4), slice(None))
+            if i < LATE[0]:
+                done[at] = jnp.where(odd_lane, done[at], merge(i, t, l2[t, i], l3, l4))
+            elif i % 2 == 0 and t == 0:
+                done[at] = merge(i, t, done[at], l3, l4)
     wait_rows(send, sum(arriving))
 
 
@@ -528,44 +548,15 @@
         done[0, 1, pl.ds(r, 8, 4), :] = q[1] * LIFT_K
 
 
-def finish(done, tl, e2_ref, e34_ref, tl_ref, zu_ref, out_ref, even, sem):
-    lane = lax.broadcasted_iota(jnp.int32, (8, 128), 1)
-
-    def store(source, at, side):
-        pltpu.make_async_copy(source, out_ref.at[at, side], sem).start()
-
-    for at in ((0, 16, 1), (5, 6, 0), (7, 8, 0), (9, 10, 0), (11, 12, 0), (13, 16, 0)):
-        piece = pl.ds(at[0], at[1] - at[0])
-        store(done.at[piece, at[2]], piece, at[2])
-
-    def late(u, at, rows):
-        v = stacked(tl[u].reshape(8 * (len(PAIRS) - EARLY), 256))
-        v = [dot(whole(tl_ref, h, rows=slice(at, at + rows), columns=240), v) for h in (0, 1)]
-        return jnp.where(lax.broadcasted_iota(jnp.int32, (rows, 256), 1) % 128 < 64, v[0], v[1])
-
-    v = e2_ref[0:48, :] + late(0, 0, 48)
-    l2 = wide_dot(jnp.concatenate([v[:, :128], v[:, 128:]], 0), zu_ref, 0).reshape(2, 6, 8, 128)
-    v = e34_ref[...] + late(1, 48, 96)
-    l3 = wide_dot(v[:64, :128], zu_ref, 1).reshape(8, 8, 128)
-    l4 = wide_dot(v[64:, 128:], zu_ref, 2).reshape(4, 8, 128)
-    for k, i in enumerate((0, 1, 2, 3, 4, 6, 8, 10, 12)):
-        for r in range(4):
-            v = done[i, 0, pl.ds(r, 8, 4), :]
-            if i < 5 and r % 2 == 0:
-                v = jnp.where(lane % 2 == 1, v, merge(i, r // 2, l2[r // 2, i], l3, l4))
-            elif r == 0:
-                v = merge(i, 0, v, l3, l4)
-            even[k, pl.ds(r, 8, 4), :] = v
-        if i == 4:
-            store(even.at[pl.ds(0, 5)], pl.ds(0, 5), 0)
-        elif i > 4:
-            store(even.at[k], i, 0)
+def finish(done, out_ref, sem):
+    for i in range(0, 16, 4):
+        pltpu.make_async_copy(done.at[pl.ds(i, 4)], out_ref.at[pl.ds(i, 4)], sem).start()
     pltpu.make_async_copy(done, out_ref, sem).wait()
 
 
 def solution(mesh):
     nx, ny = mesh.shape["gx"], mesh.shape["gy"]
-    weights, (zp, fy, z1, ty, te, tl, zu) = operators()
+    weights, late, (zp, fy, z1, ty, te, zu) = operators()
     vmem, hbm = pl.BlockSpec(memory_space=pltpu.VMEM), pl.BlockSpec(memory_space=pltpu.HBM)
     limit = 24 * 1024 * 1024
     block, pairs = (32, 32, 128), (16, 2, 32, 128)
@@ -574,23 +565,24 @@
         return [pltpu.with_memory_space_constraint(jnp.asarray(m), pltpu.HBM) for m in ms]
 
     def local(v):
-        parts = pl.pallas_call(
-            functools.partial(exchange, nx, ny, 8, weights.tolist()),
-            out_shape=[*(pltpu.VMEM(s, F32) for s in (pairs, (2, len(PAIRS) - EARLY, 8, 256), (128, 256), (96, 256))),
-                       *(pltpu.VMEM(m.shape, BF16) for m in (tl, zu))],
-            in_specs=[hbm] * 8, out_specs=[vmem] * 6,
-            scratch_shapes=[pltpu.VMEM(block, F32), *([pltpu.VMEM((ENTRIES, ROWS, 128), F32)] * 2), pltpu.VMEM((36, 4, 8, 128), F32), *(pltpu.VMEM(m.shape, BF16) for m in (zp, fy, z1, ty, te)),
-                            pltpu.VMEM((2, EARLY, 8, 256), F32), pltpu.VMEM(block, F32), pltpu.VMEM((20, 4, 8, 128), F32), pltpu.VMEM((2, 32, 128), F32), pltpu.VMEM((16, 2, 8, 128), F32),
-                            pltpu.VMEM((2, 80, 128), F32), pltpu.SemaphoreType.DMA, pltpu.SemaphoreType.DMA((COUNTERS,)), pltpu.SemaphoreType.REGULAR((2,)), pltpu.SemaphoreType.DMA((8,))],
+        done = pl.pallas_call(
+            functools.partial(exchange, nx, ny, 8, weights.tolist(), late),
+            out_shape=pltpu.VMEM(pairs, F32),
+            in_specs=[hbm] * 7, out_specs=vmem,
+            scratch_shapes=[*(pltpu.VMEM(s, F32) for s in (block, (ENTRIES, ROWS, 128), (ENTRIES, ROWS, 128), (36, 4, 8, 128))),
+                            *(pltpu.VMEM(m.shape, BF16) for m in (zp, fy, z1, ty, te, zu)),
+                            *(pltpu.VMEM(s, F32) for s in ((2, EARLY, 8, 256), (2, len(PAIRS) - EARLY, 8, 256), (128, 256), (96, 256),
+                                                           block, (20, 4, 8, 128), (2, 4 * (len(PAIRS) - EARLY), 8, 128), (2, 32, 128), (16, 2, 8, 128), (2, 80, 128))),
+                            pltpu.SemaphoreType.DMA, pltpu.SemaphoreType.DMA((COUNTERS,)), pltpu.SemaphoreType.REGULAR((2,)), pltpu.SemaphoreType.DMA((10,))],
             compiler_params=pltpu.CompilerParams(collective_id=0, has_side_effects=True, vmem_limit_bytes=limit),
-        )(*kept(v, zp, fy, z1, ty, te, tl, zu))
+        )(*kept(v, zp, fy, z1, ty, te, zu))
         return pl.pallas_call(
             finish,
             out_shape=jax.ShapeDtypeStruct(pairs, F32),
-            in_specs=[vmem] * 6, out_specs=pl.BlockSpec(memory_space=pl.ANY),
-            scratch_shapes=[pltpu.VMEM((9, 32, 128), F32), pltpu.SemaphoreType.DMA],
+            in_specs=[vmem], out_specs=pl.BlockSpec(memory_space=pl.ANY),
+            scratch_shapes=[pltpu.SemaphoreType.DMA],
             compiler_params=pltpu.CompilerParams(vmem_limit_bytes=limit),
-        )(*parts).reshape(block)
+        )(done).reshape(block)
 
     spec = P("gx", "gy", None)
     return jax.shard_map(local, mesh=mesh, in_specs=(spec,), out_specs=spec, check_vma=False)

time: 20.5 us -> 20.2 us (0.985)
  Pallas kernels: 20.4 us -> 20.1 us
    pallas_call x1, Pallas kernels: 1.15 us -> 0.79 us  [local(): pl.pallas_call(finish, out_shape=jax.ShapeDtypeStruct(pairs, F32), in_spe...]
where the time goes in v7:
time: 20.2 us; the launch traced here: 20.1 us
  Pallas kernels  20.1 us (100%)
    pallas_call x1, Pallas kernels, local(): pl.pallas_call(functools.partial(exchange, nx, ny, 8, weights.tolist(), l...  19.3 us
    pallas_call x1, Pallas kernels, local(): pl.pallas_call(finish, out_shape=jax.ShapeDtypeStruct(pairs, F32), in_spe...  0.79 us

profile of v7, /device:TPU:1, one launch (start us, length us, event | category | flops | bytes accessed | tf_op | source)
XLA Modules:
  0.0 20.1 jit_solution(1576734074640297229)
XLA Ops:
  0.0 19.3 %shard_map.73.done = f32[16,2,32,128]{3,2,1,0:T(8,128)S(1)} custom-call(f32[32,32,128]{2,1,0:T(8,128)} %v_hbm.1, bf16[3,256,128]{2,1,0:T(8,128)(2,1)} %constant.12.clone.zp_hbm, bf16[2,64,128]{2,1,0:T(8,128)(2,1)} %constant.13.clone.fy_hbm, bf16[3,256,128]{2,1,0:T(8,128)(2,1)} %constant.14.clone.z1_hbm, bf16[2,2,32,128]{3,2,1,0:T(8,128)(2,1)} %constant.15.clone.ty_hbm, ...), custom_call_target="tpu_custom_call" | custom-call | tf_op jit(solution)/shard_map/pallas_call | solution.py:568
  19.3 0.8 %shard_map.74 = f32[16,2,32,128]{3,2,1,0:T(8,128)} custom-call(f32[16,2,32,128]{3,2,1,0:T(8,128)S(1)} %shard_map.73.done), custom_call_target="tpu_custom_call" | custom-call | tf_op jit(solution)/shard_map/pallas_call | solution.py:579

commit v8 on v7

--- a/solution.py
+++ b/solution.py
@@ -315,7 +315,7 @@
         for dy in dys:
             pl.semaphore_signal(hello.at[dx - 1], inc=1, device_id=device(dx, dy), device_id_type=MESH)
 
-    loads = [pltpu.make_async_copy(a, b, sems.at[i]) for i, (a, b) in enumerate(
+    loads = [pltpu.make_async_copy(a, b, sems.at[(0, 1, 2, 3, 4, 4, 5, 5, 6, 7)[i]]) for i, (a, b) in enumerate(
         (*((v_hbm.at[:, pl.ds(8 * t, 8)], v_ref.at[:, pl.ds(8 * t, 8)]) for t in range(4)),
          (zp_hbm, zp_ref), (fy_hbm, fy_ref), (z1_hbm, z1_ref), (ty_hbm, ty_ref), (te_hbm, te_ref), (zu_hbm, zu_ref)))]
     for load in loads[:4]:
@@ -349,8 +349,7 @@
                 sides[h, 4 * (i - EARLY) + t] = functional(2 * i + h, values, weights)
     prepare_states(-1, v_ref, vo_ref, xh)
     pl.when(z == nz - 1)(lambda: start_ahead((True,), False))
-    loads[4].wait()
-    loads[5].wait()
+    wait_rows(sems.at[4], (zp_ref.size + fy_ref.size) // 256)
     prepare_pairs(EARLY, [sides[h].reshape(32 * (len(PAIRS) - EARLY), 128) for h in (0, 1)], zp_ref, fy_ref, vo_ref)
 
     @pl.when(z >= nz - 2)
@@ -363,7 +362,7 @@
     prepare_states(1, v_ref, vo_ref, xh)
     early = [[functional(2 * i + h, [basis[k, t] for k in range(20)], weights) for i in range(EARLY) for t in range(4)] for h in (0, 1)]
     prepare_pairs(0, [jnp.concatenate(side, 0) for side in early], zp_ref, fy_ref, vo_ref)
-    loads[6].wait()
+    wait_rows(sems.at[5], (z1_ref.size + ty_ref.size) // 256)
     for t in range(4):
         zt[:, 8 * t:8 * t + 8, :] = wide_dot(v_ref[:, 8 * t:8 * t + 8, :].reshape(256, 128), z1_ref).reshape(32, 8, 128)
     prepare_rows(vo_ref, zt)
@@ -435,7 +434,6 @@
                 for t in range(4):
                     out_ref[t // 2, first_pair % EARLY + i + j, :, 128 * (t % 2):128 * (t % 2) + 128] = r[8 * t:8 * t + 8, 128 * j:128 * j + 128]
 
-    loads[7].wait()
     arrive(0)
     for x in range(32):
         plane(x)
@@ -573,7 +571,7 @@
                             *(pltpu.VMEM(m.shape, BF16) for m in (zp, fy, z1, ty, te, zu)),
                             *(pltpu.VMEM(s, F32) for s in ((2, EARLY, 8, 256), (2, len(PAIRS) - EARLY, 8, 256), (128, 256), (96, 256),
                                                            block, (20, 4, 8, 128), (2, 4 * (len(PAIRS) - EARLY), 8, 128), (2, 32, 128), (16, 2, 8, 128), (2, 80, 128))),
-                            pltpu.SemaphoreType.DMA, pltpu.SemaphoreType.DMA((COUNTERS,)), pltpu.SemaphoreType.REGULAR((2,)), pltpu.SemaphoreType.DMA((10,))],
+                            pltpu.SemaphoreType.DMA, pltpu.SemaphoreType.DMA((COUNTERS,)), pltpu.SemaphoreType.REGULAR((2,)), pltpu.SemaphoreType.DMA((8,))],
             compiler_params=pltpu.CompilerParams(collective_id=0, has_side_effects=True, vmem_limit_bytes=limit),
         )(*kept(v, zp, fy, z1, ty, te, zu))
         return pl.pallas_call(

time: 20.2 us -> 20.2 us (level)
  no operation moved by 1% of the time
where the time goes in v8:
time: 20.2 us; the launch traced here: 20 us
  Pallas kernels  20 us (99%)
    pallas_call x1, Pallas kernels, local(): pl.pallas_call(functools.partial(exchange, nx, ny, 8, weights.tolist(), l...  19.2 us
    pallas_call x1, Pallas kernels, local(): pl.pallas_call(finish, out_shape=jax.ShapeDtypeStruct(pairs, F32), in_spe...  0.79 us

profile of v8, /device:TPU:1, one launch (start us, length us, event | category | flops | bytes accessed | tf_op | source)
XLA Modules:
  0.0 20.0 jit_solution(8881264929455674033)
XLA Ops:
  0.0 19.2 %shard_map.73.done = f32[16,2,32,128]{3,2,1,0:T(8,128)S(1)} custom-call(f32[32,32,128]{2,1,0:T(8,128)} %v_hbm.1, bf16[3,256,128]{2,1,0:T(8,128)(2,1)} %constant.12.clone.zp_hbm, bf16[2,64,128]{2,1,0:T(8,128)(2,1)} %constant.13.clone.fy_hbm, bf16[3,256,128]{2,1,0:T(8,128)(2,1)} %constant.14.clone.z1_hbm, bf16[2,2,32,128]{3,2,1,0:T(8,128)(2,1)} %constant.15.clone.ty_hbm, ...), custom_call_target="tpu_custom_call" | custom-call | tf_op jit(solution)/shard_map/pallas_call | solution.py:566
  19.3 0.8 %shard_map.74 = f32[16,2,32,128]{3,2,1,0:T(8,128)} custom-call(f32[16,2,32,128]{3,2,1,0:T(8,128)S(1)} %shard_map.73.done), custom_call_target="tpu_custom_call" | custom-call | tf_op jit(solution)/shard_map/pallas_call | solution.py:577

commit v9 on v8

--- a/solution.py
+++ b/solution.py
@@ -313,7 +313,7 @@
 
     def say_hello(dx, dys):
         for dy in dys:
-            pl.semaphore_signal(hello.at[dx - 1], inc=1, device_id=device(dx, dy), device_id_type=MESH)
+            pl.semaphore_signal(hello, inc=1, device_id=device(dx, dy), device_id_type=MESH)
 
     loads = [pltpu.make_async_copy(a, b, sems.at[(0, 1, 2, 3, 4, 4, 5, 5, 6, 7)[i]]) for i, (a, b) in enumerate(
         (*((v_hbm.at[:, pl.ds(8 * t, 8)], v_ref.at[:, pl.ds(8 * t, 8)]) for t in range(4)),
@@ -384,12 +384,12 @@
 
     @pl.when(z == nz - 2)
     def _():
-        pl.semaphore_wait(hello.at[0], 1)
+        pl.semaphore_wait(hello, 1)
         start(-1)
 
     @pl.when(z == nz - 1)
     def _():
-        pl.semaphore_wait(hello.at[1], 1)
+        pl.semaphore_wait(hello, 1)
         start_ahead((True, False), True)
 
     @pl.when(z >= nz - 2)
@@ -461,13 +461,9 @@
 
     @pl.when(z < 2)
     def _():
-        pl.semaphore_wait(hello.at[1], 5)
+        pl.semaphore_wait(hello, jnp.where(z == 0, 10, 5))
         start(2)
-
-    @pl.when(z == 0)
-    def _():
-        pl.semaphore_wait(hello.at[0], 5)
-        start(1)
+        pl.when(z == 0)(lambda: start(1))
 
     arrive(2)
     state_planes(-1)
@@ -571,7 +567,7 @@
                             *(pltpu.VMEM(m.shape, BF16) for m in (zp, fy, z1, ty, te, zu)),
                             *(pltpu.VMEM(s, F32) for s in ((2, EARLY, 8, 256), (2, len(PAIRS) - EARLY, 8, 256), (128, 256), (96, 256),
                                                            block, (20, 4, 8, 128), (2, 4 * (len(PAIRS) - EARLY), 8, 128), (2, 32, 128), (16, 2, 8, 128), (2, 80, 128))),
-                            pltpu.SemaphoreType.DMA, pltpu.SemaphoreType.DMA((COUNTERS,)), pltpu.SemaphoreType.REGULAR((2,)), pltpu.SemaphoreType.DMA((8,))],
+                            pltpu.SemaphoreType.DMA, pltpu.SemaphoreType.DMA((COUNTERS,)), pltpu.SemaphoreType.REGULAR, pltpu.SemaphoreType.DMA((8,))],
             compiler_params=pltpu.CompilerParams(collective_id=0, has_side_effects=True, vmem_limit_bytes=limit),
         )(*kept(v, zp, fy, z1, ty, te, zu))
         return pl.pallas_call(

time: 20.2 us -> 20.2 us (level)
  no operation moved by 1% of the time
where the time goes in v9:
time: 20.2 us; the launch traced here: 20 us
  Pallas kernels  20 us (99%)
    pallas_call x1, Pallas kernels, local(): pl.pallas_call(functools.partial(exchange, nx, ny, 8, weights.tolist(), l...  19.2 us
    pallas_call x1, Pallas kernels, local(): pl.pallas_call(finish, out_shape=jax.ShapeDtypeStruct(pairs, F32), in_spe...  0.79 us

profile of v9, /device:TPU:1, one launch (start us, length us, event | category | flops | bytes accessed | tf_op | source)
XLA Modules:
  0.0 20.0 jit_solution(17200788860977448733)
XLA Ops:
  0.0 19.2 %shard_map.73.done = f32[16,2,32,128]{3,2,1,0:T(8,128)S(1)} custom-call(f32[32,32,128]{2,1,0:T(8,128)} %v_hbm.1, bf16[3,256,128]{2,1,0:T(8,128)(2,1)} %constant.12.clone.zp_hbm, bf16[2,64,128]{2,1,0:T(8,128)(2,1)} %constant.13.clone.fy_hbm, bf16[3,256,128]{2,1,0:T(8,128)(2,1)} %constant.14.clone.z1_hbm, bf16[2,2,32,128]{3,2,1,0:T(8,128)(2,1)} %constant.15.clone.ty_hbm, ...), custom_call_target="tpu_custom_call" | custom-call | tf_op jit(solution)/shard_map/pallas_call | solution.py:562
  19.2 0.8 %shard_map.74 = f32[16,2,32,128]{3,2,1,0:T(8,128)} custom-call(f32[16,2,32,128]{3,2,1,0:T(8,128)S(1)} %shard_map.73.done), custom_call_target="tpu_custom_call" | custom-call | tf_op jit(solution)/shard_map/pallas_call | solution.py:573
